TPU v7x, 32 devices: a whole 2x2x4 slice. The times are simulated.
32 devices in a mesh: groups: 2 (over y), expert: 4 (over z), dp: 4 (over x, core).
Axes of the slice: x: 2, y: 2, z: 4, core: 2. Of those that a mesh axis runs over, the one named last changes fastest.
Arguments:
- routes: int32 [4096, 8], P(('groups', 'expert', 'dp')), parts along dimension 0, may hold values from 0 to 63, all different within a row; in each aligned block of 128 rows (0 to 127, 128 to 255, ...) at most 18 rows name the same one
- combine: bfloat16 [4096, 8], P(('groups', 'expert', 'dp')), parts along dimension 0, may hold values from 0.019897461 to 0.29882812
- hidden: bfloat16 [4096, 8, 768], P(('groups', 'expert', 'dp')), parts along dimension 0, may hold values from -6 to 6
- d_out: bfloat16 [4096, 2048], P(('groups', 'expert', 'dp')), parts along dimension 0, may hold values from -0.1796875 to 0.1796875
- w_down: bfloat16 [64, 768, 2048], P('expert', 'dp'), may hold values from -0.21875 to 0.21875
Outputs:
- d_w_down: bfloat16 [128, 768, 2048], P(('groups', 'expert'), 'dp'), parts along dimension 0
- d_combine: float32 [4096, 8], P(('groups', 'expert', 'dp')), parts along dimension 0
There are 2 independent parts, one for each index of `groups`. A program takes and returns all parts, laid end to end along the dimension named above; an argument that names none is the same for every part. Nothing has to cross between parts.
Inputs may be any that keep to these rules, and one draw needn't show every extreme that they name: `routes`: each row names 8 different experts, and every expert is named somewhere. Within the rows of one device (each aligned block of 128 rows) no expert is named more than 18 times, a bound that some block reaches.
All inputs are finite; a program needn't handle non-finite values.
Results may differ from a plain program's by a relative error of at most 0.012.
Values may be sent and summed in bfloat16 or wider, within the bound.
No kernel may reach another device: no remote copies, remote signals or barrier semaphores. Data moves between devices by JAX's collectives and lax.ppermute only.
A program may use at most 384 MiB of HBM per device.

v0:
```python
import jax
import jax.numpy as jnp
from jax import lax
from jax.sharding import PartitionSpec as P

MOST = 18


def route_slots(routes, experts):
    flat_routes = routes.reshape(-1)
    numbers = jnp.arange(experts, dtype=jnp.int32)
    onehot = (flat_routes[:, None] == numbers[None, :]).astype(jnp.int32)
    running = jnp.cumsum(onehot, axis=0) - 1
    slots = jnp.sum(running * onehot, axis=1)
    return (flat_routes, slots)


def route_grads(hidden_in, grad_in, w_down):
    back = jnp.einsum(
        "erd,efd->erf",
        grad_in,
        lax.all_gather(w_down, "dp", axis=1, tiled=True),
        preferred_element_type=jnp.float32,
    )
    return jnp.sum(hidden_in.astype(jnp.float32) * back, axis=2)


def body(routes, combine, hidden, d_out, w_down):
    n_expert = lax.axis_size("expert")
    ex_local = w_down.shape[0]
    experts = n_expert * ex_local
    tok_rows = routes.shape[0]
    top_k = routes.shape[1]
    hidden_units = hidden.shape[2]
    width = d_out.shape[1]
    n_routes = tok_rows * top_k
    rows = n_expert * MOST
    flat_routes, slots = route_slots(routes, experts)
    target = flat_routes * MOST + slots
    table = (
        jnp.full((experts * MOST,), n_routes, jnp.int32)
        .at[target]
        .set(jnp.arange(n_routes, dtype=jnp.int32))
    )
    token_of = table // top_k
    shaped = (n_expert, ex_local, MOST)
    hidden_send = jnp.take(
        hidden.reshape(n_routes, hidden_units), table, axis=0, mode="fill", fill_value=0
    ).reshape(shaped + (hidden_units,))
    weight_send = jnp.take(
        combine.reshape(n_routes), table, axis=0, mode="fill", fill_value=0
    ).reshape(shaped)
    grad_send = jnp.take(d_out, token_of, axis=0, mode="fill", fill_value=0).reshape(
        shaped + (width,)
    )
    hidden_in, grad_in, weight_in = (
        lax.all_to_all(hidden_send, "expert", split_axis=0, concat_axis=2, tiled=True),
        lax.all_to_all(grad_send, "expert", split_axis=0, concat_axis=2, tiled=True),
        lax.all_to_all(weight_send, "expert", split_axis=0, concat_axis=2, tiled=True),
    )
    hidden_in = hidden_in.reshape(ex_local, rows, hidden_units)
    grad_in = grad_in.reshape(ex_local, rows, width)
    weight_in = weight_in.reshape(ex_local, rows)
    slot_grads = route_grads(hidden_in, grad_in, w_down)
    returned = lax.all_to_all(
        slot_grads.reshape(1, ex_local, n_expert, MOST),
        "expert",
        split_axis=2,
        concat_axis=0,
        tiled=True,
    )
    d_combine = jnp.take(returned.reshape(experts * MOST), target, axis=0).reshape(tok_rows, top_k)
    scaled = (weight_in.astype(jnp.float32)[:, :, None] * grad_in.astype(jnp.float32)).astype(
        jnp.bfloat16
    )
    summed = lax.psum_scatter(
        jnp.einsum("erf,erd->fed", hidden_in, scaled, preferred_element_type=jnp.float32).astype(
            jnp.bfloat16
        ),
        "dp",
        scatter_dimension=0,
        tiled=True,
    ).astype(jnp.float32)
    d_w_down = jnp.transpose(summed, (1, 0, 2)).astype(jnp.bfloat16)
    return (d_w_down, d_combine)


def solution(mesh):
    placed = (
        P(("groups", "expert", "dp"), None),
        P(("groups", "expert", "dp"), None),
        P(("groups", "expert", "dp"), None, None),
        P(("groups", "expert", "dp"), None),
        P("expert", "dp", None),
    )
    return jax.shard_map(
        body,
        mesh=mesh,
        in_specs=placed,
        out_specs=(P(("groups", "expert"), "dp", None), P(("groups", "expert", "dp"), None)),
        check_vma=False,
    )
```

profile of v0, /device:TPU:0, one launch (start us, length us, event | category | flops | bytes accessed | tf_op | source)
XLA Modules:
  0.0 678.6 jit_solution(6251633024180250433)
XLA Ops:
  7.2 0.0 copy-start
  7.2 0.0 copy-start.3
  7.2 0.0 copy-start.4
  7.2 0.0 all-gather.2.cloned.1.call-start
  7.2 0.7 all-gather.2.cloned.1.call-update
  7.9 0.1 copy-done.3
  8.0 0.1 copy.41
  8.1 0.1 eq.29
  8.2 0.1 eq.25
  8.3 0.0 copy-done.4
  8.3 0.1 copy.46
  8.4 0.1 reshape.123
  8.5 0.1 mul.35
  8.7 18.0 %reduce-window.6 = s32[64,8,128]{2,1,0:T(8,128)S(1)} reduce-window(s32[64,8,128]{2,1,0:T(8,128)S(1)} %fusion.8, s32[]{:T(128)} %constant.73.clone.1), window={size=1x1x128 pad=0_0x0_0x127_0}, to_apply=%region_0.0 | reduce-window | flops 8323072 | bytes 524292 | tf_op jit(solution)/shard_map/reduce-window
  26.7 0.1 slice.16
  26.8 0.1 copy.44
  27.0 0.1 copy.45
  27.1 0.1 add_add_fusion
  27.2 0.1 fusion.7
  27.3 4.3 scatter_custom_fusion
  31.7 0.1 reduce_and.10
  31.8 7.3 %gather_fusion = bf16[1152]{0:T(1024)(128)(2,1)S(1)} fusion(bf16[1024]{0:T(1024)(128)(2,1)S(1)} %reshape.123, s32[2048]{0:T(1024)S(1)} %pad_clamp_fusion.1), kind=kCustom, calls=%fused_computation | custom fusion | bytes 9216 | tf_op jit(solution)/shard_map/jit(_take)/gather | solution.py:50
  39.1 0.1 gather.25
  39.3 0.7 reshape.177
  40.0 6.3 all-to-all-start
  46.3 0.1 broadcast_in_dim.47
  46.4 0.0 copy-done.2
  46.5 6.0 gather_fusion.1
  52.4 7.5 %gather.27 = bf16[4,16,18,2048]{3,2,1,0:T(8,128)(2,1)} reshape(bf16[1152,2048]{1,0:T(8,128)(2,1)} %gather_fusion.1) | data formatting | bytes 9437184 | tf_op jit(solution)/shard_map/jit(_take)/gather | solution.py:53
  59.9 3.3 broadcast_select_fusion
  63.2 4.8 copy.49
  68.0 0.0 all-to-all-done
  68.0 5.1 all-to-all-start.1
  73.1 0.0 copy-done
  73.1 4.5 gather_fusion.2
  77.6 1.7 gather.29
  79.3 1.9 broadcast_select_fusion.1
  81.3 1.5 copy.50
  82.8 94.7 %all-to-all-done.1 = bf16[4,16,18,2048]{3,1,2,0:T(8,128)(2,1)} async-done(((bf16[4,16,18,2048]{3,1,2,0:T(8,128)(2,1)}), bf16[4,16,18,2048]{3,1,2,0:T(8,128)(2,1)}, u32[]{:S(2)}, u32[]{:S(2)}) %all-to-all-start.1) | async-done | bytes 4718624 | tf_op jit(solution)/shard_map/all_to_all | solution.py:58
  177.5 3.6 all-to-all-start.2
  181.1 0.2 reduce-scatter.2.cloned.1.call-start
  181.3 0.1 reshape.178
  181.4 0.1 copy.59
  181.5 5.4 multiply_convert_fusion
  186.9 34.9 %all-to-all-done.2 = bf16[4,16,18,768]{3,1,2,0:T(8,128)(2,1)S(1)} async-done(((bf16[4,16,18,768]{3,1,2,0:T(8,128)(2,1)}), bf16[4,16,18,768]{3,1,2,0:T(8,128)(2,1)S(1)}, u32[]{:S(2)}, u32[]{:S(2)}) %all-to-all-start.2) | async-done | bytes 1769504 | tf_op jit(solution)/shard_map/all_to_all | solution.py:57
  221.7 27.0 %convert_bitcast_fusion = bf16[768,16,2048]{0,2,1:T(8,128)(2,1)} fusion(bf16[16,72,2048]{2,0,1:T(8,128)(2,1)} %multiply_convert_fusion, bf16[16,72,768]{2,0,1:T(8,128)(2,1)S(1)} %bitcast.54), kind=kOutput, calls=%fused_computation.5 | convolution fusion | flops 3649044480 | bytes 56819712 | tf_op jit(solution)/shard_map/erf,erd->fed/dot_general | solution.py:77
  248.7 63.8 %copy.53 = bf16[768,16,2048]{2,1,0:T(8,128)(2,1)} copy(bf16[768,16,2048]{0,2,1:T(8,128)(2,1)} %convert_bitcast_fusion) | data formatting | bytes 100663296 | tf_op jit(solution)/shard_map/convert_element_type | solution.py:77
  312.5 0.0 reduce-scatter.2.cloned.1.call-update
  312.5 0.0 all-gather.2.cloned.1.call-done
  312.5 29.6 %multiply_reduce_fusion = f32[16,72]{1,0:T(8,128)S(1)} fusion(bf16[16,768,2048]{2,1,0:T(8,128)(2,1)} %all-gather.2.cloned.1.call-done, bf16[16,72,2048]{2,0,1:T(8,128)(2,1)} %bitcast.8, bf16[16,72,768]{2,0,1:T(8,128)(2,1)S(1)} %bitcast.55), kind=kOutput, calls=%fused_computation.11 | convolution fusion | flops 3626531840 | bytes 56824320 | tf_op jit(solution)/shard_map/erd,efd->erf/dot_general | solution.py:19
  342.2 0.1 reshape.127
  342.3 0.7 reshape.179
  343.0 3.5 all-to-all-start.3
  346.5 0.1 reduce_sum.24
  346.6 5.2 all-to-all-done.3
  351.8 0.5 broadcast.103
  352.3 0.7 reduce
  353.0 0.1 reshape.180
  353.1 0.1 reshape.128
  353.2 6.2 gather_fusion.3
  359.4 0.1 gather.31
  359.5 0.7 copy.58
  360.2 296.9 %reduce-scatter.2.cloned.1.call-done = bf16[192,16,2048]{2,1,0:T(8,128)(2,1)} async-done(((bf16[768,16,2048]{2,1,0:T(8,128)(2,1)}), bf16[192,16,2048]{2,1,0:T(8,128)(2,1)}) %reduce-scatter.2.cloned.1.call-update) | async-done | bytes 12582928 | tf_op jit(solution)/shard_map/reduce_scatter | solution.py:76
  657.1 14.6 %copy.57 = bf16[16,192,2048]{2,1,0:T(8,128)(2,1)} copy(bf16[16,192,2048]{2,0,1:T(8,128)(2,1)} %bitcast.56) | data formatting | bytes 25165824
  (20 shorter events, 0.2 us)
Async XLA Ops:
  7.2 65.9 %copy-start = (bf16[128,8,768]{2,1,0:T(8,128)(2,1)S(1)}, bf16[128,8,768]{2,1,0:T(8,128)(2,1)}, u32[]{:S(2)}) copy-start(bf16[128,8,768]{2,1,0:T(8,128)(2,1)} %param.7) | copy-start | bytes 4718596
  7.2 0.8 copy-start.3
  7.2 1.1 copy-start.4
  7.2 305.3 %all-gather.2.cloned.1.call-start = ((), (), s32[]{:S(2)}) async-start(), calls=%async_computation.6 | async-start | bytes 62914560 | tf_op jit(solution)/shard_map/all_gather | solution.py:22
  8.0 38.5 %copy-start.2 = (bf16[128,2048]{1,0:T(8,128)(2,1)S(1)}, bf16[128,2048]{1,0:T(8,128)(2,1)}, u32[]{:S(2)}) copy-start(bf16[128,2048]{1,0:T(8,128)(2,1)} %param.8) | copy-start | bytes 1572868
  40.0 28.0 %all-to-all-start = ((bf16[4,2,144]{2,1,0:T(2,128)(2,1)}), bf16[4,2,144]{2,1,0:T(2,128)(2,1)S(1)}, u32[]{:S(2)}, u32[]{:S(2)}) async-start(bf16[4,2,144]{2,1,0:T(2,128)(2,1)} %reshape.177), calls=%async_computation | async-start | bytes 8192 | tf_op jit(solution)/shard_map/all_to_all | solution.py:59
  68.0 109.5 %all-to-all-start.1 = ((bf16[4,16,18,2048]{3,1,2,0:T(8,128)(2,1)}), bf16[4,16,18,2048]{3,1,2,0:T(8,128)(2,1)}, u32[]{:S(2)}, u32[]{:S(2)}) async-start(bf16[4,16,18,2048]{3,1,2,0:T(8,128)(2,1)} %copy.49), calls=%async_computation.1 | async-start | bytes 9437184 | tf_op jit(solution)/shard_map/all_to_all | solution.py:58
  177.5 44.3 %all-to-all-start.2 = ((bf16[4,16,18,768]{3,1,2,0:T(8,128)(2,1)}), bf16[4,16,18,768]{3,1,2,0:T(8,128)(2,1)S(1)}, u32[]{:S(2)}, u32[]{:S(2)}) async-start(bf16[4,16,18,768]{3,1,2,0:T(8,128)(2,1)} %copy.50), calls=%async_computation.2 | async-start | bytes 3538944 | tf_op jit(solution)/shard_map/all_to_all | solution.py:57
  181.1 476.0 %reduce-scatter.2.cloned.1.call-start = ((), (), s32[]{:S(2)}) async-start(), calls=%async_computation.5 | async-start | bytes 62914560 | tf_op jit(solution)/shard_map/reduce_scatter | solution.py:76
  343.0 8.8 %all-to-all-start.3 = ((f32[4,1,288]{2,1,0:T(1,128)}), f32[4,1,288]{2,1,0:T(1,128)S(1)}, u32[]{:S(2)}, u32[]{:S(2)}) async-start(f32[4,1,288]{2,1,0:T(1,128)} %reshape.179), calls=%async_computation.4 | async-start | bytes 12288 | tf_op jit(solution)/shard_map/all_to_all | solution.py:65
  657.1 14.6 %copy-start.1 = (bf16[128,8,768]{2,1,0:T(8,128)(2,1)S(1)}, bf16[128,8,768]{2,1,0:T(8,128)(2,1)}, u32[]{:S(2)}) copy-start(bf16[128,8,768]{2,1,0:T(8,128)(2,1)} %param.7) | copy-start | bytes 4718596
Sparse Core Ops, SparseCore 0:
  9.6 301.6 all-gather.1
  313.9 343.1 reduce-scatter.1
where the time goes:
time: 681 us; the launch traced here: 679 us
  waiting for transfers between devices  432 us (63%)
  local copies, waits for them, and re-layouts  127 us (19%)
  matrix products  56.6 us (8%)
  other arithmetic  29.6 us (4%)
  starting transfers between devices  18.7 us (3%)
  between operations  14.3 us (2%)
    reduce_scatter x1, waiting for transfers between devices, body(): lax.psum_scatter(jnp.einsum('erf,erd->fed', hidden_in, scaled, preferred_...  297 us
    all_to_all x1, waiting for transfers between devices, body(): lax.all_to_all(grad_send, 'expert', split_axis=0, concat_axis=2, tiled=True)  94.7 us
    convert_element_type x1, local copies, waits for them, and re-layouts, body(): jnp.einsum('erf,erd->fed', hidden_in, scaled, preferred_element_type=jnp....  63.8 us
    all_to_all x1, waiting for transfers between devices, body(): lax.all_to_all(hidden_send, 'expert', split_axis=0, concat_axis=2, tiled=...  34.9 us
    dot_general x1, matrix products, route_grads(): jnp.einsum('erd,efd->erf', grad_in, lax.all_gather(w_down, 'dp', axis=1,...  29.6 us
    dot_general x1, matrix products, body(): jnp.einsum('erf,erd->fed', hidden_in, scaled, preferred_element_type=jnp....  27 us
    another operation x2, other arithmetic  18 us
    unnamed x18, local copies, waits for them, and re-layouts  17.1 us
  transfers between devices with their start and end apart: 6, of which 4 were waited for; matrix products, arithmetic and copies ran while one was open for 29% of the time, Pallas kernels for 0%

commit v1 on v0

v1 whole, which is shorter than its diff:
```python
import functools

import jax
import jax.numpy as jnp
from jax import lax
from jax.experimental import pallas as pl
from jax.experimental.pallas import tpu as pltpu
from jax.sharding import PartitionSpec as P

MOST = 18
SUPER = 8
TILES = 9
GROUP = ("expert", "dp")
f32, bf16, i32 = jnp.float32, jnp.bfloat16, jnp.int32


def dot(a, b, dims=((1,), (0,))):
    return lax.dot_general(a, b, (dims, ((), ())), preferred_element_type=f32)


def iota(shape, dim):
    return lax.broadcasted_iota(i32, shape, dim)


def params(megabytes):
    return pltpu.CompilerParams(vmem_limit_bytes=megabytes * 2**20)


def cost(flops, nbytes):
    return pl.CostEstimate(flops=int(flops), bytes_accessed=int(nbytes), transcendentals=0)


def token_slots(routes_t, experts):
    top_k, tok = routes_t.shape
    numbers = iota((experts, tok), 0)
    named = jnp.zeros((experts, tok), f32)
    for k in range(top_k):
        named += jnp.where(routes_t[k : k + 1, :] == numbers, 1.0, 0.0)
    before = jnp.where(iota((tok, tok), 0) < iota((tok, tok), 1), 1.0, 0.0)
    return named, dot(named.astype(bf16), before.astype(bf16))


def pack_kernel(n_dp, half, routes_t, routes_flat, weights_flat, hidden, out, target):
    ex = pl.program_id(0)
    experts = pl.num_programs(0) * 2 * half // MOST
    n_routes = routes_flat.shape[1]
    top_k, tok = routes_t.shape
    units = hidden.shape[1]
    part = units // n_dp

    @pl.when(ex == 0)
    def _():
        _, slots = token_slots(routes_t[...], experts)
        shape = (tok, n_routes)
        spread = jnp.where(iota(shape, 1) // top_k == iota(shape, 0), 1.0, 0.0)
        slots = dot(slots.astype(bf16), spread.astype(bf16))
        numbers = iota((experts, n_routes), 0)
        rows = slots + (numbers * MOST).astype(f32)
        rows = jnp.where(routes_flat[...] == numbers, rows, 0.0)
        target[...] = jnp.sum(rows, axis=0, keepdims=True).astype(i32)

    weights = weights_flat[...].astype(f32)
    for side in range(2):
        first = ex * 2 * half + side * half
        chosen = target[...] - first == iota((half, n_routes), 0)
        chosen = jnp.where(chosen, weights, 0.0).astype(bf16)
        rows = dot(chosen, hidden[...]).astype(bf16)
        for d in range(n_dp):
            out[d, :, side * part : (side + 1) * part] = rows[:, d * part : (d + 1) * part]


def pack(routes_t, routes_flat, weights_flat, hidden, n_expert, n_dp, half):
    n_routes, units = hidden.shape
    part = units // n_dp
    whole = lambda shape: pl.BlockSpec(shape, lambda i: (0,) * len(shape))
    return pl.pallas_call(
        functools.partial(pack_kernel, n_dp, half),
        grid=(n_expert,),
        in_specs=[
            whole(routes_t.shape),
            whole(routes_flat.shape),
            whole(weights_flat.shape),
            whole(hidden.shape),
        ],
        out_specs=pl.BlockSpec((n_dp, half, 2 * part), lambda i: (i, 0, 0)),
        out_shape=jax.ShapeDtypeStruct((n_expert * n_dp, half, 2 * part), bf16),
        scratch_shapes=[pltpu.VMEM((1, n_routes), i32)],
        compiler_params=params(40),
        cost_estimate=cost(4 * n_expert * half * n_routes * units, 6 * n_routes * units),
    )(routes_t, routes_flat, weights_flat, hidden)


def tile_rows(i, rows):
    first = min(16 * i // MOST, SUPER - 2)
    place = 16 * i + iota((rows, 1), 0) % 16
    second = place >= MOST * (first + 1)
    slot = place - MOST * first - jnp.where(second, MOST, 0)
    return first, second, slot


def gather_kernel(ex_local, routes_t, grads, out):
    tok = routes_t.shape[2]
    width = grads.shape[1]
    rows = 16 * ex_local
    slots = []
    for b in range(SUPER):
        named, before = token_slots(routes_t[b], ex_local)
        slots.append(jnp.where(named > 0, before, -1.0))
    shape = (rows, ex_local)
    spread = jnp.where(iota(shape, 0) // 16 == iota(shape, 1), 1.0, 0.0).astype(bf16)
    step = min(512, width)
    for i in range(TILES):
        first, second, slot = tile_rows(i, rows)
        pair = jnp.concatenate([slots[first], slots[first + 1]], axis=1)
        pair = dot(spread, pair.astype(bf16))
        slot = slot.astype(f32)
        wanted = jnp.where(
            iota((rows, 2 * tok), 1) < tok,
            jnp.where(second, -5.0, slot),
            jnp.where(second, slot, -5.0),
        )
        chosen = jnp.where(pair == wanted, 1.0, 0.0).astype(bf16)
        for c in range(0, width, step):
            found = dot(chosen, grads[first * tok : (first + 2) * tok, c : c + step])
            found = found.astype(bf16).reshape(ex_local, 16, step)
            out[:, 16 * i : 16 * i + 16, c : c + step] = found


def gather(routes_t, grads, ex_local):
    blocks, top_k, tok = routes_t.shape
    width = grads.shape[1]
    return pl.pallas_call(
        functools.partial(gather_kernel, ex_local),
        grid=(blocks // SUPER,),
        in_specs=[
            pl.BlockSpec((SUPER, top_k, tok), lambda s: (s, 0, 0)),
            pl.BlockSpec((SUPER * tok, width), lambda s: (s, 0)),
        ],
        out_specs=pl.BlockSpec((ex_local, SUPER * MOST, width), lambda s: (0, s, 0)),
        out_shape=jax.ShapeDtypeStruct((ex_local, blocks * MOST, width), bf16),
        compiler_params=params(48),
        cost_estimate=cost(
            4 * ex_local * blocks * MOST * tok * width,
            2 * width * blocks * (tok + ex_local * MOST),
        ),
    )(routes_t, grads)


def back_kernel(grads, weights, out):
    out[0] = dot(grads[0], weights[0], ((1,), (1,)))


def back(grads, weights):
    ex_local, rows, width = grads.shape
    part = weights.shape[1]
    chunk = min(rows, 16 * MOST)
    return pl.pallas_call(
        back_kernel,
        grid=(ex_local, rows // chunk),
        in_specs=[
            pl.BlockSpec((1, chunk, width), lambda e, c: (e, c, 0)),
            pl.BlockSpec((1, part, width), lambda e, c: (e, 0, 0)),
        ],
        out_specs=pl.BlockSpec((1, chunk, part), lambda e, c: (e, c, 0)),
        out_shape=jax.ShapeDtypeStruct((ex_local, rows, part), f32),
        compiler_params=params(32),
        cost_estimate=cost(
            2 * ex_local * rows * width * part, 2 * ex_local * (rows + part) * width
        ),
    )(grads, weights)


def arrange_kernel(ex_local, received, backs, out, sums):
    blocks, half, double = received.shape
    part = double // 2
    paired = ex_local % 2 == 0
    some = ex_local // 2 if paired else ex_local
    rows = 16 * some
    for i in range(TILES):
        first, second, slot = tile_rows(i, rows)
        expert = iota((rows, 1), 0) // 16
        block = jnp.where(second, half, 0)
        source = jnp.concatenate([received[first], received[first + 1]], axis=0)
        lane = iota((rows, 128), 1)
        results = []
        for side in range(1 if paired else 2):
            place = expert * MOST + slot - side * half
            inside = (place >= 0) & (place < half)
            column = jnp.where(inside, block + place, -1)
            chosen = iota((rows, 2 * half), 1) == column
            results.append(dot(jnp.where(chosen, 1.0, 0.0).astype(bf16), source))
        if paired:
            sides = [results[0][:, :part], results[0][:, part:]]
        else:
            sides = [results[0][:, :part] + results[1][:, part:]]
        for s, piece in enumerate(sides):
            here = slice(s * some, (s + 1) * some)
            out[here, 16 * i : 16 * i + 16, :] = piece.astype(bf16).reshape(some, 16, part)
            near = backs[here, 16 * i : 16 * i + 16, :].reshape(rows, part)
            total = jnp.sum(piece * near, axis=1, keepdims=True)
            hit = lane == slot
            for b in range(2):
                mine = hit & (second if b else jnp.logical_not(second))
                found = jnp.where(mine, total, 0.0).reshape(some, 16, 128)
                found = jnp.sum(found, axis=1)
                fresh = 16 * i <= MOST * (first + b)
                if not fresh:
                    found += sums[first + b, here, :]
                sums[first + b, here, :] = found


def arrange(received, backs):
    blocks, half, double = received.shape
    ex_local, rows, part = backs.shape
    return pl.pallas_call(
        functools.partial(arrange_kernel, ex_local),
        grid=(blocks // SUPER,),
        in_specs=[
            pl.BlockSpec((SUPER, half, double), lambda s: (s, 0, 0)),
            pl.BlockSpec((ex_local, SUPER * MOST, part), lambda s: (0, s, 0)),
        ],
        out_specs=[
            pl.BlockSpec((ex_local, SUPER * MOST, part), lambda s: (0, s, 0)),
            pl.BlockSpec((SUPER, ex_local, 128), lambda s: (s, 0, 0)),
        ],
        out_shape=[
            jax.ShapeDtypeStruct((ex_local, rows, part), bf16),
            jax.ShapeDtypeStruct((blocks, ex_local, 128), f32),
        ],
        compiler_params=params(32),
        cost_estimate=cost(
            4 * ex_local * rows * half * double, ex_local * rows * part * 8
        ),
    )(received, backs)


def outer_kernel(hidden, grads, out, *scratch):
    found = dot(hidden[0], grads[0], ((0,), (0,)))
    if not scratch:
        out[0] = found.astype(bf16)
        return
    total, chunk = scratch[0], pl.program_id(1)

    @pl.when(chunk == 0)
    def _():
        total[...] = found

    @pl.when(chunk > 0)
    def _():
        total[...] += found

    @pl.when(chunk == pl.num_programs(1) - 1)
    def _():
        out[0] = total[...].astype(bf16)


def outer(hidden, grads):
    ex_local, rows, part = hidden.shape
    width = grads.shape[2]
    chunk = min(rows, 16 * MOST)
    return pl.pallas_call(
        outer_kernel,
        grid=(ex_local, rows // chunk),
        in_specs=[
            pl.BlockSpec((1, chunk, part), lambda e, c: (e, c, 0)),
            pl.BlockSpec((1, chunk, width), lambda e, c: (e, c, 0)),
        ],
        out_specs=pl.BlockSpec((1, part, width), lambda e, c: (e, 0, 0)),
        out_shape=jax.ShapeDtypeStruct((ex_local, part, width), bf16),
        scratch_shapes=[] if rows == chunk else [pltpu.VMEM((part, width), f32)],
        compiler_params=params(32),
        cost_estimate=cost(
            2 * ex_local * rows * width * part, 2 * ex_local * (rows + part) * width
        ),
    )(hidden, grads)


def finish_kernel(routes_t, weights_t, sums, out):
    experts = sums.shape[0]
    top_k, tok = routes_t.shape
    _, slots = token_slots(routes_t[...], experts)
    slots = slots.astype(i32)
    found = jnp.zeros((experts, tok), f32)
    for m in range(MOST):
        found = jnp.where(slots == m, sums[:, m : m + 1], found)
    numbers = iota((experts, tok), 0)
    for k in range(top_k):
        mine = jnp.where(routes_t[k : k + 1, :] == numbers, found, 0.0)
        total = jnp.sum(mine, axis=0, keepdims=True)
        out[k : k + 1, :] = total / weights_t[k : k + 1, :]


def finish(routes_t, weights_t, sums):
    return pl.pallas_call(
        finish_kernel,
        out_shape=jax.ShapeDtypeStruct(routes_t.shape, f32),
        cost_estimate=cost(10000, 100000),
    )(routes_t, weights_t, sums)


def body(routes, combine, hidden, d_out, w_down):
    n_expert = lax.axis_size("expert")
    n_dp = lax.axis_size("dp")
    ex_local = w_down.shape[0]
    experts = n_expert * ex_local
    tok, top_k = routes.shape
    blocks = n_expert * n_dp
    half = ex_local * MOST // 2
    routes_t = routes.T
    n_routes = tok * top_k
    grads = lax.all_gather(d_out, GROUP, axis=0, tiled=True)
    mine = jnp.broadcast_to(routes_t[None], (blocks, top_k, tok))
    all_routes = lax.all_to_all(mine, GROUP, split_axis=0, concat_axis=0, tiled=True)
    all_routes = all_routes - lax.axis_index("expert") * ex_local
    sent = pack(
        routes_t,
        routes.reshape(1, n_routes),
        combine.reshape(1, n_routes),
        hidden.reshape(n_routes, hidden.shape[2]),
        n_expert,
        n_dp,
        half,
    )
    received = lax.all_to_all(sent, GROUP, split_axis=0, concat_axis=0, tiled=True)
    grads = gather(all_routes, grads, ex_local)
    backs = back(grads, w_down)
    arranged, sums = arrange(received, backs)
    returned = lax.all_to_all(sums, GROUP, split_axis=0, concat_axis=0, tiled=True)
    d_w_down = outer(arranged, grads)
    returned = jnp.sum(returned.reshape(n_expert, n_dp, ex_local, 128), axis=1)
    d_combine = finish(routes_t, combine.T.astype(f32), returned.reshape(experts, 128))
    return d_w_down, d_combine.T


def solution(mesh):
    placed = (
        P(("groups", "expert", "dp"), None),
        P(("groups", "expert", "dp"), None),
        P(("groups", "expert", "dp"), None, None),
        P(("groups", "expert", "dp"), None),
        P("expert", "dp", None),
    )
    return jax.shard_map(
        body,
        mesh=mesh,
        in_specs=placed,
        out_specs=(P(("groups", "expert"), "dp", None), P(("groups", "expert", "dp"), None)),
        check_vma=False,
    )
```

time: 681 us -> 195 us (0.29)
  waiting for transfers between devices: 432 us -> 85 us
  local copies, waits for them, and re-layouts: 127 us -> 23.8 us
  matrix products: 56.6 us -> 0 us
  Pallas kernels: 0 us -> 53 us
  other arithmetic: 29.6 us -> 1.21 us
    reduce_scatter x1 -> x0, waiting for transfers between devices: 297 us -> none  [body(): lax.psum_scatter(jnp.einsum('erf,erd->fed', hidden_in, scaled, preferred_...]
    all_to_all x4 -> x3, waiting for transfers between devices: 135 us -> 0.01 us  [the longest x1 0.01 us: body(): lax.all_to_all(mine, GROUP, split_axis=0, concat_axis=0, tiled=True)]
    all_gather x1, waiting for transfers between devices: 0.02 us -> 84.3 us  [body(): grads = lax.all_gather(d_out, GROUP, axis=0, tiled=True)]
    convert_element_type x3 -> x0, local copies, waits for them, and re-layouts: 63.9 us -> none  [the longest x1 63.8 us: body(): jnp.einsum('erf,erd->fed', hidden_in, scaled, preferred_element_type=jnp....]
    dot_general x2 -> x0, matrix products: 56.6 us -> none  [the longest x1 29.6 us: route_grads(): jnp.einsum('erd,efd->erf', grad_in, lax.all_gather(w_down, 'dp', axis=1,...]
    pallas_call x0 -> x6, Pallas kernels: none -> 53 us  [the longest x1 15.3 us: back(): pl.pallas_call(back_kernel, grid=(ex_local, rows // chunk), in_specs=[pl....]
    gather x8 -> x0, local copies, waits for them, and re-layouts: 33.3 us -> none  [the longest x2 13.5 us: body(): jnp.take(d_out, token_of, axis=0, mode='fill', fill_value=0)]
    another operation x2 -> x0, other arithmetic: 18 us -> none
  transfers between devices with their start and end apart: 6 -> 4, of which waited for: 4 -> 1; matrix products, arithmetic and copies ran while one was open for 29% -> 2% of each run, Pallas kernels for 0% -> 23%
where the time goes in v1:
time: 195 us; the launch traced here: 194 us
  waiting for transfers between devices  85 us (44%)
  Pallas kernels  53 us (27%)
  local copies, waits for them, and re-layouts  23.8 us (12%)
  starting transfers between devices  17 us (9%)
  between operations  14.1 us (7%)
    all_gather x1, waiting for transfers between devices, body(): grads = lax.all_gather(d_out, GROUP, axis=0, tiled=True)  84.3 us
    unnamed x20, local copies, waits for them, and re-layouts  22.3 us
    pallas_call x1, Pallas kernels, back(): pl.pallas_call(back_kernel, grid=(ex_local, rows // chunk), in_specs=[pl....  15.3 us
    pallas_call x1, Pallas kernels, gather(): pl.pallas_call(functools.partial(gather_kernel, ex_local), grid=(blocks /...  13.3 us
    pallas_call x1, Pallas kernels, outer(): pl.pallas_call(outer_kernel, grid=(ex_local, rows // chunk), in_specs=[pl...  12.4 us
    all_to_all x1, starting transfers between devices, body(): lax.all_to_all(mine, GROUP, split_axis=0, concat_axis=0, tiled=True)  7.36 us
    pallas_call x1, Pallas kernels, arrange(): pl.pallas_call(functools.partial(arrange_kernel, ex_local), grid=(blocks...  6.35 us
    all_to_all x1, starting transfers between devices, body(): lax.all_to_all(sent, GROUP, split_axis=0, concat_axis=0, tiled=True)  6.01 us
  transfers between devices with their start and end apart: 4, of which 1 were waited for; matrix products, arithmetic and copies ran while one was open for 2% of the time, Pallas kernels for 23%

profile of v1, /device:TPU:0, one launch (start us, length us, event | category | flops | bytes accessed | tf_op | source)
XLA Modules:
  0.0 194.1 jit_solution(4272956701487036146)
XLA Ops:
  7.2 0.0 all-gather.2.cloned.1.call-start
  7.2 0.7 all-gather.2.cloned.1.call-update
  7.9 1.3 broadcast_in_dim.2
  9.2 7.4 %all-to-all-start.1 = ((s32[16,8,128]{2,1,0:T(8,128)}), s32[16,8,128]{2,1,0:T(8,128)S(1)}, u32[]{:S(2)}, u32[]{:S(2)}) async-start(s32[16,8,128]{2,1,0:T(8,128)} %broadcast_in_dim.2), calls=%async_computation.1 | async-start | bytes 131072 | tf_op jit(solution)/shard_map/all_to_all | solution.py:313
  16.6 0.8 copy.9
  17.4 0.1 reshape.20.routes_flat
  17.5 0.8 copy.10
  18.3 0.1 reshape.21.weights_flat
  18.4 0.0 copy-start.6
  18.4 0.7 copy-done.6
  19.1 0.0 copy-start.7
  19.1 1.5 copy-done.7
  20.6 0.0 copy-start.8
  20.6 4.0 %shard_map.68 = bf16[16,144,384]{2,1,0:T(8,128)(2,1)} custom-call(s32[8,128]{1,0:T(8,128)S(1)} %bitcast.10, s32[1,1024]{1,0:T(1,128)S(1)} %reshape.20.routes_flat, bf16[1,1024]{1,0:T(2,128)(2,1)S(1)} %reshape.21.weights_flat, bf16[1024,768]{1,0:T(8,128)(2,1)S(1)} %bitcast.11), custom_call_target="tpu_custom_call" | custom-call | flops 1811939328 | bytes 4718592 | tf_op jit(solution)/shard_map/pallas_call | solution.py:76
  24.6 0.0 all-to-all-done.1
  24.6 6.0 %all-to-all-start = ((bf16[16,144,384]{2,1,0:T(8,128)(2,1)}), bf16[16,144,384]{2,1,0:T(8,128)(2,1)S(1)}, u32[]{:S(2)}, u32[]{:S(2)}) async-start(bf16[16,144,384]{2,1,0:T(8,128)(2,1)} %shard_map.68), calls=%async_computation | async-start | bytes 3538944 | tf_op jit(solution)/shard_map/all_to_all | solution.py:324
  30.6 0.0 copy-done.8
  30.6 0.6 convert_bitcast_fusion.weights_t
  31.2 84.3 %all-gather.2.cloned.1.call-done.grads = bf16[2048,2048]{1,0:T(8,128)(2,1)} async-done(((bf16[128,2048]{1,0:T(8,128)(2,1)}), bf16[2048,2048]{1,0:T(8,128)(2,1)}) %all-gather.2.cloned.1.call-update) | async-done | bytes 8388624 | tf_op jit(solution)/shard_map/all_gather | solution.py:311
  115.5 13.3 %shard_map.69.grads = bf16[16,288,2048]{2,1,0:T(8,128)(2,1)} custom-call(s32[16,8,128]{2,1,0:T(8,128)S(1)} %broadcast_subtract_fusion.routes_t, bf16[2048,2048]{1,0:T(8,128)(2,1)} %all-gather.2.cloned.1.call-done.grads), custom_call_target="tpu_custom_call" | custom-call | flops 4831838208 | bytes 27262976 | tf_op jit(solution)/shard_map/pallas_call | solution.py:132
  128.8 0.0 copy-start.3
  128.8 4.6 %copy-done.3 = bf16[16,192,2048]{2,1,0:T(8,128)(2,1)S(1)} copy-done((bf16[16,192,2048]{2,1,0:T(8,128)(2,1)S(1)}, bf16[16,192,2048]{2,1,0:T(8,128)(2,1)}, u32[]{:S(2)}) %copy-start.3) | copy-done | bytes 12582936
  133.4 15.3 %shard_map.70.backs = f32[16,288,192]{2,1,0:T(8,128)S(1)} custom-call(bf16[16,288,2048]{2,1,0:T(8,128)(2,1)} %shard_map.69.grads, bf16[16,192,2048]{2,1,0:T(8,128)(2,1)S(1)} %copy-done.3), custom_call_target="tpu_custom_call" | custom-call | flops 3623878656 | bytes 31457280 | tf_op jit(solution)/shard_map/pallas_call | solution.py:157
  148.7 0.0 copy-start.1
  148.7 2.2 %copy-done.1 = f32[16,288,192]{2,1,0:T(8,128)} copy-done((f32[16,288,192]{2,1,0:T(8,128)}, f32[16,288,192]{2,1,0:T(8,128)S(1)}, u32[]{:S(2)}) %copy-start.1) | copy-done | bytes 3538968
  150.8 0.0 all-to-all-done.received
  150.9 0.0 copy-start.2
  150.9 2.3 %copy-done.2 = f32[16,288,192]{2,1,0:T(8,128)S(1)} copy-done((f32[16,288,192]{2,1,0:T(8,128)S(1)}, f32[16,288,192]{2,1,0:T(8,128)}, u32[]{:S(2)}) %copy-start.2) | copy-done | bytes 3538968
  153.2 6.4 %shard_map.71 = (bf16[16,288,192]{2,1,0:T(8,128)(2,1)S(1)}, f32[16,16,128]{2,1,0:T(8,128)}) custom-call(bf16[16,144,384]{2,1,0:T(8,128)(2,1)S(1)} %all-to-all-done.received, f32[16,288,192]{2,1,0:T(8,128)S(1)} %copy-done.2), custom_call_target="tpu_custom_call" | custom-call | flops 1019215872 | bytes 7077888 | tf_op jit(solution)/shard_map/pallas_call | solution.py:215
  159.5 0.0 copy-start.4
  159.5 1.4 copy-done.4
  161.0 3.6 %all-to-all-start.2 = ((f32[16,16,128]{2,1,0:T(8,128)}), f32[16,16,128]{2,1,0:T(8,128)S(1)}, u32[]{:S(2)}, u32[]{:S(2)}) async-start(f32[16,16,128]{2,1,0:T(8,128)} %get-tuple-element.5), calls=%async_computation.2 | async-start | bytes 262144 | tf_op jit(solution)/shard_map/all_to_all | solution.py:328
  164.6 0.0 copy-start
  164.6 6.4 %copy-done = bf16[16,288,2048]{2,1,0:T(8,128)(2,1)S(1)} copy-done((bf16[16,288,2048]{2,1,0:T(8,128)(2,1)S(1)}, bf16[16,288,2048]{2,1,0:T(8,128)(2,1)}, u32[]{:S(2)}) %copy-start) | copy-done | bytes 18874392
  171.0 0.0 copy-start.5
  171.0 1.7 copy-done.5
  172.6 12.4 %shard_map.72 = bf16[16,192,2048]{2,1,0:T(8,128)(2,1)} custom-call(bf16[16,288,192]{2,1,0:T(8,128)(2,1)S(1)} %copy-done.5, bf16[16,288,2048]{2,1,0:T(8,128)(2,1)S(1)} %copy-done), custom_call_target="tpu_custom_call" | custom-call | flops 3623878656 | bytes 31457280 | tf_op jit(solution)/shard_map/pallas_call | solution.py:261
  185.0 0.0 all-to-all-done.2
  185.0 0.6 bitcast_reduce_fusion
  185.7 1.6 shard_map.73
  (1 shorter events, 0.0 us)
Async XLA Ops:
  7.2 108.4 %all-gather.2.cloned.1.call-start = ((), (), s32[]{:S(2)}) async-start(), calls=%async_computation.3 | async-start | bytes 8912896 | tf_op jit(solution)/shard_map/all_gather | solution.py:311
  9.2 15.4 %all-to-all-start.1 = ((s32[16,8,128]{2,1,0:T(8,128)}), s32[16,8,128]{2,1,0:T(8,128)S(1)}, u32[]{:S(2)}, u32[]{:S(2)}) async-start(s32[16,8,128]{2,1,0:T(8,128)} %broadcast_in_dim.2), calls=%async_computation.1 | async-start | bytes 131072 | tf_op jit(solution)/shard_map/all_to_all | solution.py:313
  18.4 0.7 copy-start.6
  19.1 1.5 copy-start.7
  20.6 10.0 %copy-start.8 = (bf16[128,8]{0,1:T(8,128)(2,1)S(1)}, bf16[128,8]{0,1:T(8,128)(2,1)}, u32[]{:S(2)}) copy-start(bf16[128,8]{0,1:T(8,128)(2,1)} %param.6) | copy-start | bytes 6148
  24.6 126.3 %all-to-all-start = ((bf16[16,144,384]{2,1,0:T(8,128)(2,1)}), bf16[16,144,384]{2,1,0:T(8,128)(2,1)S(1)}, u32[]{:S(2)}, u32[]{:S(2)}) async-start(bf16[16,144,384]{2,1,0:T(8,128)(2,1)} %shard_map.68), calls=%async_computation | async-start | bytes 3538944 | tf_op jit(solution)/shard_map/all_to_all | solution.py:324
  128.8 4.6 %copy-start.3 = (bf16[16,192,2048]{2,1,0:T(8,128)(2,1)S(1)}, bf16[16,192,2048]{2,1,0:T(8,128)(2,1)}, u32[]{:S(2)}) copy-start(bf16[16,192,2048]{2,1,0:T(8,128)(2,1)} %weights.1) | copy-start | bytes 37748740
  148.7 2.2 %copy-start.1 = (f32[16,288,192]{2,1,0:T(8,128)}, f32[16,288,192]{2,1,0:T(8,128)S(1)}, u32[]{:S(2)}) copy-start(f32[16,288,192]{2,1,0:T(8,128)S(1)} %shard_map.70.backs) | copy-start | bytes 10616836
  150.9 2.3 %copy-start.2 = (f32[16,288,192]{2,1,0:T(8,128)S(1)}, f32[16,288,192]{2,1,0:T(8,128)}, u32[]{:S(2)}) copy-start(f32[16,288,192]{2,1,0:T(8,128)} %copy-done.1) | copy-start | bytes 10616836
  159.5 1.4 copy-start.4
  161.0 24.1 %all-to-all-start.2 = ((f32[16,16,128]{2,1,0:T(8,128)}), f32[16,16,128]{2,1,0:T(8,128)S(1)}, u32[]{:S(2)}, u32[]{:S(2)}) async-start(f32[16,16,128]{2,1,0:T(8,128)} %get-tuple-element.5), calls=%async_computation.2 | async-start | bytes 262144 | tf_op jit(solution)/shard_map/all_to_all | solution.py:328
  164.6 6.4 %copy-start = (bf16[16,288,2048]{2,1,0:T(8,128)(2,1)S(1)}, bf16[16,288,2048]{2,1,0:T(8,128)(2,1)}, u32[]{:S(2)}) copy-start(bf16[16,288,2048]{2,1,0:T(8,128)(2,1)} %shard_map.69.grads) | copy-start | bytes 56623108
  171.0 1.7 copy-start.5
Sparse Core Ops, SparseCore 0:
  10.2 105.3 all-gather.1

commit v2 on v1

v2 whole, which is shorter than its diff:
```python
import functools

import jax
import jax.numpy as jnp
from jax import lax
from jax.experimental import pallas as pl
from jax.experimental.pallas import tpu as pltpu
from jax.sharding import PartitionSpec as P

MOST = 18
SUPER = 8
TILES = 9
GROUP = ("expert", "dp")
f32, bf16, i32 = jnp.float32, jnp.bfloat16, jnp.int32


def dot(a, b, dims=((1,), (0,))):
    return lax.dot_general(a, b, (dims, ((), ())), preferred_element_type=f32)


def iota(shape, dim):
    return lax.broadcasted_iota(i32, shape, dim)


def params(megabytes):
    return pltpu.CompilerParams(vmem_limit_bytes=megabytes * 2**20)


def cost(flops, nbytes):
    return pl.CostEstimate(flops=int(flops), bytes_accessed=int(nbytes), transcendentals=0)


def token_slots(routes_t, experts):
    top_k, tok = routes_t.shape
    numbers = iota((experts, tok), 0)
    named = jnp.zeros((experts, tok), f32)
    for k in range(top_k):
        named += jnp.where(routes_t[k : k + 1, :] == numbers, 1.0, 0.0)
    before = jnp.where(iota((tok, tok), 0) < iota((tok, tok), 1), 1.0, 0.0)
    return named, dot(named.astype(bf16), before.astype(bf16))


def pack_kernel(n_dp, half, routes_t, routes_flat, weights_flat, hidden, out, target):
    ex = pl.program_id(0)
    experts = pl.num_programs(0) * 2 * half // MOST
    n_routes = routes_flat.shape[1]
    top_k, tok = routes_t.shape
    units = hidden.shape[1]
    part = units // n_dp

    @pl.when(ex == 0)
    def _():
        _, slots = token_slots(routes_t[...], experts)
        shape = (tok, n_routes)
        spread = jnp.where(iota(shape, 1) // top_k == iota(shape, 0), 1.0, 0.0)
        slots = dot(slots.astype(bf16), spread.astype(bf16))
        numbers = iota((experts, n_routes), 0)
        rows = slots + (numbers * MOST).astype(f32)
        rows = jnp.where(routes_flat[...] == numbers, rows, 0.0)
        target[...] = jnp.sum(rows, axis=0, keepdims=True).astype(i32)

    weights = weights_flat[...].astype(f32)
    for side in range(2):
        first = ex * 2 * half + side * half
        chosen = target[...] - first == iota((half, n_routes), 0)
        chosen = jnp.where(chosen, weights, 0.0).astype(bf16)
        rows = dot(chosen, hidden[...]).astype(bf16)
        for d in range(n_dp):
            out[d, :, side * part : (side + 1) * part] = rows[:, d * part : (d + 1) * part]


def pack(routes_t, routes_flat, weights_flat, hidden, n_expert, n_dp, half):
    n_routes, units = hidden.shape
    part = units // n_dp
    whole = lambda shape: pl.BlockSpec(shape, lambda i: (0,) * len(shape))
    return pl.pallas_call(
        functools.partial(pack_kernel, n_dp, half),
        grid=(n_expert,),
        in_specs=[
            whole(routes_t.shape),
            whole(routes_flat.shape),
            whole(weights_flat.shape),
            whole(hidden.shape),
        ],
        out_specs=pl.BlockSpec((n_dp, half, 2 * part), lambda i: (i, 0, 0)),
        out_shape=jax.ShapeDtypeStruct((n_expert * n_dp, half, 2 * part), bf16),
        scratch_shapes=[pltpu.VMEM((1, n_routes), i32)],
        compiler_params=params(56),
        cost_estimate=cost(4 * n_expert * half * n_routes * units, 6 * n_routes * units),
    )(routes_t, routes_flat, weights_flat, hidden)


def tile_rows(i, rows):
    first = min(16 * i // MOST, SUPER - 2)
    place = 16 * i + iota((rows, 1), 0) % 16
    second = place >= MOST * (first + 1)
    slot = place - MOST * first - jnp.where(second, MOST, 0)
    return first, second, slot


def gather_kernel(ex_local, order, routes_t, *refs):
    grads, (weights, out, backs, held) = refs[:SUPER], refs[SUPER:]
    tok = routes_t.shape[2]
    width = held.shape[2]
    rows = 16 * ex_local
    start = pl.program_id(0) * SUPER
    expert = pl.program_id(1)

    @pl.when(expert == 0)
    def _():
        slots = []
        for b in range(SUPER):
            named, before = token_slots(routes_t[order[start + b]], ex_local)
            slots.append(jnp.where(named > 0, before, -1.0))
        shape = (rows, ex_local)
        spread = jnp.where(iota(shape, 0) // 16 == iota(shape, 1), 1.0, 0.0).astype(bf16)
        step = min(512, width)
        for i in range(TILES):
            first, second, slot = tile_rows(i, rows)
            pair = jnp.concatenate([slots[first], slots[first + 1]], axis=1)
            pair = dot(spread, pair.astype(bf16))
            slot = slot.astype(f32)
            wanted = jnp.where(
                iota((rows, 2 * tok), 1) < tok,
                jnp.where(second, -5.0, slot),
                jnp.where(second, slot, -5.0),
            )
            chosen = jnp.where(pair == wanted, 1.0, 0.0).astype(bf16)
            for c in range(0, width, step):
                here = slice(c, c + step)
                both = [grads[first][:, here], grads[first + 1][:, here]]
                found = dot(chosen, jnp.concatenate(both, axis=0))
                found = found.astype(bf16).reshape(ex_local, 16, step)
                held[:, 16 * i : 16 * i + 16, here] = found

    mine = held[expert]
    out[0] = mine
    backs[0] = dot(mine, weights[0], ((1,), (1,)))


def gather(order, routes_t, grads, weights):
    blocks, top_k, tok = routes_t.shape
    ex_local, part, width = weights.shape
    if len(grads) == 1:
        supers, grads = blocks // SUPER, list(grads) * SUPER
    else:
        supers = 1
    rows = supers * SUPER * MOST
    place = lambda j: (lambda s, e, order: (SUPER * s + j if supers > 1 else 0, 0))
    return pl.pallas_call(
        functools.partial(gather_kernel, ex_local),
        grid_spec=pltpu.PrefetchScalarGridSpec(
            num_scalar_prefetch=1,
            grid=(supers, ex_local),
            in_specs=[pl.BlockSpec((blocks, top_k, tok), lambda s, e, order: (0, 0, 0))]
            + [pl.BlockSpec((tok, width), place(j)) for j in range(SUPER)]
            + [pl.BlockSpec((1, part, width), lambda s, e, order: (e, 0, 0))],
            out_specs=[
                pl.BlockSpec((1, SUPER * MOST, width), lambda s, e, order: (e, s, 0)),
                pl.BlockSpec((1, SUPER * MOST, part), lambda s, e, order: (e, s, 0)),
            ],
            scratch_shapes=[pltpu.VMEM((ex_local, SUPER * MOST, width), bf16)],
        ),
        out_shape=[
            jax.ShapeDtypeStruct((ex_local, rows, width), bf16),
            jax.ShapeDtypeStruct((ex_local, rows, part), f32),
        ],
        compiler_params=params(56),
        cost_estimate=cost(
            2 * ex_local * rows * width * (2 * tok + part),
            2 * width * (supers * SUPER * tok + ex_local * (rows + part)),
        ),
    )(order, routes_t, *grads, weights)


def arrange_kernel(ex_local, pieces, order, received, *refs):
    backs, outs, sums = refs[:pieces], refs[pieces : 2 * pieces], refs[2 * pieces]
    _, half, double = received.shape
    part = double // 2
    paired = ex_local % 2 == 0
    some = ex_local // 2 if paired else ex_local
    rows = 16 * some
    lane = iota((rows, 128), 1)
    expert = iota((rows, 1), 0) // 16
    for piece in range(pieces):
        start = (pl.program_id(0) * pieces + piece) * SUPER
        totals = {}
        for i in range(TILES):
            first, second, slot = tile_rows(i, rows)
            block = jnp.where(second, half, 0)
            source = [received[order[start + first]], received[order[start + first + 1]]]
            source = jnp.concatenate(source, axis=0)
            results = []
            for side in range(1 if paired else 2):
                place = expert * MOST + slot - side * half
                inside = (place >= 0) & (place < half)
                column = jnp.where(inside, block + place, -1)
                chosen = iota((rows, 2 * half), 1) == column
                results.append(dot(jnp.where(chosen, 1.0, 0.0).astype(bf16), source))
            if paired:
                sides = [results[0][:, :part], results[0][:, part:]]
            else:
                sides = [results[0][:, :part] + results[1][:, part:]]
            for s, found in enumerate(sides):
                here = slice(s * some, (s + 1) * some)
                tile = slice(16 * i, 16 * i + 16)
                outs[piece][here, tile, :] = found.astype(bf16).reshape(some, 16, part)
                near = backs[piece][here, tile, :].reshape(rows, part)
                total = jnp.sum(found * near, axis=1, keepdims=True)
                total = jnp.where(lane == slot, total, 0.0)
                for b in range(2):
                    mine = jnp.where(second == (b == 1), total, 0.0)
                    mine = jnp.sum(mine.reshape(some, 16, 128), axis=1)
                    key = (first + b, s)
                    totals[key] = totals[key] + mine if key in totals else mine
        for (b, s), total in totals.items():
            sums[order[start + b], s * some : (s + 1) * some, :] = total


def arrange(order, received, backs):
    blocks, half, double = received.shape
    ex_local, rows, part = backs[0].shape
    pieces = len(backs)
    steps = blocks // (SUPER * pieces)
    tall = (ex_local, SUPER * MOST, part)
    return pl.pallas_call(
        functools.partial(arrange_kernel, ex_local, pieces),
        grid_spec=pltpu.PrefetchScalarGridSpec(
            num_scalar_prefetch=1,
            grid=(steps,),
            in_specs=[pl.BlockSpec(received.shape, lambda s, order: (0, 0, 0))]
            + [pl.BlockSpec(tall, lambda s, order: (0, s, 0))] * pieces,
            out_specs=[pl.BlockSpec(tall, lambda s, order: (0, s, 0))] * pieces
            + [pl.BlockSpec((blocks, ex_local, 128), lambda s, order: (0, 0, 0))],
        ),
        out_shape=[jax.ShapeDtypeStruct((ex_local, rows, part), bf16)] * pieces
        + [jax.ShapeDtypeStruct((blocks, ex_local, 128), f32)],
        compiler_params=params(56),
        cost_estimate=cost(
            4 * pieces * ex_local * rows * half * double, pieces * ex_local * rows * part * 8
        ),
    )(order, received, *backs)


def outer_kernel(pieces, *refs):
    hidden, grads, out = refs[:pieces], refs[pieces : 2 * pieces], refs[2 * pieces]
    found = sum(dot(h[0], g[0], ((0,), (0,))) for h, g in zip(hidden, grads))
    if len(refs) == 2 * pieces + 1:
        out[0] = found.astype(bf16)
        return
    total, chunk = refs[-1], pl.program_id(1)

    @pl.when(chunk == 0)
    def _():
        total[...] = found

    @pl.when(chunk > 0)
    def _():
        total[...] += found

    @pl.when(chunk == pl.num_programs(1) - 1)
    def _():
        out[0] = total[...].astype(bf16)


def outer(hidden, grads):
    pieces = len(hidden)
    ex_local, rows, part = hidden[0].shape
    width = grads[0].shape[2]
    chunk = min(rows, 16 * MOST)
    return pl.pallas_call(
        functools.partial(outer_kernel, pieces),
        grid=(ex_local, rows // chunk),
        in_specs=[pl.BlockSpec((1, chunk, part), lambda e, c: (e, c, 0))] * pieces
        + [pl.BlockSpec((1, chunk, width), lambda e, c: (e, c, 0))] * pieces,
        out_specs=pl.BlockSpec((1, part, width), lambda e, c: (e, 0, 0)),
        out_shape=jax.ShapeDtypeStruct((ex_local, part, width), bf16),
        scratch_shapes=[] if rows == chunk else [pltpu.VMEM((part, width), f32)],
        compiler_params=params(56),
        cost_estimate=cost(
            2 * pieces * ex_local * rows * width * part,
            2 * ex_local * (pieces * rows + part) * width,
        ),
    )(*hidden, *grads)


def finish_kernel(routes_t, weights_t, sums, out):
    experts = sums.shape[0]
    top_k, tok = routes_t.shape
    _, slots = token_slots(routes_t[...], experts)
    slots = slots.astype(i32)
    found = jnp.zeros((experts, tok), f32)
    for m in range(MOST):
        found = jnp.where(slots == m, sums[:, m : m + 1], found)
    numbers = iota((experts, tok), 0)
    for k in range(top_k):
        mine = jnp.where(routes_t[k : k + 1, :] == numbers, found, 0.0)
        total = jnp.sum(mine, axis=0, keepdims=True)
        out[k : k + 1, :] = total / weights_t[k : k + 1, :]


def finish(routes_t, weights_t, sums):
    return pl.pallas_call(
        finish_kernel,
        out_shape=jax.ShapeDtypeStruct(routes_t.shape, f32),
        cost_estimate=cost(10000, 100000),
    )(routes_t, weights_t, sums)


def hop(block, axis, flip):
    size = lax.axis_size(axis)
    return lax.ppermute(block, axis, [(i, i ^ flip) for i in range(size)])


def gather_blocks(own, n_expert, n_dp):
    if (n_expert, n_dp) != (4, 4):
        return [[lax.all_gather(own, GROUP, axis=0, tiled=True)]]
    far = hop(own, "expert", 2)
    near = hop(own, "expert", 1)
    side = hop(own, "dp", 2)
    both = hop(far, "expert", 1)
    far_side = hop(far, "dp", 2)
    near_side = hop(near, "dp", 2)
    both_side = hop(both, "dp", 2)
    early = [(0, own), (8, far), (4, near), (2, side)]
    late = [(12, both), (10, far_side), (6, near_side), (14, both_side)]
    twin = lambda some: some + [(index + 1, hop(block, "dp", 1)) for index, block in some]
    return [twin(early), twin(late)]


def body(routes, combine, hidden, d_out, w_down):
    n_expert = lax.axis_size("expert")
    n_dp = lax.axis_size("dp")
    ex_local = w_down.shape[0]
    experts = n_expert * ex_local
    tok, top_k = routes.shape
    blocks = n_expert * n_dp
    half = ex_local * MOST // 2
    routes_t = routes.T
    n_routes = tok * top_k
    grads = gather_blocks(d_out, n_expert, n_dp)
    me = lax.axis_index("expert") * n_dp + lax.axis_index("dp")
    mine = jnp.broadcast_to(routes_t[None], (blocks, top_k, tok))
    all_routes = lax.all_to_all(mine, GROUP, split_axis=0, concat_axis=0, tiled=True)
    all_routes = all_routes - lax.axis_index("expert") * ex_local
    sent = pack(
        routes_t,
        routes.reshape(1, n_routes),
        combine.reshape(1, n_routes),
        hidden.reshape(n_routes, hidden.shape[2]),
        n_expert,
        n_dp,
        half,
    )
    received = lax.all_to_all(sent, GROUP, split_axis=0, concat_axis=0, tiled=True)
    if len(grads) == 1:
        order = [jnp.arange(blocks, dtype=i32)]
    else:
        order = [me ^ jnp.asarray([far for far, _ in some], i32) for some in grads]
        grads = [[block for _, block in some] for some in grads]
    found = [gather(o, all_routes, some, w_down) for o, some in zip(order, grads)]
    order = jnp.concatenate(order)
    *arranged, sums = arrange(order, received, [b for _, b in found])
    returned = lax.all_to_all(sums, GROUP, split_axis=0, concat_axis=0, tiled=True)
    d_w_down = outer(arranged, [g for g, _ in found])
    returned = jnp.sum(returned.reshape(n_expert, n_dp, ex_local, 128), axis=1)
    d_combine = finish(routes_t, combine.T.astype(f32), returned.reshape(experts, 128))
    return d_w_down, d_combine.T


def solution(mesh):
    placed = (
        P(("groups", "expert", "dp"), None),
        P(("groups", "expert", "dp"), None),
        P(("groups", "expert", "dp"), None, None),
        P(("groups", "expert", "dp"), None),
        P("expert", "dp", None),
    )
    return jax.shard_map(
        body,
        mesh=mesh,
        in_specs=placed,
        out_specs=(P(("groups", "expert"), "dp", None), P(("groups", "expert", "dp"), None)),
        check_vma=False,
    )
```

time: 195 us -> 208 us (1.067)
  Pallas kernels: 53 us -> 77.8 us
  local copies, waits for them, and re-layouts: 23.8 us -> 8.35 us
  between operations: 14.1 us -> 0.88 us
  starting transfers between devices: 17 us -> 28.2 us
  waiting for transfers between devices: 85 us -> 89.1 us
    ppermute x0 -> x15, waiting for transfers between devices: none -> 89.1 us  [hop(): return lax.ppermute(block, axis, [(i, i ^ flip) for i in range(size)])]
    all_gather x1 -> x0, waiting for transfers between devices: 84.3 us -> none  [body(): grads = lax.all_gather(d_out, GROUP, axis=0, tiled=True)]
    pallas_call x4, Pallas kernels: 47.3 us -> 70.7 us  [the longest x2 40.9 us: gather(): pl.pallas_call(functools.partial(gather_kernel, ex_local), grid_spec=pltp...]
    unnamed x20 -> x38, local copies, waits for them, and re-layouts: 22.3 us -> 5.63 us
    ppermute x0 -> x15, starting transfers between devices: none -> 10.4 us  [hop(): return lax.ppermute(block, axis, [(i, i ^ flip) for i in range(size)])]
  transfers between devices with their start and end apart: 4 -> 18, of which waited for: 1 -> 4; matrix products, arithmetic and copies ran while one was open for 2% -> 2% of each run, Pallas kernels for 23% -> 32%
where the time goes in v2:
time: 208 us; the launch traced here: 207 us
  waiting for transfers between devices  89.1 us (43%)
  Pallas kernels  77.8 us (37%)
  starting transfers between devices  28.2 us (14%)
  local copies, waits for them, and re-layouts  8.35 us (4%)
  other arithmetic  2.48 us (1%)
    ppermute x15, waiting for transfers between devices, hop(): return lax.ppermute(block, axis, [(i, i ^ flip) for i in range(size)])  89.1 us
    pallas_call x2, Pallas kernels, gather(): pl.pallas_call(functools.partial(gather_kernel, ex_local), grid_spec=pltp...  40.9 us
    pallas_call x1, Pallas kernels, outer(): pl.pallas_call(functools.partial(outer_kernel, pieces), grid=(ex_local, r...  20.3 us
    ppermute x15, starting transfers between devices, hop(): return lax.ppermute(block, axis, [(i, i ^ flip) for i in range(size)])  10.4 us
    pallas_call x1, Pallas kernels, arrange(): pl.pallas_call(functools.partial(arrange_kernel, ex_local, pieces), grid_...  9.57 us
    all_to_all x1, starting transfers between devices, body(): lax.all_to_all(mine, GROUP, split_axis=0, concat_axis=0, tiled=True)  7.36 us
    all_to_all x1, starting transfers between devices, body(): lax.all_to_all(sent, GROUP, split_axis=0, concat_axis=0, tiled=True)  6.15 us
    unnamed x38, local copies, waits for them, and re-layouts  5.63 us
  transfers between devices with their start and end apart: 18, of which 4 were waited for; matrix products, arithmetic and copies ran while one was open for 2% of the time, Pallas kernels for 32%

profile of v2, /device:TPU:0, one launch (start us, length us, event | category | flops | bytes accessed | tf_op | source)
XLA Modules:
  0.0 206.8 jit_solution(11900528374279639260)
XLA Ops:
  0.6 1.3 broadcast_in_dim.2
  2.0 7.4 %all-to-all-start.1 = ((s32[16,8,128]{2,1,0:T(8,128)}), s32[16,8,128]{2,1,0:T(8,128)S(1)}, u32[]{:S(2)}, u32[]{:S(2)}) async-start(s32[16,8,128]{2,1,0:T(8,128)} %broadcast_in_dim.2), calls=%async_computation.1 | async-start | bytes 131072 | tf_op jit(solution)/shard_map/all_to_all | solution.py:344
  9.3 0.8 copy.11
  10.1 0.7 reshape.20.routes_flat
  10.8 0.8 copy.12
  11.6 0.7 reshape.21.weights_flat
  12.3 5.5 %shard_map.86 = bf16[16,144,384]{2,1,0:T(8,128)(2,1)} custom-call(s32[8,128]{1,0:T(8,128)} %bitcast.10, s32[1,1024]{1,0:T(1,128)} %reshape.20.routes_flat, bf16[1,1024]{1,0:T(2,128)(2,1)} %reshape.21.weights_flat, bf16[1024,768]{1,0:T(8,128)(2,1)} %bitcast.13), custom_call_target="tpu_custom_call" | custom-call | flops 1811939328 | bytes 4718592 | tf_op jit(solution)/shard_map/pallas_call | solution.py:76
  17.8 0.0 copy-start.13
  17.8 0.0 all-to-all-done.1
  17.8 6.1 %all-to-all-start = ((bf16[16,144,384]{2,1,0:T(8,128)(2,1)}), bf16[16,144,384]{2,1,0:T(8,128)(2,1)S(1)}, u32[]{:S(2)}, u32[]{:S(2)}) async-start(bf16[16,144,384]{2,1,0:T(8,128)(2,1)} %shard_map.86), calls=%async_computation | async-start | bytes 3538944 | tf_op jit(solution)/shard_map/all_to_all | solution.py:355
  24.0 0.0 copy-done.1
  24.0 2.9 %collective-permute-start = (bf16[128,2048]{1,0:T(8,128)(2,1)S(1)}, bf16[128,2048]{1,0:T(8,128)(2,1)}, u32[]{:S(2)}, u32[]{:S(2)}) collective-permute-start(bf16[128,2048]{1,0:T(8,128)(2,1)S(1)} %copy-done.1), channel_id=1, source_target_pairs={{0,8},{4,12},{8,0},{12,4},{1,9},{5,13},{9,1},{13,5},{2,10},{6,14},... | collective-permute-start | bytes 1572872 | tf_op jit(solution)/shard_map/ppermute | solution.py:312
  26.9 1.5 collective-permute-start.1
  28.3 1.5 collective-permute-start.2
  29.8 0.0 collective-permute-start.3
  29.8 58.8 %collective-permute-done.refs_1_ = bf16[128,2048]{1,0:T(8,128)(2,1)} collective-permute-done((bf16[128,2048]{1,0:T(8,128)(2,1)S(1)}, bf16[128,2048]{1,0:T(8,128)(2,1)}, u32[]{:S(2)}, u32[]{:S(2)}) %collective-permute-start) | collective-permute-done | bytes 524320 | tf_op jit(solution)/shard_map/ppermute | solution.py:312
  88.6 0.0 collective-permute-start.7
  88.6 1.6 collective-permute-start.8
  90.2 0.0 collective-permute-done.1.refs_2_
  90.2 0.0 collective-permute-start.4
  90.2 0.0 collective-permute-done.2.refs_3_
  90.2 0.4 collective-permute-start.9
  90.7 0.0 collective-permute-done.3.refs_4_
  90.7 0.2 collective-permute-start.5
  90.9 11.4 %collective-permute-done.7.refs_0_ = bf16[128,2048]{1,0:T(8,128)(2,1)S(1)} collective-permute-done((bf16[128,2048]{1,0:T(8,128)(2,1)}, bf16[128,2048]{1,0:T(8,128)(2,1)S(1)}, u32[]{:S(2)}, u32[]{:S(2)}) %collective-permute-start.7) | collective-permute-done | bytes 524320 | tf_op jit(solution)/shard_map/ppermute | solution.py:312
  102.3 1.6 collective-permute-start.10
  103.9 0.0 copy-done.16
  103.9 0.0 copy-done.17
  103.9 0.0 collective-permute-done.8.refs_1_
  104.0 0.1 collective-permute-start.6
  104.0 0.6 pad_add_fusion.order
  104.6 0.0 copy-done.13
  104.6 0.6 convert_bitcast_fusion.weights_t
  105.2 9.6 %collective-permute-done.9.refs_2_ = bf16[128,2048]{1,0:T(8,128)(2,1)S(1)} collective-permute-done((bf16[128,2048]{1,0:T(8,128)(2,1)}, bf16[128,2048]{1,0:T(8,128)(2,1)S(1)}, u32[]{:S(2)}, u32[]{:S(2)}) %collective-permute-start.9) | collective-permute-done | bytes 524320 | tf_op jit(solution)/shard_map/ppermute | solution.py:312
  114.9 0.0 collective-permute-start.11
  114.9 0.0 collective-permute-done.4.refs_5_
  114.9 0.5 collective-permute-start.12
  115.4 0.0 collective-permute-done.5.refs_6_
  115.4 0.1 collective-permute-start.13
  115.5 9.3 %collective-permute-done.10.refs_3_ = bf16[128,2048]{1,0:T(8,128)(2,1)S(1)} collective-permute-done((bf16[128,2048]{1,0:T(8,128)(2,1)S(1)}, bf16[128,2048]{1,0:T(8,128)(2,1)S(1)}, u32[]{:S(2)}, u32[]{:S(2)}) %collective-permute-start.10) | collective-permute-done | bytes 524320 | tf_op jit(solution)/shard_map/ppermute | solution.py:312
  124.7 0.0 collective-permute-start.14
  124.7 0.7 broadcast_subtract_fusion.routes_t
  125.4 0.0 collective-permute-done.6.refs_7_
  125.4 0.8 copy-done.10
  126.2 20.4 %shard_map.87 = (bf16[16,144,2048]{2,1,0:T(8,128)(2,1)}, f32[16,144,192]{2,1,0:T(8,128)}) custom-call(s32[8]{0:T(128)} %copy-done.15, s32[16,8,128]{2,1,0:T(8,128)} %broadcast_subtract_fusion.routes_t, bf16[128,2048]{1,0:T(8,128)(2,1)} %refs_0_.1, bf16[128,2048]{1,0:T(8,128)(2,1)} %collective-permute-done.refs_1_, ...), custom_call_target="tpu_custom_call" | custom-call | flops 4227858432 | bytes 26214400 | tf_op jit(solution)/shard_map/pallas_call | solution.py:150
  146.7 0.0 collective-permute-done.11.refs_4_
  146.7 0.0 collective-permute-done.12.refs_5_
  146.7 0.0 copy-start.9
  146.7 0.0 collective-permute-done.13.refs_6_
  146.8 0.0 collective-permute-done.14.refs_7_
  146.8 0.8 copy-done.8
  147.5 0.2 copy-done.9
  147.7 0.1 copy-done.11
  147.9 0.8 copy-done.12
  148.7 20.5 %shard_map.88 = (bf16[16,144,2048]{2,1,0:T(8,128)(2,1)}, f32[16,144,192]{2,1,0:T(8,128)}) custom-call(s32[8]{0:T(128)} %copy-done.14, s32[16,8,128]{2,1,0:T(8,128)} %broadcast_subtract_fusion.routes_t, bf16[128,2048]{1,0:T(8,128)(2,1)} %copy-done.2, bf16[128,2048]{1,0:T(8,128)(2,1)} %copy-done.3, bf16[128,2048]{1,0:T(8,128)(2,1)} %copy-done.4, ...), custom_call_target="tpu_custom_call" | custom-call | flops 4227858432 | bytes 26214400 | tf_op jit(solution)/shard_map/pallas_call | solution.py:150
  169.1 0.0 all-to-all-done.received
  169.1 0.0 copy-start
  169.2 1.3 copy-done
  170.4 9.6 %shard_map.89 = (bf16[16,144,192]{2,1,0:T(8,128)(2,1)}, bf16[16,144,192]{2,1,0:T(8,128)(2,1)}, f32[16,16,128]{2,1,0:T(8,128)}) custom-call(s32[16]{0:T(128)} %pad_add_fusion.order, bf16[16,144,384]{2,1,0:T(8,128)(2,1)} %copy-done, f32[16,144,192]{2,1,0:T(8,128)} %get-tuple-element.9.refs_0_, f32[16,144,192]{2,1,0:T(8,128)} %get-tuple-element.10.refs_1_), custom_call_target="tpu_custom_call" | custom-call | flops 1019215872 | bytes 7077888 | tf_op jit(solution)/shard_map/pallas_call | solution.py:226
  180.0 4.3 %all-to-all-start.2 = ((f32[16,16,128]{2,1,0:T(8,128)}), f32[16,16,128]{2,1,0:T(8,128)S(1)}, u32[]{:S(2)}, u32[]{:S(2)}) async-start(f32[16,16,128]{2,1,0:T(8,128)} %get-tuple-element.15), calls=%async_computation.2 | async-start | bytes 262144 | tf_op jit(solution)/shard_map/all_to_all | solution.py:364
  184.3 20.3 %shard_map.90 = bf16[16,192,2048]{2,1,0:T(8,128)(2,1)} custom-call(bf16[16,144,192]{2,1,0:T(8,128)(2,1)} %get-tuple-element.11.refs_0_, bf16[16,144,192]{2,1,0:T(8,128)(2,1)} %get-tuple-element.12.refs_1_, bf16[16,144,2048]{2,1,0:T(8,128)(2,1)} %get-tuple-element.13.refs_2_, bf16[16,144,2048]{2,1,0:T(8,128)(2,1)} %get-tuple-element.14.refs_3_), custom_call_target="tpu_custom_call" | custom-call | flops 3623878656 | bytes 31457280 | tf_op jit(solution)/shard_map/pallas_call | solution.py:271
  204.6 0.0 all-to-all-done.2
  204.6 0.6 bitcast_reduce_fusion
  205.2 1.6 shard_map.91
  (24 shorter events, 0.0 us)
Async XLA Ops:
  2.0 15.8 %all-to-all-start.1 = ((s32[16,8,128]{2,1,0:T(8,128)}), s32[16,8,128]{2,1,0:T(8,128)S(1)}, u32[]{:S(2)}, u32[]{:S(2)}) async-start(s32[16,8,128]{2,1,0:T(8,128)} %broadcast_in_dim.2), calls=%async_computation.1 | async-start | bytes 131072 | tf_op jit(solution)/shard_map/all_to_all | solution.py:344
  17.8 6.2 %copy-start.1 = (bf16[128,2048]{1,0:T(8,128)(2,1)S(1)}, bf16[128,2048]{1,0:T(8,128)(2,1)}, u32[]{:S(2)}) copy-start(bf16[128,2048]{1,0:T(8,128)(2,1)} %refs_0_.1) | copy-start | bytes 1572868
  17.8 86.1 %copy-start.16 = (s32[8]{0:T(128)S(1)}, s32[8]{0:T(128)}, u32[]{:S(2)}) copy-start(s32[8]{0:T(128)} %constant.17.clone) | copy-start | bytes 100
  17.8 86.1 %copy-start.17 = (s32[8]{0:T(128)S(1)}, s32[8]{0:T(128)}, u32[]{:S(2)}) copy-start(s32[8]{0:T(128)} %constant.18.clone) | copy-start | bytes 100
  17.8 86.9 %copy-start.13 = (bf16[128,8]{0,1:T(8,128)(2,1)S(1)}, bf16[128,8]{0,1:T(8,128)(2,1)}, u32[]{:S(2)}) copy-start(bf16[128,8]{0,1:T(8,128)(2,1)} %param.8) | copy-start | bytes 6148
  17.8 151.3 %all-to-all-start = ((bf16[16,144,384]{2,1,0:T(8,128)(2,1)}), bf16[16,144,384]{2,1,0:T(8,128)(2,1)S(1)}, u32[]{:S(2)}, u32[]{:S(2)}) async-start(bf16[16,144,384]{2,1,0:T(8,128)(2,1)} %shard_map.86), calls=%async_computation | async-start | bytes 3538944 | tf_op jit(solution)/shard_map/all_to_all | solution.py:355
  24.0 64.6 %collective-permute-start = (bf16[128,2048]{1,0:T(8,128)(2,1)S(1)}, bf16[128,2048]{1,0:T(8,128)(2,1)}, u32[]{:S(2)}, u32[]{:S(2)}) collective-permute-start(bf16[128,2048]{1,0:T(8,128)(2,1)S(1)} %copy-done.1), channel_id=1, source_target_pairs={{0,8},{4,12},{8,0},{12,4},{1,9},{5,13},{9,1},{13,5},{2,10},{6,14},... | collective-permute-start | bytes 1572872 | tf_op jit(solution)/shard_map/ppermute | solution.py:312
  26.9 63.4 %collective-permute-start.1 = (bf16[128,2048]{1,0:T(8,128)(2,1)S(1)}, bf16[128,2048]{1,0:T(8,128)(2,1)}, u32[]{:S(2)}, u32[]{:S(2)}) collective-permute-start(bf16[128,2048]{1,0:T(8,128)(2,1)S(1)} %copy-done.1), channel_id=1, source_target_pairs={{0,4},{4,0},{8,12},{12,8},{1,5},{5,1},{9,13},{13,9},{2,6},{6,2},{1... | collective-permute-start | bytes 1572872 | tf_op jit(solution)/shard_map/ppermute | solution.py:312
  28.3 61.9 %collective-permute-start.2 = (bf16[128,2048]{1,0:T(8,128)(2,1)S(1)}, bf16[128,2048]{1,0:T(8,128)(2,1)}, u32[]{:S(2)}, u32[]{:S(2)}) collective-permute-start(bf16[128,2048]{1,0:T(8,128)(2,1)S(1)} %copy-done.1), channel_id=1, source_target_pairs={{0,2},{1,3},{2,0},{3,1},{4,6},{5,7},{6,4},{7,5},{8,10},{9,11},{10,... | collective-permute-start | bytes 1572872 | tf_op jit(solution)/shard_map/ppermute | solution.py:312
  29.8 60.9 %collective-permute-start.3 = (bf16[128,2048]{1,0:T(8,128)(2,1)S(1)}, bf16[128,2048]{1,0:T(8,128)(2,1)}, u32[]{:S(2)}, u32[]{:S(2)}) collective-permute-start(bf16[128,2048]{1,0:T(8,128)(2,1)S(1)} %copy-done.1), channel_id=1, source_target_pairs={{0,1},{1,0},{2,3},{3,2},{4,5},{5,4},{6,7},{7,6},{8,9},{9,8},{10,11... | collective-permute-start | bytes 1572872 | tf_op jit(solution)/shard_map/ppermute | solution.py:312
  88.6 13.7 %collective-permute-start.7 = (bf16[128,2048]{1,0:T(8,128)(2,1)}, bf16[128,2048]{1,0:T(8,128)(2,1)S(1)}, u32[]{:S(2)}, u32[]{:S(2)}) collective-permute-start(bf16[128,2048]{1,0:T(8,128)(2,1)} %collective-permute-done.refs_1_), channel_id=1, source_target_pairs={{0,4},{4,0},{8,12},{12,8},{1,5},{5,1},{9,13},{13,9},{2,6},{6,2},{1... | collective-permute-start | bytes 1572872 | tf_op jit(solution)/shard_map/ppermute | solution.py:312
  88.6 15.4 %collective-permute-start.8 = (bf16[128,2048]{1,0:T(8,128)(2,1)}, bf16[128,2048]{1,0:T(8,128)(2,1)S(1)}, u32[]{:S(2)}, u32[]{:S(2)}) collective-permute-start(bf16[128,2048]{1,0:T(8,128)(2,1)} %collective-permute-done.refs_1_), channel_id=1, source_target_pairs={{0,2},{1,3},{2,0},{3,1},{4,6},{5,7},{6,4},{7,5},{8,10},{9,11},{10,... | collective-permute-start | bytes 1572872 | tf_op jit(solution)/shard_map/ppermute | solution.py:312
  90.2 24.6 %collective-permute-start.4 = (bf16[128,2048]{1,0:T(8,128)(2,1)}, bf16[128,2048]{1,0:T(8,128)(2,1)S(1)}, u32[]{:S(2)}, u32[]{:S(2)}) collective-permute-start(bf16[128,2048]{1,0:T(8,128)(2,1)} %collective-permute-done.refs_1_), channel_id=1, source_target_pairs={{0,1},{1,0},{2,3},{3,2},{4,5},{5,4},{6,7},{7,6},{8,9},{9,8},{10,11... | collective-permute-start | bytes 1572872 | tf_op jit(solution)/shard_map/ppermute | solution.py:312
  90.2 24.6 %collective-permute-start.9 = (bf16[128,2048]{1,0:T(8,128)(2,1)}, bf16[128,2048]{1,0:T(8,128)(2,1)S(1)}, u32[]{:S(2)}, u32[]{:S(2)}) collective-permute-start(bf16[128,2048]{1,0:T(8,128)(2,1)} %collective-permute-done.1.refs_2_), channel_id=1, source_target_pairs={{0,2},{1,3},{2,0},{3,1},{4,6},{5,7},{6,4},{7,5},{8,10},{9,11},{10,... | collective-permute-start | bytes 1572872 | tf_op jit(solution)/shard_map/ppermute | solution.py:312
  90.7 24.7 %collective-permute-start.5 = (bf16[128,2048]{1,0:T(8,128)(2,1)}, bf16[128,2048]{1,0:T(8,128)(2,1)S(1)}, u32[]{:S(2)}, u32[]{:S(2)}) collective-permute-start(bf16[128,2048]{1,0:T(8,128)(2,1)} %collective-permute-done.1.refs_2_), channel_id=1, source_target_pairs={{0,1},{1,0},{2,3},{3,2},{4,5},{5,4},{6,7},{7,6},{8,9},{9,8},{10,11... | collective-permute-start | bytes 1572872 | tf_op jit(solution)/shard_map/ppermute | solution.py:312
  102.3 44.4 %copy-start.2 = (bf16[128,2048]{1,0:T(8,128)(2,1)}, bf16[128,2048]{1,0:T(8,128)(2,1)S(1)}, u32[]{:S(2)}) copy-start(bf16[128,2048]{1,0:T(8,128)(2,1)S(1)} %collective-permute-done.7.refs_0_) | copy-start | bytes 1572868
  102.3 22.5 %collective-permute-start.10 = (bf16[128,2048]{1,0:T(8,128)(2,1)S(1)}, bf16[128,2048]{1,0:T(8,128)(2,1)S(1)}, u32[]{:S(2)}, u32[]{:S(2)}) collective-permute-start(bf16[128,2048]{1,0:T(8,128)(2,1)S(1)} %collective-permute-done.7.refs_0_), channel_id=1, source_target_pairs={{0,2},{1,3},{2,0},{3,1},{4,6},{5,7},{6,4},{7,5},{8,10},{9,11},{10,... | collective-permute-start | bytes 1572872 | tf_op jit(solution)/shard_map/ppermute | solution.py:312
  103.9 21.5 %copy-start.15 = (s32[8]{0:T(128)}, s32[8]{0:T(128)S(1)}, u32[]{:S(2)}) copy-start(s32[8]{0:T(128)S(1)} %get-tuple-element.17.order) | copy-start | bytes 100
  103.9 42.7 %copy-start.14 = (s32[8]{0:T(128)}, s32[8]{0:T(128)S(1)}, u32[]{:S(2)}) copy-start(s32[8]{0:T(128)S(1)} %get-tuple-element.16.order) | copy-start | bytes 100
  104.0 42.7 %copy-start.3 = (bf16[128,2048]{1,0:T(8,128)(2,1)}, bf16[128,2048]{1,0:T(8,128)(2,1)S(1)}, u32[]{:S(2)}) copy-start(bf16[128,2048]{1,0:T(8,128)(2,1)S(1)} %collective-permute-done.8.refs_1_) | copy-start | bytes 1572868
  104.0 21.5 %collective-permute-start.6 = (bf16[128,2048]{1,0:T(8,128)(2,1)}, bf16[128,2048]{1,0:T(8,128)(2,1)S(1)}, u32[]{:S(2)}, u32[]{:S(2)}) collective-permute-start(bf16[128,2048]{1,0:T(8,128)(2,1)} %collective-permute-done.2.refs_3_), channel_id=1, source_target_pairs={{0,1},{1,0},{2,3},{3,2},{4,5},{5,4},{6,7},{7,6},{8,9},{9,8},{10,11... | collective-permute-start | bytes 1572872 | tf_op jit(solution)/shard_map/ppermute | solution.py:312
  114.9 31.8 %copy-start.4 = (bf16[128,2048]{1,0:T(8,128)(2,1)}, bf16[128,2048]{1,0:T(8,128)(2,1)S(1)}, u32[]{:S(2)}) copy-start(bf16[128,2048]{1,0:T(8,128)(2,1)S(1)} %collective-permute-done.9.refs_2_) | copy-start | bytes 1572868
  114.9 31.8 %collective-permute-start.11 = (bf16[128,2048]{1,0:T(8,128)(2,1)S(1)}, bf16[128,2048]{1,0:T(8,128)(2,1)S(1)}, u32[]{:S(2)}, u32[]{:S(2)}) collective-permute-start(bf16[128,2048]{1,0:T(8,128)(2,1)S(1)} %collective-permute-done.7.refs_0_), channel_id=1, source_target_pairs={{0,1},{1,0},{2,3},{3,2},{4,5},{5,4},{6,7},{7,6},{8,9},{9,8},{10,11... | collective-permute-start | bytes 1572872 | tf_op jit(solution)/shard_map/ppermute | solution.py:312
  114.9 10.5 %copy-start.6 = (bf16[128,2048]{1,0:T(8,128)(2,1)}, bf16[128,2048]{1,0:T(8,128)(2,1)S(1)}, u32[]{:S(2)}) copy-start(bf16[128,2048]{1,0:T(8,128)(2,1)S(1)} %collective-permute-done.4.refs_5_) | copy-start | bytes 1572868
  114.9 31.8 %collective-permute-start.12 = (bf16[128,2048]{1,0:T(8,128)(2,1)S(1)}, bf16[128,2048]{1,0:T(8,128)(2,1)S(1)}, u32[]{:S(2)}, u32[]{:S(2)}) collective-permute-start(bf16[128,2048]{1,0:T(8,128)(2,1)S(1)} %collective-permute-done.8.refs_1_), channel_id=1, source_target_pairs={{0,1},{1,0},{2,3},{3,2},{4,5},{5,4},{6,7},{7,6},{8,9},{9,8},{10,11... | collective-permute-start | bytes 1572872 | tf_op jit(solution)/shard_map/ppermute | solution.py:312
  115.4 10.0 %copy-start.7 = (bf16[128,2048]{1,0:T(8,128)(2,1)}, bf16[128,2048]{1,0:T(8,128)(2,1)S(1)}, u32[]{:S(2)}) copy-start(bf16[128,2048]{1,0:T(8,128)(2,1)S(1)} %collective-permute-done.5.refs_6_) | copy-start | bytes 1572868
  115.4 31.3 %collective-permute-start.13 = (bf16[128,2048]{1,0:T(8,128)(2,1)S(1)}, bf16[128,2048]{1,0:T(8,128)(2,1)S(1)}, u32[]{:S(2)}, u32[]{:S(2)}) collective-permute-start(bf16[128,2048]{1,0:T(8,128)(2,1)S(1)} %collective-permute-done.9.refs_2_), channel_id=1, source_target_pairs={{0,1},{1,0},{2,3},{3,2},{4,5},{5,4},{6,7},{7,6},{8,9},{9,8},{10,11... | collective-permute-start | bytes 1572872 | tf_op jit(solution)/shard_map/ppermute | solution.py:312
  124.7 22.0 %copy-start.5 = (bf16[128,2048]{1,0:T(8,128)(2,1)}, bf16[128,2048]{1,0:T(8,128)(2,1)S(1)}, u32[]{:S(2)}) copy-start(bf16[128,2048]{1,0:T(8,128)(2,1)S(1)} %collective-permute-done.10.refs_3_) | copy-start | bytes 1572868
  124.7 22.0 %collective-permute-start.14 = (bf16[128,2048]{1,0:T(8,128)(2,1)S(1)}, bf16[128,2048]{1,0:T(8,128)(2,1)S(1)}, u32[]{:S(2)}, u32[]{:S(2)}) collective-permute-start(bf16[128,2048]{1,0:T(8,128)(2,1)S(1)} %collective-permute-done.10.refs_3_), channel_id=1, source_target_pairs={{0,1},{1,0},{2,3},{3,2},{4,5},{5,4},{6,7},{7,6},{8,9},{9,8},{10,11... | collective-permute-start | bytes 1572872 | tf_op jit(solution)/shard_map/ppermute | solution.py:312
  125.4 0.8 copy-start.10
  146.7 0.8 copy-start.8
  146.7 1.0 copy-start.9
  146.7 1.1 copy-start.11
  147.9 0.8 copy-start.12
  169.1 1.3 copy-start
  180.0 24.6 %all-to-all-start.2 = ((f32[16,16,128]{2,1,0:T(8,128)}), f32[16,16,128]{2,1,0:T(8,128)S(1)}, u32[]{:S(2)}, u32[]{:S(2)}) async-start(f32[16,16,128]{2,1,0:T(8,128)} %get-tuple-element.15), calls=%async_computation.2 | async-start | bytes 262144 | tf_op jit(solution)/shard_map/all_to_all | solution.py:364

commit v3 on v1

v3 whole, which is shorter than its diff:
```python
import functools

import jax
import jax.numpy as jnp
from jax import lax
from jax.experimental import pallas as pl
from jax.experimental.pallas import tpu as pltpu
import numpy as np
from jax.sharding import PartitionSpec as P

MOST = 18
SUPER = 8
TILES = 9
GROUP = ("expert", "dp")
f32, bf16, i32 = jnp.float32, jnp.bfloat16, jnp.int32


SMEM = pl.BlockSpec(memory_space=pltpu.SMEM)
VMEM = pl.BlockSpec(memory_space=pltpu.VMEM)


def dot(a, b, dims=((1,), (0,))):
    return lax.dot_general(a, b, (dims, ((), ())), preferred_element_type=f32)


def iota(shape, dim):
    return lax.broadcasted_iota(i32, shape, dim)


def params(megabytes):
    return pltpu.CompilerParams(vmem_limit_bytes=megabytes * 2**20)


def cost(flops, nbytes):
    return pl.CostEstimate(flops=int(flops), bytes_accessed=int(nbytes), transcendentals=0)


def token_slots(routes_t, experts):
    top_k, tok = routes_t.shape
    numbers = iota((experts, tok), 0)
    named = jnp.zeros((experts, tok), f32)
    for k in range(top_k):
        named += jnp.where(routes_t[k : k + 1, :] == numbers, 1.0, 0.0)
    before = jnp.where(iota((tok, tok), 0) < iota((tok, tok), 1), 1.0, 0.0)
    return named, dot(named.astype(bf16), before.astype(bf16))


def pack_kernel(n_dp, half, routes_t, routes_flat, weights_flat, hidden, early, out, copies, target):
    del early
    ex = pl.program_id(0)
    experts = pl.num_programs(0) * 2 * half // MOST
    n_routes = routes_flat.shape[1]
    top_k, tok = routes_t.shape
    part = hidden.shape[1] // n_dp
    copies[...] = jnp.broadcast_to(routes_t[...][None], copies.shape)

    @pl.when(ex == 0)
    def _():
        _, slots = token_slots(routes_t[...], experts)
        shape = (tok, n_routes)
        spread = jnp.where(iota(shape, 1) // top_k == iota(shape, 0), 1.0, 0.0)
        slots = dot(slots.astype(bf16), spread.astype(bf16))
        numbers = iota((experts, n_routes), 0)
        rows = slots + (numbers * MOST).astype(f32)
        rows = jnp.where(routes_flat[...] == numbers, rows, 0.0)
        target[...] = jnp.sum(rows, axis=0, keepdims=True).astype(i32)

    weights = weights_flat[...].astype(f32)
    for side in range(2):
        first = ex * 2 * half + side * half
        chosen = target[...] - first == iota((half, n_routes), 0)
        chosen = jnp.where(chosen, weights, 0.0).astype(bf16)
        rows = dot(chosen, hidden[...]).astype(bf16)
        for d in range(n_dp):
            out[d, :, side * part : (side + 1) * part] = rows[:, d * part : (d + 1) * part]


def pack(routes_t, routes_flat, weights_flat, hidden, early, n_expert, n_dp, half):
    n_routes, units = hidden.shape
    part = units // n_dp
    whole = lambda shape: pl.BlockSpec(shape, lambda i: (0,) * len(shape))
    return pl.pallas_call(
        functools.partial(pack_kernel, n_dp, half),
        grid=(n_expert,),
        in_specs=[
            whole(routes_t.shape),
            whole(routes_flat.shape),
            whole(weights_flat.shape),
            whole(hidden.shape),
            pl.BlockSpec(memory_space=pl.ANY),
        ],
        out_specs=[
            pl.BlockSpec((n_dp, half, 2 * part), lambda i: (i, 0, 0)),
            pl.BlockSpec((n_dp,) + routes_t.shape, lambda i: (i, 0, 0)),
        ],
        out_shape=[
            jax.ShapeDtypeStruct((n_expert * n_dp, half, 2 * part), bf16),
            jax.ShapeDtypeStruct((n_expert * n_dp,) + routes_t.shape, i32),
        ],
        scratch_shapes=[pltpu.VMEM((1, n_routes), i32)],
        compiler_params=params(16),
        cost_estimate=cost(4 * n_expert * half * n_routes * units, 6 * n_routes * units),
    )(routes_t, routes_flat, weights_flat, hidden, early)


def after_kernel(*refs):
    pass


def after(array, *events):
    anywhere = pl.BlockSpec(memory_space=pl.ANY)
    return pl.pallas_call(
        after_kernel,
        in_specs=[anywhere] * (1 + len(events)),
        out_specs=anywhere,
        out_shape=jax.ShapeDtypeStruct(array.shape, array.dtype),
        input_output_aliases={0: 0},
    )(array, *events)


def tile_rows(i, rows):
    first = min(16 * i // MOST, SUPER - 2)
    place = 16 * i + iota((rows, 1), 0) % 16
    second = place >= MOST * (first + 1)
    slot = place - MOST * first - jnp.where(second, MOST, 0)
    return first, second, slot


def block_at(place, order, index):
    return place[0] ^ order[index] if order else pl.program_id(0) * SUPER + index


def gather_rows(order, place, routes_t, grads, out, start=0):
    tok = routes_t.shape[2]
    ex_local, _, width = out.shape
    rows = 16 * ex_local
    slots = []
    for b in range(SUPER):
        mine = routes_t[block_at(place, order, b)] - place[1]
        named, before = token_slots(mine, ex_local)
        slots.append(jnp.where(named > 0, before, -1.0))
    shape = (rows, ex_local)
    spread = jnp.where(iota(shape, 0) // 16 == iota(shape, 1), 1.0, 0.0).astype(bf16)
    step = min(512, width)
    for i in range(TILES):
        first, second, slot = tile_rows(i, rows)
        pair = jnp.concatenate([slots[first], slots[first + 1]], axis=1)
        pair = dot(spread, pair.astype(bf16))
        slot = slot.astype(f32)
        wanted = jnp.where(
            iota((rows, 2 * tok), 1) < tok,
            jnp.where(second, -5.0, slot),
            jnp.where(second, slot, -5.0),
        )
        chosen = jnp.where(pair == wanted, 1.0, 0.0).astype(bf16)
        near, far = grads(first), grads(first + 1)
        tile = start + 16 * i
        for c in range(0, width, step):
            here = slice(c, c + step)
            both = jnp.concatenate([near[:, here], far[:, here]], axis=0)
            found = dot(chosen, both).astype(bf16).reshape(ex_local, 16, step)
            out[:, tile : tile + 16, here] = found


def gather_kernel(place, routes_t, *refs):
    gather_rows(None, place, routes_t, lambda b: refs[b], refs[SUPER])


def gather(place, routes_t, grads, ex_local):
    blocks, top_k, tok = routes_t.shape
    width = grads.shape[1]
    tall = SUPER * MOST
    picked = lambda j: pl.BlockSpec((tok, width), lambda s: (SUPER * s + j, 0))
    return pl.pallas_call(
        gather_kernel,
        grid=(blocks // SUPER,),
        in_specs=[SMEM, pl.BlockSpec(routes_t.shape, lambda s: (0, 0, 0))]
        + [picked(j) for j in range(SUPER)],
        out_specs=pl.BlockSpec((ex_local, tall, width), lambda s: (0, s, 0)),
        out_shape=jax.ShapeDtypeStruct((ex_local, blocks * MOST, width), bf16),
        compiler_params=params(48),
    )(place, routes_t, *([grads] * SUPER))


def fetch(sources, held, sems):
    copies = [
        pltpu.make_async_copy(source, held.at[i], sems.at[i]) for i, source in enumerate(sources)
    ]
    for copy in copies:
        copy.start()
    waited = set()

    def block(i):
        if i not in waited:
            copies[i].wait()
            waited.add(i)
        return held.at[i]

    return block


def arrange_kernel(orders, ex_local, place, received, out):
    _, half, double = received.shape
    part = double // 2
    paired = ex_local % 2 == 0
    some = ex_local // 2 if paired else ex_local
    rows = 16 * some
    expert = iota((rows, 1), 0) // 16
    for i in range(TILES):
        first, second, slot = tile_rows(i, rows)
        block = jnp.where(second, half, 0)
        chosen = []
        for side in range(1 if paired else 2):
            spot = expert * MOST + slot - side * half
            column = jnp.where((spot >= 0) & (spot < half), block + spot, -1)
            hit = iota((rows, 2 * half), 1) == column
            chosen.append(jnp.where(hit, 1.0, 0.0).astype(bf16))
        for piece, order in enumerate(orders):
            pair = [received[block_at(place, order, first + b)] for b in range(2)]
            pair = jnp.concatenate(pair, axis=0)
            results = [dot(c, pair) for c in chosen]
            if paired:
                sides = [results[0][:, :part], results[0][:, part:]]
            else:
                sides = [results[0][:, :part] + results[1][:, part:]]
            tile = piece * SUPER * MOST + 16 * i
            for s, found in enumerate(sides):
                here = slice(s * some, (s + 1) * some)
                out[here, tile : tile + 16, :] = found.astype(bf16).reshape(some, 16, part)


def arrange(place, orders, received, ex_local):
    blocks, half, double = received.shape
    part = double // 2
    shape = (ex_local, blocks * MOST, part)
    kernel = functools.partial(arrange_kernel, orders, ex_local)
    if orders[0]:
        return pl.pallas_call(
            kernel,
            in_specs=[SMEM, VMEM],
            out_specs=VMEM,
            out_shape=jax.ShapeDtypeStruct(shape, bf16),
            compiler_params=params(24),
            cost_estimate=cost(4 * ex_local * blocks * MOST * half * double, 2**22),
        )(place, received)
    return pl.pallas_call(
        kernel,
        grid=(blocks // SUPER,),
        in_specs=[SMEM, pl.BlockSpec(received.shape, lambda s: (0, 0, 0))],
        out_specs=pl.BlockSpec((ex_local, SUPER * MOST, part), lambda s: (0, s, 0)),
        out_shape=jax.ShapeDtypeStruct(shape, bf16),
        compiler_params=params(32),
    )(place, received)


def back_rows(place, expert, hidden, grads, weights, sums):
    found = dot(grads, weights, ((1,), (1,)))
    total = jnp.sum(hidden.astype(f32) * found, axis=1, keepdims=True)
    sums[...] += jnp.where(iota(sums.shape, 1) == place[1] + expert, total, 0.0)


def back_kernel(place, hidden, grads, weights, out, sums):
    expert = pl.program_id(1)

    @pl.when(expert == 0)
    def _():
        sums[...] = jnp.zeros_like(sums)

    back_rows(place, expert, hidden[0], grads[0], weights[0], sums)

    @pl.when(expert == pl.num_programs(1) - 1)
    def _():
        for b in range(SUPER):
            out[b] = sums[b * MOST : (b + 1) * MOST, :]


def back(place, hidden, grads, weights):
    ex_local, rows, width = grads.shape
    part = weights.shape[1]
    tall = SUPER * MOST
    return pl.pallas_call(
        back_kernel,
        grid=(rows // tall, ex_local),
        in_specs=[
            SMEM,
            pl.BlockSpec((1, tall, part), lambda s, e: (e, s, 0)),
            pl.BlockSpec((1, tall, width), lambda s, e: (e, s, 0)),
            pl.BlockSpec((1, part, width), lambda s, e: (e, 0, 0)),
        ],
        out_specs=pl.BlockSpec((SUPER, MOST, 128), lambda s, e: (s, 0, 0)),
        out_shape=jax.ShapeDtypeStruct((rows // MOST, MOST, 128), f32),
        scratch_shapes=[pltpu.VMEM((tall, 128), f32)],
        compiler_params=params(32),
    )(place, hidden, grads, weights)


def gather_back_kernel(orders, place, routes_t, hidden, weights, *refs):
    piece = len(orders) - 1
    blocks, refs = refs[:SUPER], refs[SUPER:]
    earlier, (out, sums, held, rows, sems) = refs[:piece], refs[piece:]
    step = pl.program_id(0)

    @pl.when(step == 0)
    def _():
        sums[...] = jnp.zeros_like(sums)
        gather_rows(orders[-1], place, routes_t, fetch(blocks, held, sems), rows)

    for j in range(GROUPED):
        expert = step * GROUPED + j
        back_rows(place, expert, hidden[j], rows[expert], weights[j], sums)

    @pl.when(step == pl.num_programs(0) - 1)
    def _():
        for b in range(SUPER):
            mine = sums[b * MOST : (b + 1) * MOST, :]
            if earlier:
                out[block_at(place, orders[0], b)] = earlier[0][b]
                out[block_at(place, orders[1], b)] = mine
            else:
                out[b] = mine


def gather_back(place, orders, routes_t, hidden, weights, blocks, earlier):
    ex_local, part, width = weights.shape
    tok = blocks[0].shape[0]
    piece = len(orders) - 1
    tall = SUPER * MOST
    return pl.pallas_call(
        functools.partial(gather_back_kernel, orders),
        grid=(ex_local // GROUPED,),
        in_specs=[
            SMEM,
            VMEM,
            pl.BlockSpec((GROUPED, tall, part), lambda e: (e, piece, 0)),
            pl.BlockSpec((GROUPED, part, width), lambda e: (e, 0, 0)),
        ]
        + [pl.BlockSpec(memory_space=pl.ANY)] * SUPER
        + [VMEM] * len(earlier),
        out_specs=pl.BlockSpec((SUPER * (piece + 1), MOST, 128), lambda e: (0, 0, 0)),
        out_shape=jax.ShapeDtypeStruct((SUPER * (piece + 1), MOST, 128), f32),
        scratch_shapes=[
            pltpu.VMEM((tall, 128), f32),
            pltpu.VMEM((SUPER, tok, width), bf16),
            pltpu.VMEM((ex_local, tall, width), bf16),
            pltpu.SemaphoreType.DMA((SUPER,)),
        ],
        compiler_params=params(40),
        cost_estimate=cost(
            2 * ex_local * tall * width * (part + 2 * tok), 2 * ex_local * part * width
        ),
    )(place, routes_t, hidden, weights, *blocks, *earlier)


GROUPED = 2


def gather_outer_kernel(orders, place, routes_t, hidden, *refs):
    count = SUPER * len(orders)
    blocks, (out, held, rows, sems) = refs[:count], refs[count:]
    step = pl.program_id(0)
    width = out.shape[2]
    columns = min(512, width)

    @pl.when(step == 0)
    def _():
        block = fetch(blocks, held, sems)
        for piece, order in enumerate(orders):
            mine = lambda b, piece=piece: block(piece * SUPER + b)
            gather_rows(order, place, routes_t, mine, rows, piece * SUPER * MOST)

    for j in range(GROUPED):
        expert = step * GROUPED + j
        for c in range(0, width, columns):
            here = slice(c, c + columns)
            found = dot(hidden[j], rows[expert, :, here], ((0,), (0,)))
            out[j, :, here] = found.astype(bf16)


def gather_outer(place, orders, routes_t, hidden, blocks):
    ex_local, tall, part = hidden.shape
    tok, width = blocks[0].shape
    return pl.pallas_call(
        functools.partial(gather_outer_kernel, orders),
        grid=(ex_local // GROUPED,),
        in_specs=[SMEM, VMEM, pl.BlockSpec((GROUPED, tall, part), lambda e: (e, 0, 0))]
        + [pl.BlockSpec(memory_space=pl.ANY)] * len(blocks),
        out_specs=pl.BlockSpec((GROUPED, part, width), lambda e: (e, 0, 0)),
        out_shape=jax.ShapeDtypeStruct((ex_local, part, width), bf16),
        scratch_shapes=[
            pltpu.VMEM((len(blocks), tok, width), bf16),
            pltpu.VMEM((ex_local, tall, width), bf16),
            pltpu.SemaphoreType.DMA((len(blocks),)),
        ],
        compiler_params=params(52),
        cost_estimate=cost(
            2 * ex_local * tall * width * (part + 2 * tok), 2 * ex_local * part * width
        ),
    )(place, routes_t, hidden, *blocks)


def kept(array):
    return pltpu.with_memory_space_constraint(array, pltpu.VMEM)


def outer_kernel(hidden, grads, out, total):
    chunk = pl.program_id(1)

    @pl.when(chunk == 0)
    def _():
        total[...] = jnp.zeros_like(total)

    total[...] += dot(hidden[0], grads[0], ((0,), (0,)))

    @pl.when(chunk == pl.num_programs(1) - 1)
    def _():
        out[0] = total[...].astype(bf16)


def outer(hidden, grads):
    ex_local, rows, part = hidden.shape
    width = grads.shape[2]
    tall = SUPER * MOST
    return pl.pallas_call(
        outer_kernel,
        grid=(ex_local, rows // tall),
        in_specs=[
            pl.BlockSpec((1, tall, part), lambda e, c: (e, c, 0)),
            pl.BlockSpec((1, tall, width), lambda e, c: (e, c, 0)),
        ],
        out_specs=pl.BlockSpec((1, part, width), lambda e, c: (e, 0, 0)),
        out_shape=jax.ShapeDtypeStruct((ex_local, part, width), bf16),
        scratch_shapes=[pltpu.VMEM((part, width), f32)],
        compiler_params=params(32),
    )(hidden, grads)


def finish_kernel(experts, routes_t, weights_t, returned, out):
    top_k, tok = routes_t.shape
    total = jnp.sum(returned[...], axis=0)
    total = jnp.concatenate([total, jnp.zeros((128 - MOST, 128), f32)], axis=0)
    total = total.T[:experts]
    _, slots = token_slots(routes_t[...], experts)
    slots = slots.astype(i32)
    found = jnp.zeros((experts, tok), f32)
    for m in range(MOST):
        found = jnp.where(slots == m, total[:, m : m + 1], found)
    numbers = iota((experts, tok), 0)
    for k in range(top_k):
        mine = jnp.where(routes_t[k : k + 1, :] == numbers, found, 0.0)
        mine = jnp.sum(mine, axis=0, keepdims=True)
        out[k : k + 1, :] = mine / weights_t[k : k + 1, :].astype(f32)


def finish(routes_t, weights_t, returned, experts):
    return pl.pallas_call(
        functools.partial(finish_kernel, experts),
        out_shape=jax.ShapeDtypeStruct(routes_t.shape, f32),
        compiler_params=params(24),
        cost_estimate=cost(10000, 100000),
    )(routes_t, weights_t, returned)


def hop(block, axis, flip):
    size = lax.axis_size(axis)
    return lax.ppermute(block, axis, [(i, i ^ flip) for i in range(size)])


def body(routes, combine, hidden, d_out, w_down):
    n_expert = lax.axis_size("expert")
    n_dp = lax.axis_size("dp")
    ex_local = w_down.shape[0]
    experts = n_expert * ex_local
    tok, top_k = routes.shape
    half = ex_local * MOST // 2
    routes_t, weights_t = routes.T, combine.T
    n_routes = tok * top_k
    me, mine = lax.axis_index("expert") * n_dp + lax.axis_index("dp"), lax.axis_index("expert")
    place = jnp.stack([me, mine * ex_local]).astype(i32)
    small = (n_expert, n_dp) == (4, 4)
    trade = lambda x: lax.all_to_all(x, GROUP, split_axis=0, concat_axis=0, tiled=True)
    if small:
        near = hop(d_out, "expert", 1)
        side = hop(d_out, "dp", 2)
        far = hop(d_out, "expert", 2)
        twin = hop(d_out, "dp", 1)
    else:
        twin = d_out
    sent, copies = pack(
        routes_t,
        routes.reshape(1, n_routes),
        combine.reshape(1, n_routes),
        hidden.reshape(n_routes, hidden.shape[2]),
        twin,
        n_expert,
        n_dp,
        half,
    )
    all_routes = trade(copies)
    if small:
        received = trade(after(sent, near, side, far))
        near_side = hop(near, "dp", 2)
        far_side = hop(far, "dp", 2)
        both = hop(far, "expert", 1)
        both_side = hop(both, "dp", 2)
        early = [(0, d_out), (4, near), (2, side), (8, far)]
        late = [(6, near_side), (10, far_side), (12, both), (14, both_side)]
        early = early + [(1, twin)] + [(n + 1, hop(x, "dp", 1)) for n, x in early[1:]]
        late = late + [(n + 1, hop(x, "dp", 1)) for n, x in late]
        orders = [[n for n, _ in some] for some in (early, late)]
        blocks = [[x for _, x in some] for some in (early, late)]
        arranged = arrange(place, orders, received, ex_local)
        sums = []
        for i, some in enumerate(blocks):
            now = orders[: i + 1]
            sums = [gather_back(place, now, all_routes, arranged, w_down, some, sums)]
        sums = sums[0]
        d_w_down = gather_outer(place, orders, all_routes, arranged, sum(blocks, []))
    else:
        received = trade(sent)
        grads = lax.all_gather(d_out, GROUP, axis=0, tiled=True)
        grads = gather(place, all_routes, grads, ex_local)
        arranged = arrange(place, [None], received, ex_local)
        sums = back(place, arranged, grads, w_down)
        d_w_down = outer(arranged, grads)
    d_combine = finish(routes_t, weights_t, trade(sums), experts)
    return d_w_down, d_combine.T


def solution(mesh):
    placed = (
        P(("groups", "expert", "dp"), None),
        P(("groups", "expert", "dp"), None),
        P(("groups", "expert", "dp"), None, None),
        P(("groups", "expert", "dp"), None),
        P("expert", "dp", None),
    )
    return jax.shard_map(
        body,
        mesh=mesh,
        in_specs=placed,
        out_specs=(P(("groups", "expert"), "dp", None), P(("groups", "expert", "dp"), None)),
        check_vma=False,
    )
```

time: 195 us -> 160 us (0.82)
  waiting for transfers between devices: 85 us -> 58.3 us
  between operations: 14.1 us -> 0.9 us
  starting transfers between devices: 17 us -> 28.8 us
  local copies, waits for them, and re-layouts: 23.8 us -> 12.1 us
  Pallas kernels: 53 us -> 58.3 us
    all_gather x1 -> x0, waiting for transfers between devices: 84.3 us -> none  [body(): grads = lax.all_gather(d_out, GROUP, axis=0, tiled=True)]
    ppermute x0 -> x15, waiting for transfers between devices: none -> 58.3 us  [hop(): return lax.ppermute(block, axis, [(i, i ^ flip) for i in range(size)])]
    ppermute x0 -> x15, starting transfers between devices: none -> 14.2 us  [hop(): return lax.ppermute(block, axis, [(i, i ^ flip) for i in range(size)])]
    unnamed x20 -> x38, local copies, waits for them, and re-layouts: 22.3 us -> 11.9 us
    pallas_call x5 -> x6, Pallas kernels: 48.9 us -> 55 us  [the longest x2 31.6 us: gather_back(): pl.pallas_call(functools.partial(gather_back_kernel, orders), grid=(ex_lo...]
    all_to_all x3, starting transfers between devices: 17 us -> 14.6 us  [body(): lax.all_to_all(x, GROUP, split_axis=0, concat_axis=0, tiled=True)]
  transfers between devices with their start and end apart: 4 -> 18, of which waited for: 1 -> 4; matrix products, arithmetic and copies ran while one was open for 2% -> 1% of each run, Pallas kernels for 23% -> 26%
where the time goes in v3:
time: 160 us; the launch traced here: 159 us
  waiting for transfers between devices  58.3 us (36%)
  Pallas kernels  58.3 us (36%)
  starting transfers between devices  28.8 us (18%)
  local copies, waits for them, and re-layouts  12.1 us (8%)
    ppermute x15, waiting for transfers between devices, hop(): return lax.ppermute(block, axis, [(i, i ^ flip) for i in range(size)])  58.3 us
    pallas_call x2, Pallas kernels, gather_back(): pl.pallas_call(functools.partial(gather_back_kernel, orders), grid=(ex_lo...  31.6 us
    pallas_call x1, Pallas kernels, gather_outer(): pl.pallas_call(functools.partial(gather_outer_kernel, orders), grid=(ex_l...  20.5 us
    all_to_all x3, starting transfers between devices, body(): lax.all_to_all(x, GROUP, split_axis=0, concat_axis=0, tiled=True)  14.6 us
    ppermute x15, starting transfers between devices, hop(): return lax.ppermute(block, axis, [(i, i ^ flip) for i in range(size)])  14.2 us
    unnamed x38, local copies, waits for them, and re-layouts  11.9 us
    pallas_call x1, Pallas kernels, pack(): pl.pallas_call(functools.partial(pack_kernel, n_dp, half), grid=(n_expert...  3.3 us
  transfers between devices with their start and end apart: 18, of which 4 were waited for; matrix products, arithmetic and copies ran while one was open for 1% of the time, Pallas kernels for 26%

profile of v3, /device:TPU:0, one launch (start us, length us, event | category | flops | bytes accessed | tf_op | source)
XLA Modules:
  0.0 158.5 jit_solution(3077832608652316656)
XLA Ops:
  0.6 0.5 collective-permute-start
  1.1 3.7 %collective-permute-start.3 = (bf16[128,2048]{1,0:T(8,128)(2,1)}, bf16[128,2048]{1,0:T(8,128)(2,1)S(1)}, u32[]{:S(2)}, u32[]{:S(2)}) collective-permute-start(bf16[128,2048]{1,0:T(8,128)(2,1)} %refs_0_.3), channel_id=1, source_target_pairs={{0,8},{4,12},{8,0},{12,4},{1,9},{5,13},{9,1},{13,5},{2,10},{6,14},... | collective-permute-start | bytes 1572872 | tf_op jit(solution)/shard_map/ppermute | solution.py:465
  4.8 1.5 collective-permute-start.2
  6.3 1.6 collective-permute-start.1
  7.9 0.8 copy.11
  8.7 0.1 reshape.14.weights_flat
  8.8 0.8 copy.10
  9.6 0.1 reshape.13.routes_flat
  9.7 0.0 collective-permute-done.early.refs_4_
  9.7 0.0 copy-start.10
  9.7 0.0 copy-start.14
  9.7 0.7 copy-done.14
  10.4 1.4 copy-done.17
  11.8 3.3 %shard_map.68 = (bf16[16,144,384]{2,1,0:T(8,128)(2,1)S(1)}, s32[16,8,128]{2,1,0:T(8,128)}) custom-call(s32[8,128]{1,0:T(8,128)S(1)} %bitcast.6, s32[1,1024]{1,0:T(1,128)S(1)} %reshape.13.routes_flat, bf16[1,1024]{1,0:T(2,128)(2,1)S(1)} %reshape.14.weights_flat, bf16[1024,768]{1,0:T(8,128)(2,1)S(1)} %bitcast.9, ...), custom_call_target="tpu_custom_call" | custom-call | flops 1811939328 | bytes 4718592 | tf_op jit(solution)/shard_map/pallas_call | solution.py:82
  15.1 0.0 copy-done.10
  15.1 1.2 copy-done.1
  16.3 12.6 %collective-permute-done.3.refs_3_ = bf16[128,2048]{1,0:T(8,128)(2,1)S(1)} collective-permute-done((bf16[128,2048]{1,0:T(8,128)(2,1)}, bf16[128,2048]{1,0:T(8,128)(2,1)S(1)}, u32[]{:S(2)}, u32[]{:S(2)}) %collective-permute-start.3) | collective-permute-done | bytes 524320 | tf_op jit(solution)/shard_map/ppermute | solution.py:465
  28.9 0.0 collective-permute-done.2.refs_2_
  28.9 1.5 collective-permute-done.1.refs_1_
  30.4 5.3 %all-to-all-start.1 = ((bf16[16,144,384]{2,1,0:T(8,128)(2,1)}), bf16[16,144,384]{2,1,0:T(8,128)(2,1)S(1)}, u32[]{:S(2)}, u32[]{:S(2)}) async-start(bf16[16,144,384]{2,1,0:T(8,128)(2,1)} %shard_map.69), calls=%async_computation.1 | async-start | bytes 3538944 | tf_op jit(solution)/shard_map/all_to_all | solution.py:480
  35.7 2.0 %collective-permute-start.9 = (bf16[128,2048]{1,0:T(8,128)(2,1)S(1)}, bf16[128,2048]{1,0:T(8,128)(2,1)}, u32[]{:S(2)}, u32[]{:S(2)}) collective-permute-start(bf16[128,2048]{1,0:T(8,128)(2,1)S(1)} %copy-done.5), channel_id=1, source_target_pairs={{0,4},{4,0},{8,12},{12,8},{1,5},{5,1},{9,13},{13,9},{2,6},{6,2},{1... | collective-permute-start | bytes 1572872 | tf_op jit(solution)/shard_map/ppermute | solution.py:465
  37.7 1.5 collective-permute-start.8
  39.2 0.0 collective-permute-start.6
  39.2 0.5 collective-permute-start.5
  39.7 0.6 collective-permute-start.7
  40.3 38.5 %collective-permute-done.9.refs_10_.refs_2_ = bf16[128,2048]{1,0:T(8,128)(2,1)} collective-permute-done((bf16[128,2048]{1,0:T(8,128)(2,1)S(1)}, bf16[128,2048]{1,0:T(8,128)(2,1)}, u32[]{:S(2)}, u32[]{:S(2)}) %collective-permute-start.9) | collective-permute-done | bytes 524320 | tf_op jit(solution)/shard_map/ppermute | solution.py:465
  78.7 1.5 collective-permute-start.10
  80.2 0.0 collective-permute-done.8.refs_9_.refs_1_
  80.2 0.0 collective-permute-start.4
  80.2 0.0 all-to-all-done.1.received
  80.2 0.0 copy-start.2
  80.2 1.2 copy-done.2
  81.4 4.2 %all-to-all-start = ((s32[16,8,128]{2,1,0:T(8,128)}), s32[16,8,128]{2,1,0:T(8,128)S(1)}, u32[]{:S(2)}, u32[]{:S(2)}) async-start(s32[16,8,128]{2,1,0:T(8,128)} %get-tuple-element.4), calls=%async_computation | async-start | bytes 131072 | tf_op jit(solution)/shard_map/all_to_all | solution.py:480
  85.6 0.0 collective-permute-done.6.refs_7_
  85.6 0.8 copy-done.12
  86.4 0.4 collective-permute-start.13
  86.8 0.0 collective-permute-done.5.refs_6_
  86.8 0.1 collective-permute-start.12
  86.9 0.0 collective-permute-done.7.refs_8_.refs_0_
  86.9 0.4 collective-permute-start.11
  87.3 5.8 %collective-permute-done.10.refs_11_.refs_3_ = bf16[128,2048]{1,0:T(8,128)(2,1)} collective-permute-done((bf16[128,2048]{1,0:T(8,128)(2,1)}, bf16[128,2048]{1,0:T(8,128)(2,1)}, u32[]{:S(2)}, u32[]{:S(2)}) %collective-permute-start.10) | collective-permute-done | bytes 524320 | tf_op jit(solution)/shard_map/ppermute | solution.py:465
  93.1 0.0 collective-permute-start.14
  93.1 0.1 pad_add_fusion.place
  93.2 1.5 copy-done.3
  94.7 2.0 %shard_map.70.hidden = bf16[16,288,192]{2,1,0:T(8,128)(2,1)S(1)} custom-call(s32[2]{0:T(128)S(1)} %pad_add_fusion.place, bf16[16,144,384]{2,1,0:T(8,128)(2,1)S(1)} %copy-done.3), custom_call_target="tpu_custom_call" | custom-call | flops 1019215872 | bytes 4194304 | tf_op jit(solution)/shard_map/pallas_call | solution.py:238
  96.7 0.0 all-to-all-done.routes_t
  96.7 0.0 collective-permute-done.4.refs_5_
  96.7 0.0 copy-start.8
  96.7 1.4 copy-done.8
  98.1 1.0 copy-done.11
  99.2 1.0 copy-done.13
  100.2 15.4 %shard_map.72.refs_8_ = f32[8,18,128]{2,1,0:T(8,128)S(1)} custom-call(s32[2]{0:T(128)S(1)} %pad_add_fusion.place, s32[16,8,128]{2,1,0:T(8,128)S(1)} %all-to-all-done.routes_t, bf16[16,288,192]{2,1,0:T(8,128)(2,1)S(1)} %shard_map.70.hidden, bf16[16,192,2048]{2,1,0:T(8,128)(2,1)} %weights.3, bf16[128,2048]{1,0:T(8,128)(2,1)S(1)} %copy-done.8, ...), custom_call_target="tpu_custom_call" | custom-call | flops 4227858432 | bytes 12582912 | tf_op jit(solution)/shard_map/pallas_call | solution.py:328
  115.6 0.0 copy-start.9
  115.6 0.0 collective-permute-done.13.refs_14_.refs_6_
  115.6 0.0 collective-permute-done.12.refs_13_.refs_5_
  115.6 0.0 collective-permute-done.11.refs_12_.refs_4_
  115.6 0.0 collective-permute-done.14.refs_15_.refs_7_
  115.6 16.2 %shard_map.73 = f32[16,18,128]{2,1,0:T(8,128)} custom-call(s32[2]{0:T(128)S(1)} %pad_add_fusion.place, s32[16,8,128]{2,1,0:T(8,128)S(1)} %all-to-all-done.routes_t, bf16[16,288,192]{2,1,0:T(8,128)(2,1)S(1)} %shard_map.70.hidden, bf16[16,192,2048]{2,1,0:T(8,128)(2,1)} %weights.3, bf16[128,2048]{1,0:T(8,128)(2,1)} %collective-permute-done.7.refs_8_.refs_0_, ...), custom_call_target="tpu_custom_call" | custom-call | flops 4227858432 | bytes 12582912 | tf_op jit(solution)/shard_map/pallas_call | solution.py:328
  131.9 5.1 %all-to-all-start.2 = ((f32[16,18,128]{2,1,0:T(8,128)}), f32[16,18,128]{2,1,0:T(8,128)S(1)}, u32[]{:S(2)}, u32[]{:S(2)}) async-start(f32[16,18,128]{2,1,0:T(8,128)} %shard_map.73), calls=%async_computation.2 | async-start | bytes 393216 | tf_op jit(solution)/shard_map/all_to_all | solution.py:480
  137.0 0.0 copy-start.15
  137.0 0.0 copy-start.16
  137.0 20.5 %shard_map.71 = bf16[16,192,2048]{2,1,0:T(8,128)(2,1)} custom-call(s32[2]{0:T(128)S(1)} %pad_add_fusion.place, s32[16,8,128]{2,1,0:T(8,128)S(1)} %all-to-all-done.routes_t, bf16[16,288,192]{2,1,0:T(8,128)(2,1)} %copy-done, bf16[128,2048]{1,0:T(8,128)(2,1)S(1)} %copy-done.9, bf16[128,2048]{1,0:T(8,128)(2,1)} %collective-permute-done.1.refs_1_, ...), custom_call_target="tpu_custom_call" | custom-call | flops 8455716864 | bytes 12582912 | tf_op jit(solution)/shard_map/pallas_call | solution.py:382
  157.5 0.0 all-to-all-done.2.returned
  157.6 1.0 shard_map.74
  (20 shorter events, 0.0 us)
Async XLA Ops:
  0.6 9.0 %collective-permute-start = (bf16[128,2048]{1,0:T(8,128)(2,1)}, bf16[128,2048]{1,0:T(8,128)(2,1)S(1)}, u32[]{:S(2)}, u32[]{:S(2)}) collective-permute-start(bf16[128,2048]{1,0:T(8,128)(2,1)} %refs_0_.3), channel_id=1, source_target_pairs={{0,1},{1,0},{2,3},{3,2},{4,5},{5,4},{6,7},{7,6},{8,9},{9,8},{10,11... | collective-permute-start | bytes 1572872 | tf_op jit(solution)/shard_map/ppermute | solution.py:465
  1.1 27.7 %collective-permute-start.3 = (bf16[128,2048]{1,0:T(8,128)(2,1)}, bf16[128,2048]{1,0:T(8,128)(2,1)S(1)}, u32[]{:S(2)}, u32[]{:S(2)}) collective-permute-start(bf16[128,2048]{1,0:T(8,128)(2,1)} %refs_0_.3), channel_id=1, source_target_pairs={{0,8},{4,12},{8,0},{12,4},{1,9},{5,13},{9,1},{13,5},{2,10},{6,14},... | collective-permute-start | bytes 1572872 | tf_op jit(solution)/shard_map/ppermute | solution.py:465
  4.8 24.1 %collective-permute-start.2 = (bf16[128,2048]{1,0:T(8,128)(2,1)}, bf16[128,2048]{1,0:T(8,128)(2,1)S(1)}, u32[]{:S(2)}, u32[]{:S(2)}) collective-permute-start(bf16[128,2048]{1,0:T(8,128)(2,1)} %refs_0_.3), channel_id=1, source_target_pairs={{0,2},{1,3},{2,0},{3,1},{4,6},{5,7},{6,4},{7,5},{8,10},{9,11},{10,... | collective-permute-start | bytes 1572872 | tf_op jit(solution)/shard_map/ppermute | solution.py:465
  6.3 24.1 %collective-permute-start.1 = (bf16[128,2048]{1,0:T(8,128)(2,1)}, bf16[128,2048]{1,0:T(8,128)(2,1)}, u32[]{:S(2)}, u32[]{:S(2)}) collective-permute-start(bf16[128,2048]{1,0:T(8,128)(2,1)} %refs_0_.3), channel_id=1, source_target_pairs={{0,4},{4,0},{8,12},{12,8},{1,5},{5,1},{9,13},{13,9},{2,6},{6,2},{1... | collective-permute-start | bytes 1572872 | tf_op jit(solution)/shard_map/ppermute | solution.py:465
  9.7 5.4 %copy-start.10 = (bf16[128,2048]{1,0:T(8,128)(2,1)}, bf16[128,2048]{1,0:T(8,128)(2,1)S(1)}, u32[]{:S(2)}) copy-start(bf16[128,2048]{1,0:T(8,128)(2,1)S(1)} %collective-permute-done.early.refs_4_) | copy-start | bytes 1572868
  9.7 0.7 copy-start.14
  10.4 1.4 copy-start.17
  15.1 1.2 copy-start.1
  28.9 1.5 copy-start.4
  28.9 1.5 copy-start.6
  30.4 5.3 %copy-start.5 = (bf16[128,2048]{1,0:T(8,128)(2,1)S(1)}, bf16[128,2048]{1,0:T(8,128)(2,1)}, u32[]{:S(2)}) copy-start(bf16[128,2048]{1,0:T(8,128)(2,1)} %copy-done.4) | copy-start | bytes 1572868
  30.4 8.8 %copy-start.7 = (bf16[128,2048]{1,0:T(8,128)(2,1)S(1)}, bf16[128,2048]{1,0:T(8,128)(2,1)}, u32[]{:S(2)}) copy-start(bf16[128,2048]{1,0:T(8,128)(2,1)} %copy-done.6) | copy-start | bytes 1572868
  30.4 49.8 %all-to-all-start.1 = ((bf16[16,144,384]{2,1,0:T(8,128)(2,1)}), bf16[16,144,384]{2,1,0:T(8,128)(2,1)S(1)}, u32[]{:S(2)}, u32[]{:S(2)}) async-start(bf16[16,144,384]{2,1,0:T(8,128)(2,1)} %shard_map.69), calls=%async_computation.1 | async-start | bytes 3538944 | tf_op jit(solution)/shard_map/all_to_all | solution.py:480
  35.7 43.0 %collective-permute-start.9 = (bf16[128,2048]{1,0:T(8,128)(2,1)S(1)}, bf16[128,2048]{1,0:T(8,128)(2,1)}, u32[]{:S(2)}, u32[]{:S(2)}) collective-permute-start(bf16[128,2048]{1,0:T(8,128)(2,1)S(1)} %copy-done.5), channel_id=1, source_target_pairs={{0,4},{4,0},{8,12},{12,8},{1,5},{5,1},{9,13},{13,9},{2,6},{6,2},{1... | collective-permute-start | bytes 1572872 | tf_op jit(solution)/shard_map/ppermute | solution.py:465
  37.7 42.5 %collective-permute-start.8 = (bf16[128,2048]{1,0:T(8,128)(2,1)S(1)}, bf16[128,2048]{1,0:T(8,128)(2,1)}, u32[]{:S(2)}, u32[]{:S(2)}) collective-permute-start(bf16[128,2048]{1,0:T(8,128)(2,1)S(1)} %copy-done.5), channel_id=1, source_target_pairs={{0,2},{1,3},{2,0},{3,1},{4,6},{5,7},{6,4},{7,5},{8,10},{9,11},{10,... | collective-permute-start | bytes 1572872 | tf_op jit(solution)/shard_map/ppermute | solution.py:465
  39.2 46.4 %collective-permute-start.6 = (bf16[128,2048]{1,0:T(8,128)(2,1)S(1)}, bf16[128,2048]{1,0:T(8,128)(2,1)S(1)}, u32[]{:S(2)}, u32[]{:S(2)}) collective-permute-start(bf16[128,2048]{1,0:T(8,128)(2,1)S(1)} %copy-done.5), channel_id=1, source_target_pairs={{0,1},{1,0},{2,3},{3,2},{4,5},{5,4},{6,7},{7,6},{8,9},{9,8},{10,11... | collective-permute-start | bytes 1572872 | tf_op jit(solution)/shard_map/ppermute | solution.py:465
  39.2 47.6 %collective-permute-start.5 = (bf16[128,2048]{1,0:T(8,128)(2,1)S(1)}, bf16[128,2048]{1,0:T(8,128)(2,1)}, u32[]{:S(2)}, u32[]{:S(2)}) collective-permute-start(bf16[128,2048]{1,0:T(8,128)(2,1)S(1)} %copy-done.7), channel_id=1, source_target_pairs={{0,1},{1,0},{2,3},{3,2},{4,5},{5,4},{6,7},{7,6},{8,9},{9,8},{10,11... | collective-permute-start | bytes 1572872 | tf_op jit(solution)/shard_map/ppermute | solution.py:465
  39.7 47.2 %collective-permute-start.7 = (bf16[128,2048]{1,0:T(8,128)(2,1)}, bf16[128,2048]{1,0:T(8,128)(2,1)}, u32[]{:S(2)}, u32[]{:S(2)}) collective-permute-start(bf16[128,2048]{1,0:T(8,128)(2,1)} %collective-permute-done.1.refs_1_), channel_id=1, source_target_pairs={{0,2},{1,3},{2,0},{3,1},{4,6},{5,7},{6,4},{7,5},{8,10},{9,11},{10,... | collective-permute-start | bytes 1572872 | tf_op jit(solution)/shard_map/ppermute | solution.py:465
  78.7 14.4 %collective-permute-start.10 = (bf16[128,2048]{1,0:T(8,128)(2,1)}, bf16[128,2048]{1,0:T(8,128)(2,1)}, u32[]{:S(2)}, u32[]{:S(2)}) collective-permute-start(bf16[128,2048]{1,0:T(8,128)(2,1)} %collective-permute-done.9.refs_10_.refs_2_), channel_id=1, source_target_pairs={{0,2},{1,3},{2,0},{3,1},{4,6},{5,7},{6,4},{7,5},{8,10},{9,11},{10,... | collective-permute-start | bytes 1572872 | tf_op jit(solution)/shard_map/ppermute | solution.py:465
  80.2 16.5 %collective-permute-start.4 = (bf16[128,2048]{1,0:T(8,128)(2,1)}, bf16[128,2048]{1,0:T(8,128)(2,1)}, u32[]{:S(2)}, u32[]{:S(2)}) collective-permute-start(bf16[128,2048]{1,0:T(8,128)(2,1)} %collective-permute-done.1.refs_1_), channel_id=1, source_target_pairs={{0,1},{1,0},{2,3},{3,2},{4,5},{5,4},{6,7},{7,6},{8,9},{9,8},{10,11... | collective-permute-start | bytes 1572872 | tf_op jit(solution)/shard_map/ppermute | solution.py:465
  80.2 1.2 copy-start.2
  81.4 15.3 %all-to-all-start = ((s32[16,8,128]{2,1,0:T(8,128)}), s32[16,8,128]{2,1,0:T(8,128)S(1)}, u32[]{:S(2)}, u32[]{:S(2)}) async-start(s32[16,8,128]{2,1,0:T(8,128)} %get-tuple-element.4), calls=%async_computation | async-start | bytes 131072 | tf_op jit(solution)/shard_map/all_to_all | solution.py:480
  85.6 0.8 copy-start.12
  86.4 29.2 %collective-permute-start.13 = (bf16[128,2048]{1,0:T(8,128)(2,1)}, bf16[128,2048]{1,0:T(8,128)(2,1)}, u32[]{:S(2)}, u32[]{:S(2)}) collective-permute-start(bf16[128,2048]{1,0:T(8,128)(2,1)} %collective-permute-done.9.refs_10_.refs_2_), channel_id=1, source_target_pairs={{0,1},{1,0},{2,3},{3,2},{4,5},{5,4},{6,7},{7,6},{8,9},{9,8},{10,11... | collective-permute-start | bytes 1572872 | tf_op jit(solution)/shard_map/ppermute | solution.py:465
  86.8 28.8 %collective-permute-start.12 = (bf16[128,2048]{1,0:T(8,128)(2,1)}, bf16[128,2048]{1,0:T(8,128)(2,1)}, u32[]{:S(2)}, u32[]{:S(2)}) collective-permute-start(bf16[128,2048]{1,0:T(8,128)(2,1)} %collective-permute-done.8.refs_9_.refs_1_), channel_id=1, source_target_pairs={{0,1},{1,0},{2,3},{3,2},{4,5},{5,4},{6,7},{7,6},{8,9},{9,8},{10,11... | collective-permute-start | bytes 1572872 | tf_op jit(solution)/shard_map/ppermute | solution.py:465
  86.9 28.7 %collective-permute-start.11 = (bf16[128,2048]{1,0:T(8,128)(2,1)}, bf16[128,2048]{1,0:T(8,128)(2,1)}, u32[]{:S(2)}, u32[]{:S(2)}) collective-permute-start(bf16[128,2048]{1,0:T(8,128)(2,1)} %collective-permute-done.7.refs_8_.refs_0_), channel_id=1, source_target_pairs={{0,1},{1,0},{2,3},{3,2},{4,5},{5,4},{6,7},{7,6},{8,9},{9,8},{10,11... | collective-permute-start | bytes 1572872 | tf_op jit(solution)/shard_map/ppermute | solution.py:465
  93.1 22.5 %collective-permute-start.14 = (bf16[128,2048]{1,0:T(8,128)(2,1)}, bf16[128,2048]{1,0:T(8,128)(2,1)}, u32[]{:S(2)}, u32[]{:S(2)}) collective-permute-start(bf16[128,2048]{1,0:T(8,128)(2,1)} %collective-permute-done.10.refs_11_.refs_3_), channel_id=1, source_target_pairs={{0,1},{1,0},{2,3},{3,2},{4,5},{5,4},{6,7},{7,6},{8,9},{9,8},{10,11... | collective-permute-start | bytes 1572872 | tf_op jit(solution)/shard_map/ppermute | solution.py:465
  93.2 1.5 copy-start.3
  96.7 19.0 %copy-start = (bf16[16,288,192]{2,1,0:T(8,128)(2,1)}, bf16[16,288,192]{2,1,0:T(8,128)(2,1)S(1)}, u32[]{:S(2)}) copy-start(bf16[16,288,192]{2,1,0:T(8,128)(2,1)S(1)} %shard_map.70.hidden) | copy-start | bytes 5308420
  96.7 1.4 copy-start.8
  98.1 1.0 copy-start.11
  99.2 1.0 copy-start.13
  115.6 21.4 %copy-start.9 = (bf16[128,2048]{1,0:T(8,128)(2,1)S(1)}, bf16[128,2048]{1,0:T(8,128)(2,1)}, u32[]{:S(2)}) copy-start(bf16[128,2048]{1,0:T(8,128)(2,1)} %refs_0_.3) | copy-start | bytes 1572868
  131.9 25.7 %all-to-all-start.2 = ((f32[16,18,128]{2,1,0:T(8,128)}), f32[16,18,128]{2,1,0:T(8,128)S(1)}, u32[]{:S(2)}, u32[]{:S(2)}) async-start(f32[16,18,128]{2,1,0:T(8,128)} %shard_map.73), calls=%async_computation.2 | async-start | bytes 393216 | tf_op jit(solution)/shard_map/all_to_all | solution.py:480
  137.0 20.5 %copy-start.15 = (s32[128,8]{0,1:T(8,128)S(1)}, s32[128,8]{0,1:T(8,128)}, u32[]{:S(2)}) copy-start(s32[128,8]{0,1:T(8,128)} %param.5) | copy-start | bytes 12292
  137.0 20.5 %copy-start.16 = (bf16[128,8]{0,1:T(8,128)(2,1)S(1)}, bf16[128,8]{0,1:T(8,128)(2,1)}, u32[]{:S(2)}) copy-start(bf16[128,8]{0,1:T(8,128)(2,1)} %param.6) | copy-start | bytes 6148

commit v4 on v3

--- a/solution.py
+++ b/solution.py
@@ -294,61 +294,90 @@
     )(place, hidden, grads, weights)
 
 
-def gather_back_kernel(orders, place, routes_t, hidden, weights, *refs):
-    piece = len(orders) - 1
-    blocks, refs = refs[:SUPER], refs[SUPER:]
-    earlier, (out, sums, held, rows, sems) = refs[:piece], refs[piece:]
+def early_kernel(order, place, routes_t, weights, *refs):
+    blocks, (out, held, rows, sems) = refs[:SUPER], refs[SUPER:]
     step = pl.program_id(0)
 
     @pl.when(step == 0)
     def _():
+        gather_rows(order, place, routes_t, fetch(blocks, held, sems), rows)
+
+    for j in range(GROUPED):
+        out[j] = dot(rows[step * GROUPED + j], weights[j], ((1,), (1,)))
+
+
+def late_kernel(orders, place, routes_t, weights, hidden, backs, *refs):
+    blocks, (out, sums, held, rows, sems) = refs[:SUPER], refs[SUPER:]
+    step = pl.program_id(0)
+    tall, width = rows.shape[1:]
+    columns = min(512, width)
+
+    @pl.when(step == 0)
+    def _():
         sums[...] = jnp.zeros_like(sums)
-        gather_rows(orders[-1], place, routes_t, fetch(blocks, held, sems), rows)
-
+        gather_rows(orders[1], place, routes_t, fetch(blocks, held, sems), rows)
+
+    lane = iota((tall, 128), 1) - place[1]
     for j in range(GROUPED):
         expert = step * GROUPED + j
-        back_rows(place, expert, hidden[j], rows[expert], weights[j], sums)
+        found = hidden[j, :tall, :].astype(f32) * backs[j]
+        total = jnp.sum(found, axis=1, keepdims=True)
+        sums[:tall, :] += jnp.where(lane == expert, total, 0.0)
+        mine = hidden[j, tall:, :]
+        found = jnp.zeros((tall, 128), f32)
+        for c in range(0, width, columns):
+            here = slice(c, c + columns)
+            part = dot(mine, weights[j, :, here]) * rows[expert, :, here].astype(f32)
+            for piece in range(0, columns, 128):
+                found += part[:, piece : piece + 128]
+        total = jnp.sum(found, axis=1, keepdims=True)
+        sums[tall:, :] += jnp.where(lane == expert, total, 0.0)
 
     @pl.when(step == pl.num_programs(0) - 1)
     def _():
-        for b in range(SUPER):
-            mine = sums[b * MOST : (b + 1) * MOST, :]
-            if earlier:
-                out[block_at(place, orders[0], b)] = earlier[0][b]
-                out[block_at(place, orders[1], b)] = mine
-            else:
-                out[b] = mine
-
-
-def gather_back(place, orders, routes_t, hidden, weights, blocks, earlier):
+        for i, order in enumerate(orders):
+            for b in range(SUPER):
+                start = (i * SUPER + b) * MOST
+                out[block_at(place, order, b)] = sums[start : start + MOST, :]
+
+
+def gather_back(place, orders, routes_t, weights, blocks, hidden=None, backs=None):
     ex_local, part, width = weights.shape
     tok = blocks[0].shape[0]
-    piece = len(orders) - 1
     tall = SUPER * MOST
-    return pl.pallas_call(
-        functools.partial(gather_back_kernel, orders),
+    scratch = [
+        pltpu.VMEM((SUPER, tok, width), bf16),
+        pltpu.VMEM((ex_local, tall, width), bf16),
+        pltpu.SemaphoreType.DMA((SUPER,)),
+    ]
+    grouped = lambda rows, columns: pl.BlockSpec((GROUPED, rows, columns), lambda e: (e, 0, 0))
+    in_specs = [SMEM, VMEM, grouped(part, width)]
+    anywhere = [pl.BlockSpec(memory_space=pl.ANY)] * SUPER
+    rest = dict(
         grid=(ex_local // GROUPED,),
-        in_specs=[
-            SMEM,
-            VMEM,
-            pl.BlockSpec((GROUPED, tall, part), lambda e: (e, piece, 0)),
-            pl.BlockSpec((GROUPED, part, width), lambda e: (e, 0, 0)),
-        ]
-        + [pl.BlockSpec(memory_space=pl.ANY)] * SUPER
-        + [VMEM] * len(earlier),
-        out_specs=pl.BlockSpec((SUPER * (piece + 1), MOST, 128), lambda e: (0, 0, 0)),
-        out_shape=jax.ShapeDtypeStruct((SUPER * (piece + 1), MOST, 128), f32),
-        scratch_shapes=[
-            pltpu.VMEM((tall, 128), f32),
-            pltpu.VMEM((SUPER, tok, width), bf16),
-            pltpu.VMEM((ex_local, tall, width), bf16),
-            pltpu.SemaphoreType.DMA((SUPER,)),
-        ],
         compiler_params=params(40),
         cost_estimate=cost(
             2 * ex_local * tall * width * (part + 2 * tok), 2 * ex_local * part * width
         ),
-    )(place, routes_t, hidden, weights, *blocks, *earlier)
+    )
+    if hidden is None:
+        return pl.pallas_call(
+            functools.partial(early_kernel, orders[0]),
+            in_specs=in_specs + anywhere,
+            out_specs=grouped(tall, part),
+            out_shape=jax.ShapeDtypeStruct((ex_local, tall, part), f32),
+            scratch_shapes=scratch,
+            **rest,
+        )(place, routes_t, weights, *blocks)
+    count = SUPER * len(orders)
+    return pl.pallas_call(
+        functools.partial(late_kernel, orders),
+        in_specs=in_specs + [grouped(2 * tall, part), grouped(tall, part)] + anywhere,
+        out_specs=pl.BlockSpec((count, MOST, 128), lambda e: (0, 0, 0)),
+        out_shape=jax.ShapeDtypeStruct((count, MOST, 128), f32),
+        scratch_shapes=[pltpu.VMEM((2 * tall, 128), f32)] + scratch,
+        **rest,
+    )(place, routes_t, weights, hidden, backs, *blocks)
 
 
 GROUPED = 2
@@ -497,24 +526,22 @@
     )
     all_routes = trade(copies)
     if small:
-        received = trade(after(sent, near, side, far))
+        near_twin, side_twin, far_twin = [hop(x, "dp", 1) for x in (near, side, far)]
+        early = [(0, d_out), (4, near), (2, side), (8, far)]
+        early += [(1, twin), (5, near_twin), (3, side_twin), (9, far_twin)]
         near_side = hop(near, "dp", 2)
         far_side = hop(far, "dp", 2)
         both = hop(far, "expert", 1)
-        both_side = hop(both, "dp", 2)
-        early = [(0, d_out), (4, near), (2, side), (8, far)]
-        late = [(6, near_side), (10, far_side), (12, both), (14, both_side)]
-        early = early + [(1, twin)] + [(n + 1, hop(x, "dp", 1)) for n, x in early[1:]]
-        late = late + [(n + 1, hop(x, "dp", 1)) for n, x in late]
-        orders = [[n for n, _ in some] for some in (early, late)]
-        blocks = [[x for _, x in some] for some in (early, late)]
+        received = trade(after(sent, near, side, far))
+        orders = [[n for n, _ in early], [6, 10, 12, 14, 7, 11, 13, 15]]
+        early = [x for _, x in early]
+        backs = gather_back(place, orders, all_routes, w_down, early)
+        both_side = hop(after(both, backs), "dp", 2)
         arranged = arrange(place, orders, received, ex_local)
-        sums = []
-        for i, some in enumerate(blocks):
-            now = orders[: i + 1]
-            sums = [gather_back(place, now, all_routes, arranged, w_down, some, sums)]
-        sums = sums[0]
-        d_w_down = gather_outer(place, orders, all_routes, arranged, sum(blocks, []))
+        late = [near_side, far_side, both, after(both_side, arranged)]
+        late += [hop(x, "dp", 1) for x in late]
+        sums = gather_back(place, orders, all_routes, w_down, late, arranged, backs)
+        d_w_down = gather_outer(place, orders, all_routes, arranged, early + late)
     else:
         received = trade(sent)
         grads = lax.all_gather(d_out, GROUP, axis=0, tiled=True)

time: 160 us -> 143 us (0.89)
  waiting for transfers between devices: 58.3 us -> 42.4 us
  local copies, waits for them, and re-layouts: 12.1 us -> 16.9 us
  Pallas kernels: 58.3 us -> 54.6 us
  starting transfers between devices: 28.8 us -> 26.7 us
    ppermute x15, waiting for transfers between devices: 58.3 us -> 42.4 us  [hop(): return lax.ppermute(block, axis, [(i, i ^ flip) for i in range(size)])]
    unnamed x38 -> x47, local copies, waits for them, and re-layouts: 11.9 us -> 16.7 us
    pallas_call x2, Pallas kernels: 31.6 us -> 28.5 us  [the longest x1 14.5 us: gather_back(): pl.pallas_call(functools.partial(late_kernel, orders), in_specs=in_specs...]
    all_to_all x3, starting transfers between devices: 14.6 us -> 12.7 us  [body(): lax.all_to_all(x, GROUP, split_axis=0, concat_axis=0, tiled=True)]
  transfers between devices with their start and end apart: 18 -> 18, of which waited for: 4 -> 5; matrix products, arithmetic and copies ran while one was open for 1% -> 3% of each run, Pallas kernels for 26% -> 28%
where the time goes in v4:
time: 143 us; the launch traced here: 142 us
  Pallas kernels  54.6 us (38%)
  waiting for transfers between devices  42.4 us (30%)
  starting transfers between devices  26.7 us (19%)
  local copies, waits for them, and re-layouts  16.9 us (12%)
    ppermute x15, waiting for transfers between devices, hop(): return lax.ppermute(block, axis, [(i, i ^ flip) for i in range(size)])  42.4 us
    pallas_call x1, Pallas kernels, gather_outer(): pl.pallas_call(functools.partial(gather_outer_kernel, orders), grid=(ex_l...  19.9 us
    unnamed x47, local copies, waits for them, and re-layouts  16.7 us
    pallas_call x1, Pallas kernels, gather_back(): pl.pallas_call(functools.partial(late_kernel, orders), in_specs=in_specs...  14.5 us
    pallas_call x1, Pallas kernels, gather_back(): pl.pallas_call(functools.partial(early_kernel, orders[0]), in_specs=in_sp...  14 us
    ppermute x15, starting transfers between devices, hop(): return lax.ppermute(block, axis, [(i, i ^ flip) for i in range(size)])  14 us
    all_to_all x3, starting transfers between devices, body(): lax.all_to_all(x, GROUP, split_axis=0, concat_axis=0, tiled=True)  12.7 us
    pallas_call x1, Pallas kernels, pack(): pl.pallas_call(functools.partial(pack_kernel, n_dp, half), grid=(n_expert...  3.27 us
  transfers between devices with their start and end apart: 18, of which 5 were waited for; matrix products, arithmetic and copies ran while one was open for 3% of the time, Pallas kernels for 28%

profile of v4, /device:TPU:0, one launch (start us, length us, event | category | flops | bytes accessed | tf_op | source)
XLA Modules:
  0.0 141.6 jit_solution(4709864521782419361)
XLA Ops:
  0.6 0.5 collective-permute-start
  1.1 3.7 %collective-permute-start.3 = (bf16[128,2048]{1,0:T(8,128)(2,1)}, bf16[128,2048]{1,0:T(8,128)(2,1)S(1)}, u32[]{:S(2)}, u32[]{:S(2)}) collective-permute-start(bf16[128,2048]{1,0:T(8,128)(2,1)} %refs_0_.3), channel_id=1, source_target_pairs={{0,8},{4,12},{8,0},{12,4},{1,9},{5,13},{9,1},{13,5},{2,10},{6,14},... | collective-permute-start | bytes 1572872 | tf_op jit(solution)/shard_map/ppermute | solution.py:494
  4.8 1.5 %collective-permute-start.2 = (bf16[128,2048]{1,0:T(8,128)(2,1)}, bf16[128,2048]{1,0:T(8,128)(2,1)S(1)}, u32[]{:S(2)}, u32[]{:S(2)}) collective-permute-start(bf16[128,2048]{1,0:T(8,128)(2,1)} %refs_0_.3), channel_id=1, source_target_pairs={{0,2},{1,3},{2,0},{3,1},{4,6},{5,7},{6,4},{7,5},{8,10},{9,11},{10,... | collective-permute-start | bytes 1572872 | tf_op jit(solution)/shard_map/ppermute | solution.py:494
  6.3 1.6 %collective-permute-start.1 = (bf16[128,2048]{1,0:T(8,128)(2,1)}, bf16[128,2048]{1,0:T(8,128)(2,1)S(1)}, u32[]{:S(2)}, u32[]{:S(2)}) collective-permute-start(bf16[128,2048]{1,0:T(8,128)(2,1)} %refs_0_.3), channel_id=1, source_target_pairs={{0,4},{4,0},{8,12},{12,8},{1,5},{5,1},{9,13},{13,9},{2,6},{6,2},{1... | collective-permute-start | bytes 1572872 | tf_op jit(solution)/shard_map/ppermute | solution.py:494
  7.9 0.8 copy.13
  8.7 0.1 reshape.14.weights_flat
  8.8 0.8 copy.12
  9.6 0.1 reshape.13.routes_flat
  9.7 0.0 collective-permute-done.early.refs_4_
  9.7 0.0 copy-start.18
  9.7 0.7 copy-done.18
  10.4 1.4 copy-done.21
  11.8 3.3 %shard_map.68 = (bf16[16,144,384]{2,1,0:T(8,128)(2,1)S(1)}, s32[16,8,128]{2,1,0:T(8,128)}) custom-call(s32[8,128]{1,0:T(8,128)S(1)} %bitcast.6, s32[1,1024]{1,0:T(1,128)S(1)} %reshape.13.routes_flat, bf16[1,1024]{1,0:T(2,128)(2,1)S(1)} %reshape.14.weights_flat, bf16[1024,768]{1,0:T(8,128)(2,1)S(1)} %bitcast.9, ...), custom_call_target="tpu_custom_call" | custom-call | flops 1811939328 | bytes 4718592 | tf_op jit(solution)/shard_map/pallas_call | solution.py:82
  15.1 1.2 copy-done.4
  16.3 3.5 %all-to-all-start = ((s32[16,8,128]{2,1,0:T(8,128)}), s32[16,8,128]{2,1,0:T(8,128)S(1)}, u32[]{:S(2)}, u32[]{:S(2)}) async-start(s32[16,8,128]{2,1,0:T(8,128)} %get-tuple-element.4), calls=%async_computation | async-start | bytes 131072 | tf_op jit(solution)/shard_map/all_to_all | solution.py:509
  19.8 9.3 %collective-permute-done.3.refs_3_ = bf16[128,2048]{1,0:T(8,128)(2,1)S(1)} collective-permute-done((bf16[128,2048]{1,0:T(8,128)(2,1)}, bf16[128,2048]{1,0:T(8,128)(2,1)S(1)}, u32[]{:S(2)}, u32[]{:S(2)}) %collective-permute-start.3) | collective-permute-done | bytes 524320 | tf_op jit(solution)/shard_map/ppermute | solution.py:494
  29.1 0.0 collective-permute-done.2.refs_2_
  29.1 2.1 %collective-permute-done.1.refs_1_ = bf16[128,2048]{1,0:T(8,128)(2,1)S(1)} collective-permute-done((bf16[128,2048]{1,0:T(8,128)(2,1)}, bf16[128,2048]{1,0:T(8,128)(2,1)S(1)}, u32[]{:S(2)}, u32[]{:S(2)}) %collective-permute-start.1) | collective-permute-done | bytes 524320 | tf_op jit(solution)/shard_map/ppermute | solution.py:494
  31.2 0.0 copy-done.5
  31.2 0.8 copy-done.9
  32.0 0.0 all-to-all-done.routes_t
  32.0 4.3 %all-to-all-start.1 = ((bf16[16,144,384]{2,1,0:T(8,128)(2,1)}), bf16[16,144,384]{2,1,0:T(8,128)(2,1)S(1)}, u32[]{:S(2)}, u32[]{:S(2)}) async-start(bf16[16,144,384]{2,1,0:T(8,128)(2,1)} %shard_map.69), calls=%async_computation.1 | async-start | bytes 3538944 | tf_op jit(solution)/shard_map/all_to_all | solution.py:509
  36.3 0.5 collective-permute-start.6
  36.7 0.1 collective-permute-start.5
  36.8 0.4 collective-permute-start.4
  37.2 1.7 %collective-permute-start.9 = (bf16[128,2048]{1,0:T(8,128)(2,1)S(1)}, bf16[128,2048]{1,0:T(8,128)(2,1)}, u32[]{:S(2)}, u32[]{:S(2)}) collective-permute-start(bf16[128,2048]{1,0:T(8,128)(2,1)S(1)} %copy-done.6), channel_id=1, source_target_pairs={{0,4},{4,0},{8,12},{12,8},{1,5},{5,1},{9,13},{13,9},{2,6},{6,2},{1... | collective-permute-start | bytes 1572872 | tf_op jit(solution)/shard_map/ppermute | solution.py:494
  38.9 0.1 pad_add_fusion.place
  39.0 1.5 %collective-permute-start.8 = (bf16[128,2048]{1,0:T(8,128)(2,1)S(1)}, bf16[128,2048]{1,0:T(8,128)(2,1)}, u32[]{:S(2)}, u32[]{:S(2)}) collective-permute-start(bf16[128,2048]{1,0:T(8,128)(2,1)S(1)} %copy-done.6), channel_id=1, source_target_pairs={{0,2},{1,3},{2,0},{3,1},{4,6},{5,7},{6,4},{7,5},{8,10},{9,11},{10,... | collective-permute-start | bytes 1572872 | tf_op jit(solution)/shard_map/ppermute | solution.py:494
  40.5 0.0 collective-permute-done.6.refs_7_
  40.5 0.6 collective-permute-start.7
  41.0 0.0 collective-permute-done.5.refs_6_
  41.0 0.0 collective-permute-done.4.refs_5_
  41.0 1.0 copy-done.13
  42.1 1.0 copy-done.16
  43.1 14.0 %shard_map.71.refs_1_.backs = f32[16,144,192]{2,1,0:T(8,128)S(1)} custom-call(s32[2]{0:T(128)S(1)} %pad_add_fusion.place, s32[16,8,128]{2,1,0:T(8,128)S(1)} %all-to-all-done.routes_t, bf16[16,192,2048]{2,1,0:T(8,128)(2,1)} %weights.3, bf16[128,2048]{1,0:T(8,128)(2,1)S(1)} %copy-done.13, bf16[128,2048]{1,0:T(8,128)(2,1)S(1)} %copy-done.10, ...), custom_call_target="tpu_custom_call" | custom-call | flops 4227858432 | bytes 12582912 | tf_op jit(solution)/shard_map/pallas_call | solution.py:364
  57.2 0.0 copy-start.2
  57.2 1.4 copy-done.2
  58.6 20.7 %collective-permute-done.9.refs_10_.refs_2_ = bf16[128,2048]{1,0:T(8,128)(2,1)} collective-permute-done((bf16[128,2048]{1,0:T(8,128)(2,1)S(1)}, bf16[128,2048]{1,0:T(8,128)(2,1)}, u32[]{:S(2)}, u32[]{:S(2)}) %collective-permute-start.9) | collective-permute-done | bytes 524320 | tf_op jit(solution)/shard_map/ppermute | solution.py:494
  79.2 1.9 %copy.15.refs_0_ = bf16[128,2048]{1,0:T(8,128)(2,1)} copy(bf16[128,2048]{1,0:T(8,128)(2,1)} %collective-permute-done.9.refs_10_.refs_2_) | data formatting | bytes 1048576
  81.1 1.5 %collective-permute-start.10 = (bf16[128,2048]{1,0:T(8,128)(2,1)}, bf16[128,2048]{1,0:T(8,128)(2,1)}, u32[]{:S(2)}, u32[]{:S(2)}) collective-permute-start(bf16[128,2048]{1,0:T(8,128)(2,1)} %shard_map.72), channel_id=1, source_target_pairs={{0,2},{1,3},{2,0},{3,1},{4,6},{5,7},{6,4},{7,5},{8,10},{9,11},{10,... | collective-permute-start | bytes 1572872 | tf_op jit(solution)/shard_map/ppermute | solution.py:494
  82.6 0.0 collective-permute-start.13
  82.6 0.0 collective-permute-done.8.refs_9_.refs_1_
  82.6 0.5 collective-permute-start.12
  83.1 0.0 collective-permute-done.7.refs_8_.refs_0_
  83.1 0.1 collective-permute-start.11
  83.2 0.0 all-to-all-done.1.received
  83.2 2.0 %shard_map.70.refs_1_.hidden = bf16[16,288,192]{2,1,0:T(8,128)(2,1)S(1)} custom-call(s32[2]{0:T(128)S(1)} %pad_add_fusion.place, bf16[16,144,384]{2,1,0:T(8,128)(2,1)S(1)} %all-to-all-done.1.received), custom_call_target="tpu_custom_call" | custom-call | flops 1019215872 | bytes 4194304 | tf_op jit(solution)/shard_map/pallas_call | solution.py:238
  85.2 1.4 %copy-done = bf16[16,288,192]{2,1,0:T(8,128)(2,1)} copy-done((bf16[16,288,192]{2,1,0:T(8,128)(2,1)}, bf16[16,288,192]{2,1,0:T(8,128)(2,1)S(1)}, u32[]{:S(2)}) %copy-start) | copy-done | bytes 1769496
  86.6 8.3 %collective-permute-done.10.refs_0_ = bf16[128,2048]{1,0:T(8,128)(2,1)} collective-permute-done((bf16[128,2048]{1,0:T(8,128)(2,1)}, bf16[128,2048]{1,0:T(8,128)(2,1)}, u32[]{:S(2)}, u32[]{:S(2)}) %collective-permute-start.10) | collective-permute-done | bytes 524320 | tf_op jit(solution)/shard_map/ppermute | solution.py:494
  94.9 0.0 collective-permute-start.14
  94.9 0.0 collective-permute-done.13.refs_14_.refs_6_
  94.9 0.0 collective-permute-done.12.refs_13_.refs_5_
  94.9 0.0 collective-permute-done.11.refs_12_.refs_4_
  95.0 2.1 %collective-permute-done.14.refs_15_.refs_7_ = bf16[128,2048]{1,0:T(8,128)(2,1)S(1)} collective-permute-done((bf16[128,2048]{1,0:T(8,128)(2,1)}, bf16[128,2048]{1,0:T(8,128)(2,1)S(1)}, u32[]{:S(2)}, u32[]{:S(2)}) %collective-permute-start.14) | collective-permute-done | bytes 524320 | tf_op jit(solution)/shard_map/ppermute | solution.py:494
  97.0 1.7 %copy-done.3 = f32[16,144,192]{2,1,0:T(8,128)S(1)} copy-done((f32[16,144,192]{2,1,0:T(8,128)S(1)}, f32[16,144,192]{2,1,0:T(8,128)}, u32[]{:S(2)}) %copy-start.3) | copy-done | bytes 1769496
  98.7 14.5 %shard_map.75 = f32[16,18,128]{2,1,0:T(8,128)S(1)} custom-call(s32[2]{0:T(128)S(1)} %pad_add_fusion.place, s32[16,8,128]{2,1,0:T(8,128)S(1)} %all-to-all-done.routes_t, bf16[16,192,2048]{2,1,0:T(8,128)(2,1)} %weights.3, bf16[16,288,192]{2,1,0:T(8,128)(2,1)S(1)} %copy-done.1, f32[16,144,192]{2,1,0:T(8,128)S(1)} %copy-done.3, ...), custom_call_target="tpu_custom_call" | custom-call | flops 4227858432 | bytes 12582912 | tf_op jit(solution)/shard_map/pallas_call | solution.py:373
  113.2 0.7 copy-done.12
  113.9 0.8 copy-done.17
  114.7 5.0 %all-to-all-start.2 = ((f32[16,18,128]{2,1,0:T(8,128)}), f32[16,18,128]{2,1,0:T(8,128)S(1)}, u32[]{:S(2)}, u32[]{:S(2)}) async-start(f32[16,18,128]{2,1,0:T(8,128)} %copy-done.12), calls=%async_computation.2 | async-start | bytes 393216 | tf_op jit(solution)/shard_map/all_to_all | solution.py:509
  119.7 0.0 copy-start.14
  119.7 1.0 copy-done.14
  120.7 19.9 %shard_map.74 = bf16[16,192,2048]{2,1,0:T(8,128)(2,1)} custom-call(s32[2]{0:T(128)S(1)} %pad_add_fusion.place, s32[16,8,128]{2,1,0:T(8,128)S(1)} %all-to-all-done.routes_t, bf16[16,288,192]{2,1,0:T(8,128)(2,1)} %copy-done, bf16[128,2048]{1,0:T(8,128)(2,1)S(1)} %copy-done.14, bf16[128,2048]{1,0:T(8,128)(2,1)S(1)} %copy-done.11, ...), custom_call_target="tpu_custom_call" | custom-call | flops 8455716864 | bytes 12582912 | tf_op jit(solution)/shard_map/pallas_call | solution.py:411
  140.6 0.0 all-to-all-done.2.returned
  140.6 1.0 shard_map.76
  (31 shorter events, 0.1 us)
Async XLA Ops:
  0.6 9.0 %collective-permute-start = (bf16[128,2048]{1,0:T(8,128)(2,1)}, bf16[128,2048]{1,0:T(8,128)(2,1)S(1)}, u32[]{:S(2)}, u32[]{:S(2)}) collective-permute-start(bf16[128,2048]{1,0:T(8,128)(2,1)} %refs_0_.3), channel_id=1, source_target_pairs={{0,1},{1,0},{2,3},{3,2},{4,5},{5,4},{6,7},{7,6},{8,9},{9,8},{10,11... | collective-permute-start | bytes 1572872 | tf_op jit(solution)/shard_map/ppermute | solution.py:494
  1.1 27.9 %collective-permute-start.3 = (bf16[128,2048]{1,0:T(8,128)(2,1)}, bf16[128,2048]{1,0:T(8,128)(2,1)S(1)}, u32[]{:S(2)}, u32[]{:S(2)}) collective-permute-start(bf16[128,2048]{1,0:T(8,128)(2,1)} %refs_0_.3), channel_id=1, source_target_pairs={{0,8},{4,12},{8,0},{12,4},{1,9},{5,13},{9,1},{13,5},{2,10},{6,14},... | collective-permute-start | bytes 1572872 | tf_op jit(solution)/shard_map/ppermute | solution.py:494
  4.8 24.3 %collective-permute-start.2 = (bf16[128,2048]{1,0:T(8,128)(2,1)}, bf16[128,2048]{1,0:T(8,128)(2,1)S(1)}, u32[]{:S(2)}, u32[]{:S(2)}) collective-permute-start(bf16[128,2048]{1,0:T(8,128)(2,1)} %refs_0_.3), channel_id=1, source_target_pairs={{0,2},{1,3},{2,0},{3,1},{4,6},{5,7},{6,4},{7,5},{8,10},{9,11},{10,... | collective-permute-start | bytes 1572872 | tf_op jit(solution)/shard_map/ppermute | solution.py:494
  6.3 24.9 %collective-permute-start.1 = (bf16[128,2048]{1,0:T(8,128)(2,1)}, bf16[128,2048]{1,0:T(8,128)(2,1)S(1)}, u32[]{:S(2)}, u32[]{:S(2)}) collective-permute-start(bf16[128,2048]{1,0:T(8,128)(2,1)} %refs_0_.3), channel_id=1, source_target_pairs={{0,4},{4,0},{8,12},{12,8},{1,5},{5,1},{9,13},{13,9},{2,6},{6,2},{1... | collective-permute-start | bytes 1572872 | tf_op jit(solution)/shard_map/ppermute | solution.py:494
  9.7 5.4 %copy-start.15 = (bf16[128,2048]{1,0:T(8,128)(2,1)}, bf16[128,2048]{1,0:T(8,128)(2,1)S(1)}, u32[]{:S(2)}) copy-start(bf16[128,2048]{1,0:T(8,128)(2,1)S(1)} %collective-permute-done.early.refs_4_) | copy-start | bytes 1572868
  9.7 0.7 copy-start.18
  10.4 1.4 copy-start.21
  15.1 1.2 copy-start.4
  16.3 15.6 %all-to-all-start = ((s32[16,8,128]{2,1,0:T(8,128)}), s32[16,8,128]{2,1,0:T(8,128)S(1)}, u32[]{:S(2)}, u32[]{:S(2)}) async-start(s32[16,8,128]{2,1,0:T(8,128)} %get-tuple-element.4), calls=%async_computation | async-start | bytes 131072 | tf_op jit(solution)/shard_map/all_to_all | solution.py:509
  29.1 2.1 %copy-start.5 = (bf16[128,2048]{1,0:T(8,128)(2,1)}, bf16[128,2048]{1,0:T(8,128)(2,1)S(1)}, u32[]{:S(2)}) copy-start(bf16[128,2048]{1,0:T(8,128)(2,1)S(1)} %collective-permute-done.3.refs_3_) | copy-start | bytes 1572868
  29.1 2.1 %copy-start.7 = (bf16[128,2048]{1,0:T(8,128)(2,1)}, bf16[128,2048]{1,0:T(8,128)(2,1)S(1)}, u32[]{:S(2)}) copy-start(bf16[128,2048]{1,0:T(8,128)(2,1)S(1)} %collective-permute-done.2.refs_2_) | copy-start | bytes 1572868
  31.2 0.8 copy-start.9
  32.0 4.3 %copy-start.6 = (bf16[128,2048]{1,0:T(8,128)(2,1)S(1)}, bf16[128,2048]{1,0:T(8,128)(2,1)}, u32[]{:S(2)}) copy-start(bf16[128,2048]{1,0:T(8,128)(2,1)} %copy-done.5) | copy-start | bytes 1572868
  32.0 4.8 %copy-start.8 = (bf16[128,2048]{1,0:T(8,128)(2,1)S(1)}, bf16[128,2048]{1,0:T(8,128)(2,1)}, u32[]{:S(2)}) copy-start(bf16[128,2048]{1,0:T(8,128)(2,1)} %copy-done.7) | copy-start | bytes 1572868
  32.0 4.9 %copy-start.10 = (bf16[128,2048]{1,0:T(8,128)(2,1)S(1)}, bf16[128,2048]{1,0:T(8,128)(2,1)}, u32[]{:S(2)}) copy-start(bf16[128,2048]{1,0:T(8,128)(2,1)} %copy-done.9) | copy-start | bytes 1572868
  32.0 51.2 %all-to-all-start.1 = ((bf16[16,144,384]{2,1,0:T(8,128)(2,1)}), bf16[16,144,384]{2,1,0:T(8,128)(2,1)S(1)}, u32[]{:S(2)}, u32[]{:S(2)}) async-start(bf16[16,144,384]{2,1,0:T(8,128)(2,1)} %shard_map.69), calls=%async_computation.1 | async-start | bytes 3538944 | tf_op jit(solution)/shard_map/all_to_all | solution.py:509
  36.3 4.2 %collective-permute-start.6 = (bf16[128,2048]{1,0:T(8,128)(2,1)S(1)}, bf16[128,2048]{1,0:T(8,128)(2,1)}, u32[]{:S(2)}, u32[]{:S(2)}) collective-permute-start(bf16[128,2048]{1,0:T(8,128)(2,1)S(1)} %copy-done.6), channel_id=1, source_target_pairs={{0,1},{1,0},{2,3},{3,2},{4,5},{5,4},{6,7},{7,6},{8,9},{9,8},{10,11... | collective-permute-start | bytes 1572872 | tf_op jit(solution)/shard_map/ppermute | solution.py:494
  36.7 4.3 %collective-permute-start.5 = (bf16[128,2048]{1,0:T(8,128)(2,1)S(1)}, bf16[128,2048]{1,0:T(8,128)(2,1)}, u32[]{:S(2)}, u32[]{:S(2)}) collective-permute-start(bf16[128,2048]{1,0:T(8,128)(2,1)S(1)} %copy-done.8), channel_id=1, source_target_pairs={{0,1},{1,0},{2,3},{3,2},{4,5},{5,4},{6,7},{7,6},{8,9},{9,8},{10,11... | collective-permute-start | bytes 1572872 | tf_op jit(solution)/shard_map/ppermute | solution.py:494
  36.8 4.2 %collective-permute-start.4 = (bf16[128,2048]{1,0:T(8,128)(2,1)S(1)}, bf16[128,2048]{1,0:T(8,128)(2,1)}, u32[]{:S(2)}, u32[]{:S(2)}) collective-permute-start(bf16[128,2048]{1,0:T(8,128)(2,1)S(1)} %copy-done.10), channel_id=1, source_target_pairs={{0,1},{1,0},{2,3},{3,2},{4,5},{5,4},{6,7},{7,6},{8,9},{9,8},{10,11... | collective-permute-start | bytes 1572872 | tf_op jit(solution)/shard_map/ppermute | solution.py:494
  37.2 42.0 %collective-permute-start.9 = (bf16[128,2048]{1,0:T(8,128)(2,1)S(1)}, bf16[128,2048]{1,0:T(8,128)(2,1)}, u32[]{:S(2)}, u32[]{:S(2)}) collective-permute-start(bf16[128,2048]{1,0:T(8,128)(2,1)S(1)} %copy-done.6), channel_id=1, source_target_pairs={{0,4},{4,0},{8,12},{12,8},{1,5},{5,1},{9,13},{13,9},{2,6},{6,2},{1... | collective-permute-start | bytes 1572872 | tf_op jit(solution)/shard_map/ppermute | solution.py:494
  39.0 43.6 %collective-permute-start.8 = (bf16[128,2048]{1,0:T(8,128)(2,1)S(1)}, bf16[128,2048]{1,0:T(8,128)(2,1)}, u32[]{:S(2)}, u32[]{:S(2)}) collective-permute-start(bf16[128,2048]{1,0:T(8,128)(2,1)S(1)} %copy-done.6), channel_id=1, source_target_pairs={{0,2},{1,3},{2,0},{3,1},{4,6},{5,7},{6,4},{7,5},{8,10},{9,11},{10,... | collective-permute-start | bytes 1572872 | tf_op jit(solution)/shard_map/ppermute | solution.py:494
  40.5 42.6 %collective-permute-start.7 = (bf16[128,2048]{1,0:T(8,128)(2,1)S(1)}, bf16[128,2048]{1,0:T(8,128)(2,1)}, u32[]{:S(2)}, u32[]{:S(2)}) collective-permute-start(bf16[128,2048]{1,0:T(8,128)(2,1)S(1)} %copy-done.10), channel_id=1, source_target_pairs={{0,2},{1,3},{2,0},{3,1},{4,6},{5,7},{6,4},{7,5},{8,10},{9,11},{10,... | collective-permute-start | bytes 1572872 | tf_op jit(solution)/shard_map/ppermute | solution.py:494
  41.0 1.0 copy-start.13
  42.1 1.0 copy-start.16
  57.2 1.4 copy-start.2
  81.1 13.8 %collective-permute-start.10 = (bf16[128,2048]{1,0:T(8,128)(2,1)}, bf16[128,2048]{1,0:T(8,128)(2,1)}, u32[]{:S(2)}, u32[]{:S(2)}) collective-permute-start(bf16[128,2048]{1,0:T(8,128)(2,1)} %shard_map.72), channel_id=1, source_target_pairs={{0,2},{1,3},{2,0},{3,1},{4,6},{5,7},{6,4},{7,5},{8,10},{9,11},{10,... | collective-permute-start | bytes 1572872 | tf_op jit(solution)/shard_map/ppermute | solution.py:494
  82.6 12.3 %collective-permute-start.13 = (bf16[128,2048]{1,0:T(8,128)(2,1)}, bf16[128,2048]{1,0:T(8,128)(2,1)}, u32[]{:S(2)}, u32[]{:S(2)}) collective-permute-start(bf16[128,2048]{1,0:T(8,128)(2,1)} %collective-permute-done.9.refs_10_.refs_2_), channel_id=1, source_target_pairs={{0,1},{1,0},{2,3},{3,2},{4,5},{5,4},{6,7},{7,6},{8,9},{9,8},{10,11... | collective-permute-start | bytes 1572872 | tf_op jit(solution)/shard_map/ppermute | solution.py:494
  82.6 12.3 %collective-permute-start.12 = (bf16[128,2048]{1,0:T(8,128)(2,1)}, bf16[128,2048]{1,0:T(8,128)(2,1)}, u32[]{:S(2)}, u32[]{:S(2)}) collective-permute-start(bf16[128,2048]{1,0:T(8,128)(2,1)} %collective-permute-done.8.refs_9_.refs_1_), channel_id=1, source_target_pairs={{0,1},{1,0},{2,3},{3,2},{4,5},{5,4},{6,7},{7,6},{8,9},{9,8},{10,11... | collective-permute-start | bytes 1572872 | tf_op jit(solution)/shard_map/ppermute | solution.py:494
  83.1 11.8 %collective-permute-start.11 = (bf16[128,2048]{1,0:T(8,128)(2,1)}, bf16[128,2048]{1,0:T(8,128)(2,1)}, u32[]{:S(2)}, u32[]{:S(2)}) collective-permute-start(bf16[128,2048]{1,0:T(8,128)(2,1)} %collective-permute-done.7.refs_8_.refs_0_), channel_id=1, source_target_pairs={{0,1},{1,0},{2,3},{3,2},{4,5},{5,4},{6,7},{7,6},{8,9},{9,8},{10,11... | collective-permute-start | bytes 1572872 | tf_op jit(solution)/shard_map/ppermute | solution.py:494
  85.2 1.4 %copy-start = (bf16[16,288,192]{2,1,0:T(8,128)(2,1)}, bf16[16,288,192]{2,1,0:T(8,128)(2,1)S(1)}, u32[]{:S(2)}) copy-start(bf16[16,288,192]{2,1,0:T(8,128)(2,1)S(1)} %shard_map.70.refs_1_.hidden) | copy-start | bytes 5308420
  94.9 2.1 %copy-start.1 = (bf16[16,288,192]{2,1,0:T(8,128)(2,1)S(1)}, bf16[16,288,192]{2,1,0:T(8,128)(2,1)}, u32[]{:S(2)}) copy-start(bf16[16,288,192]{2,1,0:T(8,128)(2,1)} %copy-done) | copy-start | bytes 5308420
  94.9 24.7 %copy-start.11 = (bf16[128,2048]{1,0:T(8,128)(2,1)S(1)}, bf16[128,2048]{1,0:T(8,128)(2,1)}, u32[]{:S(2)}) copy-start(bf16[128,2048]{1,0:T(8,128)(2,1)} %copy-done.9) | copy-start | bytes 1572868
  94.9 2.1 %collective-permute-start.14 = (bf16[128,2048]{1,0:T(8,128)(2,1)}, bf16[128,2048]{1,0:T(8,128)(2,1)S(1)}, u32[]{:S(2)}, u32[]{:S(2)}) collective-permute-start(bf16[128,2048]{1,0:T(8,128)(2,1)} %shard_map.73.refs_11_.refs_3_), channel_id=1, source_target_pairs={{0,1},{1,0},{2,3},{3,2},{4,5},{5,4},{6,7},{7,6},{8,9},{9,8},{10,11... | collective-permute-start | bytes 1572872 | tf_op jit(solution)/shard_map/ppermute | solution.py:494
  97.0 1.7 %copy-start.3 = (f32[16,144,192]{2,1,0:T(8,128)S(1)}, f32[16,144,192]{2,1,0:T(8,128)}, u32[]{:S(2)}) copy-start(f32[16,144,192]{2,1,0:T(8,128)} %copy-done.2) | copy-start | bytes 5308420
  113.2 0.7 copy-start.12
  113.9 0.8 copy-start.17
  114.7 25.9 %all-to-all-start.2 = ((f32[16,18,128]{2,1,0:T(8,128)}), f32[16,18,128]{2,1,0:T(8,128)S(1)}, u32[]{:S(2)}, u32[]{:S(2)}) async-start(f32[16,18,128]{2,1,0:T(8,128)} %copy-done.12), calls=%async_computation.2 | async-start | bytes 393216 | tf_op jit(solution)/shard_map/all_to_all | solution.py:509
  119.7 1.0 copy-start.14
  120.7 19.9 %copy-start.19 = (s32[128,8]{0,1:T(8,128)S(1)}, s32[128,8]{0,1:T(8,128)}, u32[]{:S(2)}) copy-start(s32[128,8]{0,1:T(8,128)} %param.5) | copy-start | bytes 12292
  120.7 19.9 %copy-start.20 = (bf16[128,8]{0,1:T(8,128)(2,1)S(1)}, bf16[128,8]{0,1:T(8,128)(2,1)}, u32[]{:S(2)}) copy-start(bf16[128,8]{0,1:T(8,128)(2,1)} %param.6) | copy-start | bytes 6148

commit v5 on v3

--- a/solution.py
+++ b/solution.py
@@ -17,6 +17,7 @@
 
 SMEM = pl.BlockSpec(memory_space=pltpu.SMEM)
 VMEM = pl.BlockSpec(memory_space=pltpu.VMEM)
+ANYWHERE = pl.BlockSpec(memory_space=pl.ANY)
 
 
 def dot(a, b, dims=((1,), (0,))):
@@ -294,112 +295,122 @@
     )(place, hidden, grads, weights)
 
 
-def gather_back_kernel(orders, place, routes_t, hidden, weights, *refs):
-    piece = len(orders) - 1
-    blocks, refs = refs[:SUPER], refs[SUPER:]
-    earlier, (out, sums, held, rows, sems) = refs[:piece], refs[piece:]
+def early_kernel(order, place, routes_t, weights, *refs):
+    blocks, (out, held, rows, sems) = refs[:SUPER], refs[SUPER:]
     step = pl.program_id(0)
 
     @pl.when(step == 0)
     def _():
+        gather_rows(order, place, routes_t, fetch(blocks, held, sems), rows)
+
+    for j in range(GROUPED):
+        out[j] = dot(rows[step * GROUPED + j], weights[j], ((1,), (1,)))
+
+
+def early_products(place, order, routes_t, weights, blocks):
+    ex_local, part, width = weights.shape
+    tok = blocks[0].shape[0]
+    tall = SUPER * MOST
+    grouped = lambda rows, columns: pl.BlockSpec((GROUPED, rows, columns), lambda e: (e, 0, 0))
+    return pl.pallas_call(
+        functools.partial(early_kernel, order),
+        grid=(ex_local // GROUPED,),
+        in_specs=[SMEM, VMEM, grouped(part, width)] + [ANYWHERE] * SUPER,
+        out_specs=grouped(tall, part),
+        out_shape=jax.ShapeDtypeStruct((ex_local, tall, part), f32),
+        scratch_shapes=[
+            pltpu.VMEM((SUPER, tok, width), bf16),
+            pltpu.VMEM((ex_local, tall, width), bf16),
+            pltpu.SemaphoreType.DMA((SUPER,)),
+        ],
+        compiler_params=params(40),
+        cost_estimate=cost(
+            2 * ex_local * tall * width * (part + 2 * tok), 2 * ex_local * part * width
+        ),
+    )(place, routes_t, weights, *blocks)
+
+
+GROUPED = 2
+
+
+def gradients_kernel(orders, place, routes_t, weights, hidden, backs, *refs):
+    count = SUPER * len(orders)
+    blocks, (out, summed, sums, held, rows, sems) = refs[:count], refs[count:]
+    step = pl.program_id(0)
+    tall = SUPER * MOST
+    width = out.shape[2]
+    columns = min(512, width)
+
+    @pl.when(step == 0)
+    def _():
         sums[...] = jnp.zeros_like(sums)
-        gather_rows(orders[-1], place, routes_t, fetch(blocks, held, sems), rows)
-
+        block = fetch(blocks, held, sems)
+        for piece, order in enumerate(orders):
+            mine = lambda b, piece=piece: block(piece * SUPER + b)
+            gather_rows(order, place, routes_t, mine, rows, piece * tall)
+
+    lane = iota((tall, 128), 1) - place[1]
     for j in range(GROUPED):
         expert = step * GROUPED + j
-        back_rows(place, expert, hidden[j], rows[expert], weights[j], sums)
+        found = hidden[j, :tall, :].astype(f32) * backs[j]
+        total = jnp.sum(found, axis=1, keepdims=True)
+        sums[:tall, :] += jnp.where(lane == expert, total, 0.0)
+        late = hidden[j, tall:, :]
+        found = jnp.zeros((tall, 128), f32)
+        for c in range(0, width, columns):
+            here = slice(c, c + columns)
+            product = dot(hidden[j], rows[expert, :, here], ((0,), (0,)))
+            out[j, :, here] = product.astype(bf16)
+            part = dot(late, weights[j, :, here]) * rows[expert, tall:, here].astype(f32)
+            for piece in range(0, columns, 128):
+                found += part[:, piece : piece + 128]
+        total = jnp.sum(found, axis=1, keepdims=True)
+        sums[tall:, :] += jnp.where(lane == expert, total, 0.0)
 
     @pl.when(step == pl.num_programs(0) - 1)
     def _():
-        for b in range(SUPER):
-            mine = sums[b * MOST : (b + 1) * MOST, :]
-            if earlier:
-                out[block_at(place, orders[0], b)] = earlier[0][b]
-                out[block_at(place, orders[1], b)] = mine
-            else:
-                out[b] = mine
-
-
-def gather_back(place, orders, routes_t, hidden, weights, blocks, earlier):
+        for i, order in enumerate(orders):
+            for b in range(SUPER):
+                start = (i * SUPER + b) * MOST
+                summed[block_at(place, order, b)] = sums[start : start + MOST, :]
+
+
+def gradients(place, orders, routes_t, weights, hidden, backs, blocks):
     ex_local, part, width = weights.shape
+    rows = hidden.shape[1]
     tok = blocks[0].shape[0]
-    piece = len(orders) - 1
-    tall = SUPER * MOST
-    return pl.pallas_call(
-        functools.partial(gather_back_kernel, orders),
+    count = len(blocks)
+    grouped = lambda rows, columns: pl.BlockSpec((GROUPED, rows, columns), lambda e: (e, 0, 0))
+    return pl.pallas_call(
+        functools.partial(gradients_kernel, orders),
         grid=(ex_local // GROUPED,),
         in_specs=[
             SMEM,
             VMEM,
-            pl.BlockSpec((GROUPED, tall, part), lambda e: (e, piece, 0)),
-            pl.BlockSpec((GROUPED, part, width), lambda e: (e, 0, 0)),
+            grouped(part, width),
+            grouped(rows, part),
+            grouped(SUPER * MOST, part),
         ]
-        + [pl.BlockSpec(memory_space=pl.ANY)] * SUPER
-        + [VMEM] * len(earlier),
-        out_specs=pl.BlockSpec((SUPER * (piece + 1), MOST, 128), lambda e: (0, 0, 0)),
-        out_shape=jax.ShapeDtypeStruct((SUPER * (piece + 1), MOST, 128), f32),
+        + [ANYWHERE] * count,
+        out_specs=[
+            grouped(part, width),
+            pl.BlockSpec((count, MOST, 128), lambda e: (0, 0, 0)),
+        ],
+        out_shape=[
+            jax.ShapeDtypeStruct((ex_local, part, width), bf16),
+            jax.ShapeDtypeStruct((count, MOST, 128), f32),
+        ],
         scratch_shapes=[
-            pltpu.VMEM((tall, 128), f32),
-            pltpu.VMEM((SUPER, tok, width), bf16),
-            pltpu.VMEM((ex_local, tall, width), bf16),
-            pltpu.SemaphoreType.DMA((SUPER,)),
-        ],
-        compiler_params=params(40),
+            pltpu.VMEM((rows, 128), f32),
+            pltpu.VMEM((count, tok, width), bf16),
+            pltpu.VMEM((ex_local, rows, width), bf16),
+            pltpu.SemaphoreType.DMA((count,)),
+        ],
+        compiler_params=params(56),
         cost_estimate=cost(
-            2 * ex_local * tall * width * (part + 2 * tok), 2 * ex_local * part * width
+            2 * ex_local * rows * width * (2 * part + 2 * tok), 4 * ex_local * part * width
         ),
-    )(place, routes_t, hidden, weights, *blocks, *earlier)
-
-
-GROUPED = 2
-
-
-def gather_outer_kernel(orders, place, routes_t, hidden, *refs):
-    count = SUPER * len(orders)
-    blocks, (out, held, rows, sems) = refs[:count], refs[count:]
-    step = pl.program_id(0)
-    width = out.shape[2]
-    columns = min(512, width)
-
-    @pl.when(step == 0)
-    def _():
-        block = fetch(blocks, held, sems)
-        for piece, order in enumerate(orders):
-            mine = lambda b, piece=piece: block(piece * SUPER + b)
-            gather_rows(order, place, routes_t, mine, rows, piece * SUPER * MOST)
-
-    for j in range(GROUPED):
-        expert = step * GROUPED + j
-        for c in range(0, width, columns):
-            here = slice(c, c + columns)
-            found = dot(hidden[j], rows[expert, :, here], ((0,), (0,)))
-            out[j, :, here] = found.astype(bf16)
-
-
-def gather_outer(place, orders, routes_t, hidden, blocks):
-    ex_local, tall, part = hidden.shape
-    tok, width = blocks[0].shape
-    return pl.pallas_call(
-        functools.partial(gather_outer_kernel, orders),
-        grid=(ex_local // GROUPED,),
-        in_specs=[SMEM, VMEM, pl.BlockSpec((GROUPED, tall, part), lambda e: (e, 0, 0))]
-        + [pl.BlockSpec(memory_space=pl.ANY)] * len(blocks),
-        out_specs=pl.BlockSpec((GROUPED, part, width), lambda e: (e, 0, 0)),
-        out_shape=jax.ShapeDtypeStruct((ex_local, part, width), bf16),
-        scratch_shapes=[
-            pltpu.VMEM((len(blocks), tok, width), bf16),
-            pltpu.VMEM((ex_local, tall, width), bf16),
-            pltpu.SemaphoreType.DMA((len(blocks),)),
-        ],
-        compiler_params=params(52),
-        cost_estimate=cost(
-            2 * ex_local * tall * width * (part + 2 * tok), 2 * ex_local * part * width
-        ),
-    )(place, routes_t, hidden, *blocks)
-
-
-def kept(array):
-    return pltpu.with_memory_space_constraint(array, pltpu.VMEM)
+    )(place, routes_t, weights, hidden, backs, *blocks)
 
 
 def outer_kernel(hidden, grads, out, total):
@@ -497,24 +508,24 @@
     )
     all_routes = trade(copies)
     if small:
-        received = trade(after(sent, near, side, far))
+        near_twin, side_twin, far_twin = [hop(x, "dp", 1) for x in (near, side, far)]
+        early = [(0, d_out), (4, near), (2, side), (8, far)]
+        early += [(1, twin), (5, near_twin), (3, side_twin), (9, far_twin)]
         near_side = hop(near, "dp", 2)
         far_side = hop(far, "dp", 2)
         both = hop(far, "expert", 1)
+        received = trade(after(sent, near, side, far))
+        orders = [[n for n, _ in early], [6, 10, 12, 14, 7, 11, 13, 15]]
+        early = [x for _, x in early]
+        backs = early_products(place, orders[0], all_routes, w_down, early)
+        both = after(both, backs)
         both_side = hop(both, "dp", 2)
-        early = [(0, d_out), (4, near), (2, side), (8, far)]
-        late = [(6, near_side), (10, far_side), (12, both), (14, both_side)]
-        early = early + [(1, twin)] + [(n + 1, hop(x, "dp", 1)) for n, x in early[1:]]
-        late = late + [(n + 1, hop(x, "dp", 1)) for n, x in late]
-        orders = [[n for n, _ in some] for some in (early, late)]
-        blocks = [[x for _, x in some] for some in (early, late)]
         arranged = arrange(place, orders, received, ex_local)
-        sums = []
-        for i, some in enumerate(blocks):
-            now = orders[: i + 1]
-            sums = [gather_back(place, now, all_routes, arranged, w_down, some, sums)]
-        sums = sums[0]
-        d_w_down = gather_outer(place, orders, all_routes, arranged, sum(blocks, []))
+        late = [near_side, far_side, both, after(both_side, arranged)]
+        late += [hop(x, "dp", 1) for x in late]
+        d_w_down, sums = gradients(
+            place, orders, all_routes, w_down, arranged, backs, early + late
+        )
     else:
         received = trade(sent)
         grads = lax.all_gather(d_out, GROUP, axis=0, tiled=True)

time: 160 us -> 139 us (0.87)
  waiting for transfers between devices: 58.3 us -> 42.3 us
  blocking collectives: 0 us -> 14 us
  Pallas kernels: 58.3 us -> 47.1 us
  starting transfers between devices: 28.8 us -> 21.8 us
    ppermute x15, waiting for transfers between devices: 58.3 us -> 42.3 us  [hop(): return lax.ppermute(block, axis, [(i, i ^ flip) for i in range(size)])]
    all_to_all x0 -> x1, blocking collectives: none -> 14 us  [body(): lax.all_to_all(x, GROUP, split_axis=0, concat_axis=0, tiled=True)]
    pallas_call x3 -> x2, Pallas kernels: 52.1 us -> 40.9 us  [the longest x1 26.9 us: gradients(): pl.pallas_call(functools.partial(gradients_kernel, orders), grid=(ex_loca...]
    all_to_all x3 -> x2, starting transfers between devices: 14.6 us -> 7.79 us  [body(): lax.all_to_all(x, GROUP, split_axis=0, concat_axis=0, tiled=True)]
    unnamed x38 -> x46, local copies, waits for them, and re-layouts: 11.9 us -> 12.3 us
  transfers between devices with their start and end apart: 18 -> 17, of which waited for: 4 -> 5; matrix products, arithmetic and copies ran while one was open for 1% -> 1% of each run, Pallas kernels for 26% -> 14%
where the time goes in v5:
time: 139 us
  Pallas kernels  47.1 us (34%)
  waiting for transfers between devices  42.3 us (30%)
  starting transfers between devices  21.8 us (16%)
  blocking collectives  14 us (10%)
  local copies, waits for them, and re-layouts  12.5 us (9%)
    ppermute x15, waiting for transfers between devices, hop(): return lax.ppermute(block, axis, [(i, i ^ flip) for i in range(size)])  42.3 us
    pallas_call x1, Pallas kernels, gradients(): pl.pallas_call(functools.partial(gradients_kernel, orders), grid=(ex_loca...  26.9 us
    pallas_call x1, Pallas kernels, early_products(): pl.pallas_call(functools.partial(early_kernel, order), grid=(ex_local //...  14 us
    all_to_all x1, blocking collectives, body(): lax.all_to_all(x, GROUP, split_axis=0, concat_axis=0, tiled=True)  14 us
    ppermute x15, starting transfers between devices, hop(): return lax.ppermute(block, axis, [(i, i ^ flip) for i in range(size)])  14 us
    unnamed x46, local copies, waits for them, and re-layouts  12.3 us
    all_to_all x2, starting transfers between devices, body(): lax.all_to_all(x, GROUP, split_axis=0, concat_axis=0, tiled=True)  7.79 us
    pallas_call x1, Pallas kernels, pack(): pl.pallas_call(functools.partial(pack_kernel, n_dp, half), grid=(n_expert...  3.27 us
  transfers between devices with their start and end apart: 17, of which 5 were waited for; matrix products, arithmetic and copies ran while one was open for 1% of the time, Pallas kernels for 14%

profile of v5, /device:TPU:0, one launch (start us, length us, event | category | flops | bytes accessed | tf_op | source)
XLA Modules:
  0.0 138.6 jit_solution(16200377202996190133)
XLA Ops:
  0.6 0.5 collective-permute-start
  1.1 3.7 %collective-permute-start.3 = (bf16[128,2048]{1,0:T(8,128)(2,1)}, bf16[128,2048]{1,0:T(8,128)(2,1)S(1)}, u32[]{:S(2)}, u32[]{:S(2)}) collective-permute-start(bf16[128,2048]{1,0:T(8,128)(2,1)} %refs_0_.3), channel_id=1, source_target_pairs={{0,8},{4,12},{8,0},{12,4},{1,9},{5,13},{9,1},{13,5},{2,10},{6,14},... | collective-permute-start | bytes 1572872 | tf_op jit(solution)/shard_map/ppermute | solution.py:476
  4.8 1.5 %collective-permute-start.2 = (bf16[128,2048]{1,0:T(8,128)(2,1)}, bf16[128,2048]{1,0:T(8,128)(2,1)S(1)}, u32[]{:S(2)}, u32[]{:S(2)}) collective-permute-start(bf16[128,2048]{1,0:T(8,128)(2,1)} %refs_0_.3), channel_id=1, source_target_pairs={{0,2},{1,3},{2,0},{3,1},{4,6},{5,7},{6,4},{7,5},{8,10},{9,11},{10,... | collective-permute-start | bytes 1572872 | tf_op jit(solution)/shard_map/ppermute | solution.py:476
  6.3 1.6 %collective-permute-start.1 = (bf16[128,2048]{1,0:T(8,128)(2,1)}, bf16[128,2048]{1,0:T(8,128)(2,1)S(1)}, u32[]{:S(2)}, u32[]{:S(2)}) collective-permute-start(bf16[128,2048]{1,0:T(8,128)(2,1)} %refs_0_.3), channel_id=1, source_target_pairs={{0,4},{4,0},{8,12},{12,8},{1,5},{5,1},{9,13},{13,9},{2,6},{6,2},{1... | collective-permute-start | bytes 1572872 | tf_op jit(solution)/shard_map/ppermute | solution.py:476
  7.9 0.8 copy.13
  8.7 0.1 reshape.14.weights_flat
  8.8 0.8 copy.12
  9.6 0.1 reshape.13.routes_flat
  9.7 0.0 collective-permute-done.early.refs_4_
  9.7 0.0 copy-start.10
  9.7 0.0 copy-start.13
  9.7 0.7 copy-done.13
  10.4 1.4 %copy-done.17 = bf16[128,8,768]{2,1,0:T(8,128)(2,1)S(1)} copy-done((bf16[128,8,768]{2,1,0:T(8,128)(2,1)S(1)}, bf16[128,8,768]{2,1,0:T(8,128)(2,1)}, u32[]{:S(2)}) %copy-start.17) | copy-done | bytes 1572888
  11.8 3.3 %shard_map.68 = (bf16[16,144,384]{2,1,0:T(8,128)(2,1)S(1)}, s32[16,8,128]{2,1,0:T(8,128)}) custom-call(s32[8,128]{1,0:T(8,128)S(1)} %bitcast.6, s32[1,1024]{1,0:T(1,128)S(1)} %reshape.13.routes_flat, bf16[1,1024]{1,0:T(2,128)(2,1)S(1)} %reshape.14.weights_flat, bf16[1024,768]{1,0:T(8,128)(2,1)S(1)} %bitcast.9, ...), custom_call_target="tpu_custom_call" | custom-call | flops 1811939328 | bytes 4718592 | tf_op jit(solution)/shard_map/pallas_call | solution.py:83
  15.1 0.0 copy-done.10
  15.1 1.2 copy-done.2
  16.3 3.5 %all-to-all-start = ((s32[16,8,128]{2,1,0:T(8,128)}), s32[16,8,128]{2,1,0:T(8,128)S(1)}, u32[]{:S(2)}, u32[]{:S(2)}) async-start(s32[16,8,128]{2,1,0:T(8,128)} %get-tuple-element.6), calls=%async_computation | async-start | bytes 131072 | tf_op jit(solution)/shard_map/all_to_all | solution.py:491
  19.8 9.3 %collective-permute-done.3.refs_3_ = bf16[128,2048]{1,0:T(8,128)(2,1)S(1)} collective-permute-done((bf16[128,2048]{1,0:T(8,128)(2,1)}, bf16[128,2048]{1,0:T(8,128)(2,1)S(1)}, u32[]{:S(2)}, u32[]{:S(2)}) %collective-permute-start.3) | collective-permute-done | bytes 524320 | tf_op jit(solution)/shard_map/ppermute | solution.py:476
  29.1 0.0 collective-permute-done.2.refs_2_
  29.1 2.1 %collective-permute-done.1.refs_1_ = bf16[128,2048]{1,0:T(8,128)(2,1)S(1)} collective-permute-done((bf16[128,2048]{1,0:T(8,128)(2,1)}, bf16[128,2048]{1,0:T(8,128)(2,1)S(1)}, u32[]{:S(2)}, u32[]{:S(2)}) %collective-permute-start.1) | collective-permute-done | bytes 524320 | tf_op jit(solution)/shard_map/ppermute | solution.py:476
  31.2 0.0 copy-done.3
  31.2 0.0 copy-done.5
  31.2 0.8 copy-done.7
  32.0 0.0 all-to-all-done.routes_t
  32.0 0.0 copy-start.12
  32.0 4.3 %all-to-all-start.1 = ((bf16[16,144,384]{2,1,0:T(8,128)(2,1)}), bf16[16,144,384]{2,1,0:T(8,128)(2,1)S(1)}, u32[]{:S(2)}, u32[]{:S(2)}) async-start(bf16[16,144,384]{2,1,0:T(8,128)(2,1)} %shard_map.69), calls=%async_computation.1 | async-start | bytes 3538944 | tf_op jit(solution)/shard_map/all_to_all | solution.py:491
  36.3 0.0 copy-done.4
  36.3 0.5 collective-permute-start.6
  36.8 0.1 collective-permute-start.5
  36.9 0.0 copy-done.8
  36.9 0.4 collective-permute-start.4
  37.3 1.7 %collective-permute-start.9 = (bf16[128,2048]{1,0:T(8,128)(2,1)S(1)}, bf16[128,2048]{1,0:T(8,128)(2,1)}, u32[]{:S(2)}, u32[]{:S(2)}) collective-permute-start(bf16[128,2048]{1,0:T(8,128)(2,1)S(1)} %copy-done.4), channel_id=1, source_target_pairs={{0,4},{4,0},{8,12},{12,8},{1,5},{5,1},{9,13},{13,9},{2,6},{6,2},{1... | collective-permute-start | bytes 1572872 | tf_op jit(solution)/shard_map/ppermute | solution.py:476
  39.0 0.1 pad_add_fusion.place
  39.0 1.5 %collective-permute-start.8 = (bf16[128,2048]{1,0:T(8,128)(2,1)S(1)}, bf16[128,2048]{1,0:T(8,128)(2,1)}, u32[]{:S(2)}, u32[]{:S(2)}) collective-permute-start(bf16[128,2048]{1,0:T(8,128)(2,1)S(1)} %copy-done.4), channel_id=1, source_target_pairs={{0,2},{1,3},{2,0},{3,1},{4,6},{5,7},{6,4},{7,5},{8,10},{9,11},{10,... | collective-permute-start | bytes 1572872 | tf_op jit(solution)/shard_map/ppermute | solution.py:476
  40.5 0.0 collective-permute-done.6.refs_7_
  40.5 0.6 collective-permute-start.7
  41.1 0.0 collective-permute-done.5.refs_6_
  41.1 0.0 collective-permute-done.4.refs_5_
  41.1 1.0 copy-done.9
  42.1 1.0 copy-done.11
  43.2 14.0 %shard_map.71.refs_1_.backs = f32[16,144,192]{2,1,0:T(8,128)S(1)} custom-call(s32[2]{0:T(128)S(1)} %pad_add_fusion.place, s32[16,8,128]{2,1,0:T(8,128)S(1)} %all-to-all-done.routes_t, bf16[16,192,2048]{2,1,0:T(8,128)(2,1)} %weights.3, bf16[128,2048]{1,0:T(8,128)(2,1)S(1)} %copy-done.9, bf16[128,2048]{1,0:T(8,128)(2,1)S(1)} %copy-done.8, ...), custom_call_target="tpu_custom_call" | custom-call | flops 4227858432 | bytes 12582912 | tf_op jit(solution)/shard_map/pallas_call | solution.py:315
  57.2 1.4 %copy-done.1 = f32[16,144,192]{2,1,0:T(8,128)} copy-done((f32[16,144,192]{2,1,0:T(8,128)}, f32[16,144,192]{2,1,0:T(8,128)S(1)}, u32[]{:S(2)}) %copy-start.1) | copy-done | bytes 1769496
  58.6 20.7 %collective-permute-done.9.refs_0_ = bf16[128,2048]{1,0:T(8,128)(2,1)} collective-permute-done((bf16[128,2048]{1,0:T(8,128)(2,1)S(1)}, bf16[128,2048]{1,0:T(8,128)(2,1)}, u32[]{:S(2)}, u32[]{:S(2)}) %collective-permute-start.9) | collective-permute-done | bytes 524320 | tf_op jit(solution)/shard_map/ppermute | solution.py:476
  79.3 1.5 %collective-permute-start.10 = (bf16[128,2048]{1,0:T(8,128)(2,1)}, bf16[128,2048]{1,0:T(8,128)(2,1)S(1)}, u32[]{:S(2)}, u32[]{:S(2)}) collective-permute-start(bf16[128,2048]{1,0:T(8,128)(2,1)} %shard_map.72.refs_10_), channel_id=1, source_target_pairs={{0,2},{1,3},{2,0},{3,1},{4,6},{5,7},{6,4},{7,5},{8,10},{9,11},{10,... | collective-permute-start | bytes 1572872 | tf_op jit(solution)/shard_map/ppermute | solution.py:476
  80.7 0.0 collective-permute-start.13
  80.8 0.0 collective-permute-done.8.refs_9_
  80.8 0.5 collective-permute-start.12
  81.3 0.0 collective-permute-done.7.refs_8_
  81.3 0.1 collective-permute-start.11
  81.3 0.0 all-to-all-done.1.received
  81.3 2.0 %shard_map.70.refs_1_.hidden = bf16[16,288,192]{2,1,0:T(8,128)(2,1)S(1)} custom-call(s32[2]{0:T(128)S(1)} %pad_add_fusion.place, bf16[16,144,384]{2,1,0:T(8,128)(2,1)S(1)} %all-to-all-done.1.received), custom_call_target="tpu_custom_call" | custom-call | flops 1019215872 | bytes 4194304 | tf_op jit(solution)/shard_map/pallas_call | solution.py:239
  83.3 1.4 %copy-done = bf16[16,288,192]{2,1,0:T(8,128)(2,1)} copy-done((bf16[16,288,192]{2,1,0:T(8,128)(2,1)}, bf16[16,288,192]{2,1,0:T(8,128)(2,1)S(1)}, u32[]{:S(2)}) %copy-start) | copy-done | bytes 1769496
  84.8 8.2 %collective-permute-done.10.refs_0_ = bf16[128,2048]{1,0:T(8,128)(2,1)S(1)} collective-permute-done((bf16[128,2048]{1,0:T(8,128)(2,1)}, bf16[128,2048]{1,0:T(8,128)(2,1)S(1)}, u32[]{:S(2)}, u32[]{:S(2)}) %collective-permute-start.10) | collective-permute-done | bytes 524320 | tf_op jit(solution)/shard_map/ppermute | solution.py:476
  93.0 0.8 copy-done.18
  93.8 0.0 collective-permute-start.14
  93.8 0.0 collective-permute-done.12.refs_13_
  93.8 0.0 collective-permute-done.11.refs_12_
  93.8 0.0 collective-permute-done.13.refs_14_
  93.8 2.1 %collective-permute-done.14.refs_15_ = bf16[128,2048]{1,0:T(8,128)(2,1)S(1)} collective-permute-done((bf16[128,2048]{1,0:T(8,128)(2,1)}, bf16[128,2048]{1,0:T(8,128)(2,1)S(1)}, u32[]{:S(2)}, u32[]{:S(2)}) %collective-permute-start.14) | collective-permute-done | bytes 524320 | tf_op jit(solution)/shard_map/ppermute | solution.py:476
  95.9 0.8 copy-done.21
  96.7 26.9 %shard_map.74 = (bf16[16,192,2048]{2,1,0:T(8,128)(2,1)}, f32[16,18,128]{2,1,0:T(8,128)}) custom-call(s32[2]{0:T(128)} %copy-done.16, s32[16,8,128]{2,1,0:T(8,128)} %copy-done.12, bf16[16,192,2048]{2,1,0:T(8,128)(2,1)} %weights.3, bf16[16,288,192]{2,1,0:T(8,128)(2,1)} %copy-done, f32[16,144,192]{2,1,0:T(8,128)} %copy-done.1, bf16[128,2048]{1,0:T(8,128)(2,1)} %refs_0_.3, ...), custom_call_target="tpu_custom_call" | custom-call | flops 12079595520 | bytes 25165824 | tf_op jit(solution)/shard_map/pallas_call | solution.py:384
  123.6 14.0 %all_to_all.15.returned = f32[16,18,128]{2,1,0:T(8,128)S(1)} all-to-all(f32[16,18,128]{2,1,0:T(8,128)} %get-tuple-element.9), channel_id=1, replica_groups=mesh['groups'=2,'expert'=4,'dp'=4] {'expert','dp'}, dimensions={0} | all-to-all | bytes 294912 | tf_op jit(solution)/shard_map/all_to_all | solution.py:491
  137.6 0.0 copy-done.15
  137.6 1.0 shard_map.75
  (28 shorter events, 0.0 us)
Async XLA Ops:
  0.6 9.0 %collective-permute-start = (bf16[128,2048]{1,0:T(8,128)(2,1)}, bf16[128,2048]{1,0:T(8,128)(2,1)S(1)}, u32[]{:S(2)}, u32[]{:S(2)}) collective-permute-start(bf16[128,2048]{1,0:T(8,128)(2,1)} %refs_0_.3), channel_id=1, source_target_pairs={{0,1},{1,0},{2,3},{3,2},{4,5},{5,4},{6,7},{7,6},{8,9},{9,8},{10,11... | collective-permute-start | bytes 1572872 | tf_op jit(solution)/shard_map/ppermute | solution.py:476
  1.1 27.9 %collective-permute-start.3 = (bf16[128,2048]{1,0:T(8,128)(2,1)}, bf16[128,2048]{1,0:T(8,128)(2,1)S(1)}, u32[]{:S(2)}, u32[]{:S(2)}) collective-permute-start(bf16[128,2048]{1,0:T(8,128)(2,1)} %refs_0_.3), channel_id=1, source_target_pairs={{0,8},{4,12},{8,0},{12,4},{1,9},{5,13},{9,1},{13,5},{2,10},{6,14},... | collective-permute-start | bytes 1572872 | tf_op jit(solution)/shard_map/ppermute | solution.py:476
  4.8 24.3 %collective-permute-start.2 = (bf16[128,2048]{1,0:T(8,128)(2,1)}, bf16[128,2048]{1,0:T(8,128)(2,1)S(1)}, u32[]{:S(2)}, u32[]{:S(2)}) collective-permute-start(bf16[128,2048]{1,0:T(8,128)(2,1)} %refs_0_.3), channel_id=1, source_target_pairs={{0,2},{1,3},{2,0},{3,1},{4,6},{5,7},{6,4},{7,5},{8,10},{9,11},{10,... | collective-permute-start | bytes 1572872 | tf_op jit(solution)/shard_map/ppermute | solution.py:476
  6.3 24.9 %collective-permute-start.1 = (bf16[128,2048]{1,0:T(8,128)(2,1)}, bf16[128,2048]{1,0:T(8,128)(2,1)S(1)}, u32[]{:S(2)}, u32[]{:S(2)}) collective-permute-start(bf16[128,2048]{1,0:T(8,128)(2,1)} %refs_0_.3), channel_id=1, source_target_pairs={{0,4},{4,0},{8,12},{12,8},{1,5},{5,1},{9,13},{13,9},{2,6},{6,2},{1... | collective-permute-start | bytes 1572872 | tf_op jit(solution)/shard_map/ppermute | solution.py:476
  9.7 5.4 %copy-start.10 = (bf16[128,2048]{1,0:T(8,128)(2,1)}, bf16[128,2048]{1,0:T(8,128)(2,1)S(1)}, u32[]{:S(2)}) copy-start(bf16[128,2048]{1,0:T(8,128)(2,1)S(1)} %collective-permute-done.early.refs_4_) | copy-start | bytes 1572868
  9.7 0.7 copy-start.13
  10.4 1.4 %copy-start.17 = (bf16[128,8,768]{2,1,0:T(8,128)(2,1)S(1)}, bf16[128,8,768]{2,1,0:T(8,128)(2,1)}, u32[]{:S(2)}) copy-start(bf16[128,8,768]{2,1,0:T(8,128)(2,1)} %param.7) | copy-start | bytes 4718596
  15.1 1.2 copy-start.2
  16.3 15.7 %all-to-all-start = ((s32[16,8,128]{2,1,0:T(8,128)}), s32[16,8,128]{2,1,0:T(8,128)S(1)}, u32[]{:S(2)}, u32[]{:S(2)}) async-start(s32[16,8,128]{2,1,0:T(8,128)} %get-tuple-element.6), calls=%async_computation | async-start | bytes 131072 | tf_op jit(solution)/shard_map/all_to_all | solution.py:491
  29.1 2.1 %copy-start.3 = (bf16[128,2048]{1,0:T(8,128)(2,1)}, bf16[128,2048]{1,0:T(8,128)(2,1)S(1)}, u32[]{:S(2)}) copy-start(bf16[128,2048]{1,0:T(8,128)(2,1)S(1)} %collective-permute-done.3.refs_3_) | copy-start | bytes 1572868
  29.1 2.1 %copy-start.5 = (bf16[128,2048]{1,0:T(8,128)(2,1)}, bf16[128,2048]{1,0:T(8,128)(2,1)S(1)}, u32[]{:S(2)}) copy-start(bf16[128,2048]{1,0:T(8,128)(2,1)S(1)} %collective-permute-done.2.refs_2_) | copy-start | bytes 1572868
  31.2 0.8 copy-start.7
  32.0 4.3 %copy-start.4 = (bf16[128,2048]{1,0:T(8,128)(2,1)S(1)}, bf16[128,2048]{1,0:T(8,128)(2,1)}, u32[]{:S(2)}) copy-start(bf16[128,2048]{1,0:T(8,128)(2,1)} %copy-done.3) | copy-start | bytes 1572868
  32.0 4.8 %copy-start.6 = (bf16[128,2048]{1,0:T(8,128)(2,1)S(1)}, bf16[128,2048]{1,0:T(8,128)(2,1)}, u32[]{:S(2)}) copy-start(bf16[128,2048]{1,0:T(8,128)(2,1)} %copy-done.5) | copy-start | bytes 1572868
  32.0 4.9 %copy-start.8 = (bf16[128,2048]{1,0:T(8,128)(2,1)S(1)}, bf16[128,2048]{1,0:T(8,128)(2,1)}, u32[]{:S(2)}) copy-start(bf16[128,2048]{1,0:T(8,128)(2,1)} %copy-done.7) | copy-start | bytes 1572868
  32.0 25.2 %copy-start.12 = (s32[16,8,128]{2,1,0:T(8,128)}, s32[16,8,128]{2,1,0:T(8,128)S(1)}, u32[]{:S(2)}) copy-start(s32[16,8,128]{2,1,0:T(8,128)S(1)} %all-to-all-done.routes_t) | copy-start | bytes 196612
  32.0 49.4 %all-to-all-start.1 = ((bf16[16,144,384]{2,1,0:T(8,128)(2,1)}), bf16[16,144,384]{2,1,0:T(8,128)(2,1)S(1)}, u32[]{:S(2)}, u32[]{:S(2)}) async-start(bf16[16,144,384]{2,1,0:T(8,128)(2,1)} %shard_map.69), calls=%async_computation.1 | async-start | bytes 3538944 | tf_op jit(solution)/shard_map/all_to_all | solution.py:491
  36.3 4.2 %collective-permute-start.6 = (bf16[128,2048]{1,0:T(8,128)(2,1)S(1)}, bf16[128,2048]{1,0:T(8,128)(2,1)}, u32[]{:S(2)}, u32[]{:S(2)}) collective-permute-start(bf16[128,2048]{1,0:T(8,128)(2,1)S(1)} %copy-done.4), channel_id=1, source_target_pairs={{0,1},{1,0},{2,3},{3,2},{4,5},{5,4},{6,7},{7,6},{8,9},{9,8},{10,11... | collective-permute-start | bytes 1572872 | tf_op jit(solution)/shard_map/ppermute | solution.py:476
  36.8 4.3 %collective-permute-start.5 = (bf16[128,2048]{1,0:T(8,128)(2,1)S(1)}, bf16[128,2048]{1,0:T(8,128)(2,1)}, u32[]{:S(2)}, u32[]{:S(2)}) collective-permute-start(bf16[128,2048]{1,0:T(8,128)(2,1)S(1)} %copy-done.6), channel_id=1, source_target_pairs={{0,1},{1,0},{2,3},{3,2},{4,5},{5,4},{6,7},{7,6},{8,9},{9,8},{10,11... | collective-permute-start | bytes 1572872 | tf_op jit(solution)/shard_map/ppermute | solution.py:476
  36.9 4.2 %collective-permute-start.4 = (bf16[128,2048]{1,0:T(8,128)(2,1)S(1)}, bf16[128,2048]{1,0:T(8,128)(2,1)}, u32[]{:S(2)}, u32[]{:S(2)}) collective-permute-start(bf16[128,2048]{1,0:T(8,128)(2,1)S(1)} %copy-done.8), channel_id=1, source_target_pairs={{0,1},{1,0},{2,3},{3,2},{4,5},{5,4},{6,7},{7,6},{8,9},{9,8},{10,11... | collective-permute-start | bytes 1572872 | tf_op jit(solution)/shard_map/ppermute | solution.py:476
  37.3 42.0 %collective-permute-start.9 = (bf16[128,2048]{1,0:T(8,128)(2,1)S(1)}, bf16[128,2048]{1,0:T(8,128)(2,1)}, u32[]{:S(2)}, u32[]{:S(2)}) collective-permute-start(bf16[128,2048]{1,0:T(8,128)(2,1)S(1)} %copy-done.4), channel_id=1, source_target_pairs={{0,4},{4,0},{8,12},{12,8},{1,5},{5,1},{9,13},{13,9},{2,6},{6,2},{1... | collective-permute-start | bytes 1572872 | tf_op jit(solution)/shard_map/ppermute | solution.py:476
  39.0 42.3 %copy-start.16 = (s32[2]{0:T(128)}, s32[2]{0:T(128)S(1)}, u32[]{:S(2)}) copy-start(s32[2]{0:T(128)S(1)} %pad_add_fusion.place) | copy-start | bytes 28
  39.0 41.7 %collective-permute-start.8 = (bf16[128,2048]{1,0:T(8,128)(2,1)S(1)}, bf16[128,2048]{1,0:T(8,128)(2,1)}, u32[]{:S(2)}, u32[]{:S(2)}) collective-permute-start(bf16[128,2048]{1,0:T(8,128)(2,1)S(1)} %copy-done.4), channel_id=1, source_target_pairs={{0,2},{1,3},{2,0},{3,1},{4,6},{5,7},{6,4},{7,5},{8,10},{9,11},{10,... | collective-permute-start | bytes 1572872 | tf_op jit(solution)/shard_map/ppermute | solution.py:476
  40.5 40.8 %collective-permute-start.7 = (bf16[128,2048]{1,0:T(8,128)(2,1)S(1)}, bf16[128,2048]{1,0:T(8,128)(2,1)}, u32[]{:S(2)}, u32[]{:S(2)}) collective-permute-start(bf16[128,2048]{1,0:T(8,128)(2,1)S(1)} %copy-done.8), channel_id=1, source_target_pairs={{0,2},{1,3},{2,0},{3,1},{4,6},{5,7},{6,4},{7,5},{8,10},{9,11},{10,... | collective-permute-start | bytes 1572872 | tf_op jit(solution)/shard_map/ppermute | solution.py:476
  41.1 1.0 copy-start.9
  42.1 1.0 copy-start.11
  57.2 1.4 %copy-start.1 = (f32[16,144,192]{2,1,0:T(8,128)}, f32[16,144,192]{2,1,0:T(8,128)S(1)}, u32[]{:S(2)}) copy-start(f32[16,144,192]{2,1,0:T(8,128)S(1)} %shard_map.71.refs_1_.backs) | copy-start | bytes 5308420
  79.3 13.7 %collective-permute-start.10 = (bf16[128,2048]{1,0:T(8,128)(2,1)}, bf16[128,2048]{1,0:T(8,128)(2,1)S(1)}, u32[]{:S(2)}, u32[]{:S(2)}) collective-permute-start(bf16[128,2048]{1,0:T(8,128)(2,1)} %shard_map.72.refs_10_), channel_id=1, source_target_pairs={{0,2},{1,3},{2,0},{3,1},{4,6},{5,7},{6,4},{7,5},{8,10},{9,11},{10,... | collective-permute-start | bytes 1572872 | tf_op jit(solution)/shard_map/ppermute | solution.py:476
  80.7 13.1 %collective-permute-start.13 = (bf16[128,2048]{1,0:T(8,128)(2,1)}, bf16[128,2048]{1,0:T(8,128)(2,1)}, u32[]{:S(2)}, u32[]{:S(2)}) collective-permute-start(bf16[128,2048]{1,0:T(8,128)(2,1)} %shard_map.72.refs_10_), channel_id=1, source_target_pairs={{0,1},{1,0},{2,3},{3,2},{4,5},{5,4},{6,7},{7,6},{8,9},{9,8},{10,11... | collective-permute-start | bytes 1572872 | tf_op jit(solution)/shard_map/ppermute | solution.py:476
  80.8 13.0 %collective-permute-start.12 = (bf16[128,2048]{1,0:T(8,128)(2,1)}, bf16[128,2048]{1,0:T(8,128)(2,1)S(1)}, u32[]{:S(2)}, u32[]{:S(2)}) collective-permute-start(bf16[128,2048]{1,0:T(8,128)(2,1)} %collective-permute-done.8.refs_9_), channel_id=1, source_target_pairs={{0,1},{1,0},{2,3},{3,2},{4,5},{5,4},{6,7},{7,6},{8,9},{9,8},{10,11... | collective-permute-start | bytes 1572872 | tf_op jit(solution)/shard_map/ppermute | solution.py:476
  81.3 12.5 %collective-permute-start.11 = (bf16[128,2048]{1,0:T(8,128)(2,1)}, bf16[128,2048]{1,0:T(8,128)(2,1)S(1)}, u32[]{:S(2)}, u32[]{:S(2)}) collective-permute-start(bf16[128,2048]{1,0:T(8,128)(2,1)} %collective-permute-done.7.refs_8_), channel_id=1, source_target_pairs={{0,1},{1,0},{2,3},{3,2},{4,5},{5,4},{6,7},{7,6},{8,9},{9,8},{10,11... | collective-permute-start | bytes 1572872 | tf_op jit(solution)/shard_map/ppermute | solution.py:476
  83.3 1.4 %copy-start = (bf16[16,288,192]{2,1,0:T(8,128)(2,1)}, bf16[16,288,192]{2,1,0:T(8,128)(2,1)S(1)}, u32[]{:S(2)}) copy-start(bf16[16,288,192]{2,1,0:T(8,128)(2,1)S(1)} %shard_map.70.refs_1_.hidden) | copy-start | bytes 5308420
  93.0 0.8 copy-start.18
  93.8 43.8 %copy-start.14 = (s32[128,8]{0,1:T(8,128)S(1)}, s32[128,8]{0,1:T(8,128)}, u32[]{:S(2)}) copy-start(s32[128,8]{0,1:T(8,128)} %param.5) | copy-start | bytes 12292
  93.8 43.8 %copy-start.15 = (bf16[128,8]{0,1:T(8,128)(2,1)S(1)}, bf16[128,8]{0,1:T(8,128)(2,1)}, u32[]{:S(2)}) copy-start(bf16[128,8]{0,1:T(8,128)(2,1)} %param.6) | copy-start | bytes 6148
  93.8 2.1 %collective-permute-start.14 = (bf16[128,2048]{1,0:T(8,128)(2,1)}, bf16[128,2048]{1,0:T(8,128)(2,1)S(1)}, u32[]{:S(2)}, u32[]{:S(2)}) collective-permute-start(bf16[128,2048]{1,0:T(8,128)(2,1)} %shard_map.73.refs_11_), channel_id=1, source_target_pairs={{0,1},{1,0},{2,3},{3,2},{4,5},{5,4},{6,7},{7,6},{8,9},{9,8},{10,11... | collective-permute-start | bytes 1572872 | tf_op jit(solution)/shard_map/ppermute | solution.py:476
  93.8 2.1 %copy-start.19 = (bf16[128,2048]{1,0:T(8,128)(2,1)}, bf16[128,2048]{1,0:T(8,128)(2,1)S(1)}, u32[]{:S(2)}) copy-start(bf16[128,2048]{1,0:T(8,128)(2,1)S(1)} %collective-permute-done.12.refs_13_) | copy-start | bytes 1572868
  93.8 2.1 %copy-start.20 = (bf16[128,2048]{1,0:T(8,128)(2,1)}, bf16[128,2048]{1,0:T(8,128)(2,1)S(1)}, u32[]{:S(2)}) copy-start(bf16[128,2048]{1,0:T(8,128)(2,1)S(1)} %collective-permute-done.11.refs_12_) | copy-start | bytes 1572868
  95.9 0.8 copy-start.21

commit v6 on v5

--- a/solution.py
+++ b/solution.py
@@ -296,7 +296,7 @@
 
 
 def early_kernel(order, place, routes_t, weights, *refs):
-    blocks, (out, held, rows, sems) = refs[:SUPER], refs[SUPER:]
+    blocks, (out, kept_rows, held, rows, sems) = refs[:SUPER], refs[SUPER:]
     step = pl.program_id(0)
 
     @pl.when(step == 0)
@@ -304,7 +304,9 @@
         gather_rows(order, place, routes_t, fetch(blocks, held, sems), rows)
 
     for j in range(GROUPED):
-        out[j] = dot(rows[step * GROUPED + j], weights[j], ((1,), (1,)))
+        mine = rows[step * GROUPED + j]
+        kept_rows[j] = mine
+        out[j] = dot(mine, weights[j], ((1,), (1,)))
 
 
 def early_products(place, order, routes_t, weights, blocks):
@@ -316,8 +318,11 @@
         functools.partial(early_kernel, order),
         grid=(ex_local // GROUPED,),
         in_specs=[SMEM, VMEM, grouped(part, width)] + [ANYWHERE] * SUPER,
-        out_specs=grouped(tall, part),
-        out_shape=jax.ShapeDtypeStruct((ex_local, tall, part), f32),
+        out_specs=[grouped(tall, part), grouped(tall, width)],
+        out_shape=[
+            jax.ShapeDtypeStruct((ex_local, tall, part), f32),
+            jax.ShapeDtypeStruct((ex_local, tall, width), bf16),
+        ],
         scratch_shapes=[
             pltpu.VMEM((SUPER, tok, width), bf16),
             pltpu.VMEM((ex_local, tall, width), bf16),
@@ -330,11 +335,11 @@
     )(place, routes_t, weights, *blocks)
 
 
-GROUPED = 2
-
-
-def gradients_kernel(orders, place, routes_t, weights, hidden, backs, *refs):
-    count = SUPER * len(orders)
+GROUPED = 4
+
+
+def gradients_kernel(orders, place, routes_t, weights, hidden, backs, early, *refs):
+    count = SUPER
     blocks, (out, summed, sums, held, rows, sems) = refs[:count], refs[count:]
     step = pl.program_id(0)
     tall = SUPER * MOST
@@ -344,10 +349,7 @@
     @pl.when(step == 0)
     def _():
         sums[...] = jnp.zeros_like(sums)
-        block = fetch(blocks, held, sems)
-        for piece, order in enumerate(orders):
-            mine = lambda b, piece=piece: block(piece * SUPER + b)
-            gather_rows(order, place, routes_t, mine, rows, piece * tall)
+        gather_rows(orders[1], place, routes_t, fetch(blocks, held, sems), rows)
 
     lane = iota((tall, 128), 1) - place[1]
     for j in range(GROUPED):
@@ -359,9 +361,11 @@
         found = jnp.zeros((tall, 128), f32)
         for c in range(0, width, columns):
             here = slice(c, c + columns)
-            product = dot(hidden[j], rows[expert, :, here], ((0,), (0,)))
+            mine = rows[expert, :, here]
+            both = jnp.concatenate([early[j, :, here], mine], axis=0)
+            product = dot(hidden[j], both, ((0,), (0,)))
             out[j, :, here] = product.astype(bf16)
-            part = dot(late, weights[j, :, here]) * rows[expert, tall:, here].astype(f32)
+            part = dot(late, weights[j, :, here]) * mine.astype(f32)
             for piece in range(0, columns, 128):
                 found += part[:, piece : piece + 128]
         total = jnp.sum(found, axis=1, keepdims=True)
@@ -375,11 +379,12 @@
                 summed[block_at(place, order, b)] = sums[start : start + MOST, :]
 
 
-def gradients(place, orders, routes_t, weights, hidden, backs, blocks):
+def gradients(place, orders, routes_t, weights, hidden, backs, early, blocks):
     ex_local, part, width = weights.shape
     rows = hidden.shape[1]
     tok = blocks[0].shape[0]
-    count = len(blocks)
+    tall = SUPER * MOST
+    count = 2 * SUPER
     grouped = lambda rows, columns: pl.BlockSpec((GROUPED, rows, columns), lambda e: (e, 0, 0))
     return pl.pallas_call(
         functools.partial(gradients_kernel, orders),
@@ -389,9 +394,10 @@
             VMEM,
             grouped(part, width),
             grouped(rows, part),
-            grouped(SUPER * MOST, part),
+            grouped(tall, part),
+            grouped(tall, width),
         ]
-        + [ANYWHERE] * count,
+        + [ANYWHERE] * SUPER,
         out_specs=[
             grouped(part, width),
             pl.BlockSpec((count, MOST, 128), lambda e: (0, 0, 0)),
@@ -402,15 +408,15 @@
         ],
         scratch_shapes=[
             pltpu.VMEM((rows, 128), f32),
-            pltpu.VMEM((count, tok, width), bf16),
-            pltpu.VMEM((ex_local, rows, width), bf16),
-            pltpu.SemaphoreType.DMA((count,)),
+            pltpu.VMEM((SUPER, tok, width), bf16),
+            pltpu.VMEM((ex_local, tall, width), bf16),
+            pltpu.SemaphoreType.DMA((SUPER,)),
         ],
         compiler_params=params(56),
         cost_estimate=cost(
             2 * ex_local * rows * width * (2 * part + 2 * tok), 4 * ex_local * part * width
         ),
-    )(place, routes_t, weights, hidden, backs, *blocks)
+    )(place, routes_t, weights, hidden, backs, early, *blocks)
 
 
 def outer_kernel(hidden, grads, out, total):
@@ -517,14 +523,14 @@
         received = trade(after(sent, near, side, far))
         orders = [[n for n, _ in early], [6, 10, 12, 14, 7, 11, 13, 15]]
         early = [x for _, x in early]
-        backs = early_products(place, orders[0], all_routes, w_down, early)
+        backs, rows = early_products(place, orders[0], all_routes, w_down, early)
         both = after(both, backs)
         both_side = hop(both, "dp", 2)
         arranged = arrange(place, orders, received, ex_local)
         late = [near_side, far_side, both, after(both_side, arranged)]
         late += [hop(x, "dp", 1) for x in late]
         d_w_down, sums = gradients(
-            place, orders, all_routes, w_down, arranged, backs, early + late
+            place, orders, all_routes, w_down, arranged, backs, rows, late
         )
     else:
         received = trade(sent)

time: 139 us -> 138 us (level)
  Pallas kernels: 47.1 us -> 45.7 us
    pallas_call x1, Pallas kernels: 26.9 us -> 24.4 us  [gradients(): pl.pallas_call(functools.partial(gradients_kernel, orders), grid=(ex_loca...]
  transfers between devices with their start and end apart: 17 -> 17, of which waited for: 5 -> 5; matrix products, arithmetic and copies ran while one was open for 1% -> 1% of each run, Pallas kernels for 14% -> 15%
where the time goes in v6:
time: 138 us; the launch traced here: 137 us
  Pallas kernels  45.7 us (33%)
  waiting for transfers between devices  42.2 us (31%)
  starting transfers between devices  22.2 us (16%)
  blocking collectives  14 us (10%)
  local copies, waits for them, and re-layouts  12.4 us (9%)
    ppermute x15, waiting for transfers between devices, hop(): return lax.ppermute(block, axis, [(i, i ^ flip) for i in range(size)])  42.2 us
    pallas_call x1, Pallas kernels, gradients(): pl.pallas_call(functools.partial(gradients_kernel, orders), grid=(ex_loca...  24.4 us
    pallas_call x1, Pallas kernels, early_products(): pl.pallas_call(functools.partial(early_kernel, order), grid=(ex_local //...  15 us
    all_to_all x1, blocking collectives, body(): lax.all_to_all(x, GROUP, split_axis=0, concat_axis=0, tiled=True)  14 us
    ppermute x15, starting transfers between devices, hop(): return lax.ppermute(block, axis, [(i, i ^ flip) for i in range(size)])  14 us
    unnamed x46, local copies, waits for them, and re-layouts  12.2 us
    all_to_all x2, starting transfers between devices, body(): lax.all_to_all(x, GROUP, split_axis=0, concat_axis=0, tiled=True)  8.16 us
    pallas_call x1, Pallas kernels, pack(): pl.pallas_call(functools.partial(pack_kernel, n_dp, half), grid=(n_expert...  3.27 us
  transfers between devices with their start and end apart: 17, of which 5 were waited for; matrix products, arithmetic and copies ran while one was open for 1% of the time, Pallas kernels for 15%

profile of v6, /device:TPU:0, one launch (start us, length us, event | category | flops | bytes accessed | tf_op | source)
XLA Modules:
  0.0 137.3 jit_solution(12981721974713398565)
XLA Ops:
  0.6 0.5 collective-permute-start
  1.1 2.6 %collective-permute-start.2 = (bf16[128,2048]{1,0:T(8,128)(2,1)}, bf16[128,2048]{1,0:T(8,128)(2,1)S(1)}, u32[]{:S(2)}, u32[]{:S(2)}) collective-permute-start(bf16[128,2048]{1,0:T(8,128)(2,1)} %refs_0_.1), channel_id=1, source_target_pairs={{0,2},{1,3},{2,0},{3,1},{4,6},{5,7},{6,4},{7,5},{8,10},{9,11},{10,... | collective-permute-start | bytes 1572872 | tf_op jit(solution)/shard_map/ppermute | solution.py:482
  3.7 1.6 %collective-permute-start.1 = (bf16[128,2048]{1,0:T(8,128)(2,1)}, bf16[128,2048]{1,0:T(8,128)(2,1)S(1)}, u32[]{:S(2)}, u32[]{:S(2)}) collective-permute-start(bf16[128,2048]{1,0:T(8,128)(2,1)} %refs_0_.1), channel_id=1, source_target_pairs={{0,4},{4,0},{8,12},{12,8},{1,5},{5,1},{9,13},{13,9},{2,6},{6,2},{1... | collective-permute-start | bytes 1572872 | tf_op jit(solution)/shard_map/ppermute | solution.py:482
  5.3 2.6 %collective-permute-start.3 = (bf16[128,2048]{1,0:T(8,128)(2,1)}, bf16[128,2048]{1,0:T(8,128)(2,1)S(1)}, u32[]{:S(2)}, u32[]{:S(2)}) collective-permute-start(bf16[128,2048]{1,0:T(8,128)(2,1)} %refs_0_.1), channel_id=1, source_target_pairs={{0,8},{4,12},{8,0},{12,4},{1,9},{5,13},{9,1},{13,5},{2,10},{6,14},... | collective-permute-start | bytes 1572872 | tf_op jit(solution)/shard_map/ppermute | solution.py:482
  7.9 0.8 copy.13
  8.7 0.1 reshape.14.weights_flat
  8.8 0.8 copy.12
  9.6 0.1 reshape.13.routes_flat
  9.7 0.0 collective-permute-done.early.refs_4_
  9.7 0.0 copy-start.10
  9.7 0.0 copy-start.13
  9.7 0.7 copy-done.13
  10.4 1.4 %copy-done.17 = bf16[128,8,768]{2,1,0:T(8,128)(2,1)S(1)} copy-done((bf16[128,8,768]{2,1,0:T(8,128)(2,1)S(1)}, bf16[128,8,768]{2,1,0:T(8,128)(2,1)}, u32[]{:S(2)}) %copy-start.17) | copy-done | bytes 1572888
  11.8 3.3 %shard_map.68 = (bf16[16,144,384]{2,1,0:T(8,128)(2,1)S(1)}, s32[16,8,128]{2,1,0:T(8,128)}) custom-call(s32[8,128]{1,0:T(8,128)S(1)} %bitcast.6, s32[1,1024]{1,0:T(1,128)S(1)} %reshape.13.routes_flat, bf16[1,1024]{1,0:T(2,128)(2,1)S(1)} %reshape.14.weights_flat, bf16[1024,768]{1,0:T(8,128)(2,1)S(1)} %bitcast.9, ...), custom_call_target="tpu_custom_call" | custom-call | flops 1811939328 | bytes 4718592 | tf_op jit(solution)/shard_map/pallas_call | solution.py:83
  15.1 0.0 copy-done.10
  15.1 1.2 copy-done.1
  16.3 3.5 %all-to-all-start = ((s32[16,8,128]{2,1,0:T(8,128)}), s32[16,8,128]{2,1,0:T(8,128)S(1)}, u32[]{:S(2)}, u32[]{:S(2)}) async-start(s32[16,8,128]{2,1,0:T(8,128)} %get-tuple-element.8), calls=%async_computation | async-start | bytes 131072 | tf_op jit(solution)/shard_map/all_to_all | solution.py:497
  19.8 0.0 collective-permute-done.2.refs_2_
  19.8 0.0 copy-start.7
  19.8 9.4 %collective-permute-done.1.refs_1_ = bf16[128,2048]{1,0:T(8,128)(2,1)S(1)} collective-permute-done((bf16[128,2048]{1,0:T(8,128)(2,1)}, bf16[128,2048]{1,0:T(8,128)(2,1)S(1)}, u32[]{:S(2)}, u32[]{:S(2)}) %collective-permute-start.1) | collective-permute-done | bytes 524320 | tf_op jit(solution)/shard_map/ppermute | solution.py:482
  29.2 2.8 %collective-permute-done.3.refs_3_ = bf16[128,2048]{1,0:T(8,128)(2,1)S(1)} collective-permute-done((bf16[128,2048]{1,0:T(8,128)(2,1)}, bf16[128,2048]{1,0:T(8,128)(2,1)S(1)}, u32[]{:S(2)}, u32[]{:S(2)}) %collective-permute-start.3) | collective-permute-done | bytes 524320 | tf_op jit(solution)/shard_map/ppermute | solution.py:482
  32.0 0.0 copy-done.7
  32.0 0.0 copy-done.5
  32.0 0.8 copy-done.3
  32.8 0.0 all-to-all-done.routes_t
  32.8 0.0 copy-start.12
  32.8 4.7 %all-to-all-start.1 = ((bf16[16,144,384]{2,1,0:T(8,128)(2,1)}), bf16[16,144,384]{2,1,0:T(8,128)(2,1)S(1)}, u32[]{:S(2)}, u32[]{:S(2)}) async-start(bf16[16,144,384]{2,1,0:T(8,128)(2,1)} %shard_map.69), calls=%async_computation.1 | async-start | bytes 3538944 | tf_op jit(solution)/shard_map/all_to_all | solution.py:497
  37.5 0.5 collective-permute-start.5
  38.0 0.1 collective-permute-start.4
  38.1 0.0 copy-done.4
  38.1 0.4 collective-permute-start.6
  38.5 1.7 %collective-permute-start.9 = (bf16[128,2048]{1,0:T(8,128)(2,1)S(1)}, bf16[128,2048]{1,0:T(8,128)(2,1)}, u32[]{:S(2)}, u32[]{:S(2)}) collective-permute-start(bf16[128,2048]{1,0:T(8,128)(2,1)S(1)} %copy-done.4), channel_id=1, source_target_pairs={{0,4},{4,0},{8,12},{12,8},{1,5},{5,1},{9,13},{13,9},{2,6},{6,2},{1... | collective-permute-start | bytes 1572872 | tf_op jit(solution)/shard_map/ppermute | solution.py:482
  40.2 0.1 pad_add_fusion.place
  40.3 1.5 %collective-permute-start.7 = (bf16[128,2048]{1,0:T(8,128)(2,1)S(1)}, bf16[128,2048]{1,0:T(8,128)(2,1)}, u32[]{:S(2)}, u32[]{:S(2)}) collective-permute-start(bf16[128,2048]{1,0:T(8,128)(2,1)S(1)} %copy-done.6), channel_id=1, source_target_pairs={{0,2},{1,3},{2,0},{3,1},{4,6},{5,7},{6,4},{7,5},{8,10},{9,11},{10,... | collective-permute-start | bytes 1572872 | tf_op jit(solution)/shard_map/ppermute | solution.py:482
  41.7 0.0 collective-permute-done.5.refs_6_
  41.7 0.6 collective-permute-start.8
  42.3 0.0 collective-permute-done.4.refs_5_
  42.3 0.0 collective-permute-done.6.refs_7_
  42.3 1.0 copy-done.9
  43.4 1.0 copy-done.11
  44.4 15.0 %shard_map.71 = (f32[16,144,192]{2,1,0:T(8,128)S(1)}, bf16[16,144,2048]{2,1,0:T(8,128)(2,1)}) custom-call(s32[2]{0:T(128)S(1)} %pad_add_fusion.place, s32[16,8,128]{2,1,0:T(8,128)S(1)} %all-to-all-done.routes_t, bf16[16,192,2048]{2,1,0:T(8,128)(2,1)} %weights.3, bf16[128,2048]{1,0:T(8,128)(2,1)S(1)} %copy-done.9, bf16[128,2048]{1,0:T(8,128)(2,1)S(1)} %copy-done.6, ...), custom_call_target="tpu_custom_call" | custom-call | flops 4227858432 | bytes 12582912 | tf_op jit(solution)/shard_map/pallas_call | solution.py:317
  59.4 1.4 copy-done.2
  60.8 19.7 %collective-permute-done.9.refs_0_ = bf16[128,2048]{1,0:T(8,128)(2,1)} collective-permute-done((bf16[128,2048]{1,0:T(8,128)(2,1)S(1)}, bf16[128,2048]{1,0:T(8,128)(2,1)}, u32[]{:S(2)}, u32[]{:S(2)}) %collective-permute-start.9) | collective-permute-done | bytes 524320 | tf_op jit(solution)/shard_map/ppermute | solution.py:482
  80.5 1.5 %collective-permute-start.10 = (bf16[128,2048]{1,0:T(8,128)(2,1)}, bf16[128,2048]{1,0:T(8,128)(2,1)S(1)}, u32[]{:S(2)}, u32[]{:S(2)}) collective-permute-start(bf16[128,2048]{1,0:T(8,128)(2,1)} %shard_map.72.refs_2_), channel_id=1, source_target_pairs={{0,2},{1,3},{2,0},{3,1},{4,6},{5,7},{6,4},{7,5},{8,10},{9,11},{10,... | collective-permute-start | bytes 1572872 | tf_op jit(solution)/shard_map/ppermute | solution.py:482
  82.0 0.0 collective-permute-start.13
  82.0 0.0 collective-permute-done.7.refs_0_
  82.0 0.5 collective-permute-start.11
  82.5 0.0 collective-permute-done.8.refs_1_
  82.5 0.1 collective-permute-start.12
  82.6 0.0 all-to-all-done.1.received
  82.6 2.0 %shard_map.70.refs_1_.hidden = bf16[16,288,192]{2,1,0:T(8,128)(2,1)S(1)} custom-call(s32[2]{0:T(128)S(1)} %pad_add_fusion.place, bf16[16,144,384]{2,1,0:T(8,128)(2,1)S(1)} %all-to-all-done.1.received), custom_call_target="tpu_custom_call" | custom-call | flops 1019215872 | bytes 4194304 | tf_op jit(solution)/shard_map/pallas_call | solution.py:239
  84.6 1.4 %copy-done = bf16[16,288,192]{2,1,0:T(8,128)(2,1)} copy-done((bf16[16,288,192]{2,1,0:T(8,128)(2,1)}, bf16[16,288,192]{2,1,0:T(8,128)(2,1)S(1)}, u32[]{:S(2)}) %copy-start) | copy-done | bytes 1769496
  86.0 8.2 %collective-permute-done.10.refs_0_ = bf16[128,2048]{1,0:T(8,128)(2,1)S(1)} collective-permute-done((bf16[128,2048]{1,0:T(8,128)(2,1)}, bf16[128,2048]{1,0:T(8,128)(2,1)S(1)}, u32[]{:S(2)}, u32[]{:S(2)}) %collective-permute-start.10) | collective-permute-done | bytes 524320 | tf_op jit(solution)/shard_map/ppermute | solution.py:482
  94.2 0.8 copy-done.18
  95.0 0.0 collective-permute-start.14
  95.0 0.0 collective-permute-done.11.refs_4_
  95.0 0.0 collective-permute-done.12.refs_5_
  95.0 0.0 collective-permute-done.13.refs_6_
  95.0 2.1 %collective-permute-done.14.refs_7_ = bf16[128,2048]{1,0:T(8,128)(2,1)S(1)} collective-permute-done((bf16[128,2048]{1,0:T(8,128)(2,1)}, bf16[128,2048]{1,0:T(8,128)(2,1)S(1)}, u32[]{:S(2)}, u32[]{:S(2)}) %collective-permute-start.14) | collective-permute-done | bytes 524320 | tf_op jit(solution)/shard_map/ppermute | solution.py:482
  97.1 0.8 copy-done.21
  97.9 24.4 %shard_map.74 = (bf16[16,192,2048]{2,1,0:T(8,128)(2,1)}, f32[16,18,128]{2,1,0:T(8,128)}) custom-call(s32[2]{0:T(128)} %copy-done.16, s32[16,8,128]{2,1,0:T(8,128)} %copy-done.12, bf16[16,192,2048]{2,1,0:T(8,128)(2,1)} %weights.3, bf16[16,288,192]{2,1,0:T(8,128)(2,1)} %copy-done, f32[16,144,192]{2,1,0:T(8,128)} %copy-done.2, ...), custom_call_target="tpu_custom_call" | custom-call | flops 12079595520 | bytes 25165824 | tf_op jit(solution)/shard_map/pallas_call | solution.py:389
  122.3 14.0 %all_to_all.15.returned = f32[16,18,128]{2,1,0:T(8,128)S(1)} all-to-all(f32[16,18,128]{2,1,0:T(8,128)} %get-tuple-element.13), channel_id=1, replica_groups=mesh['groups'=2,'expert'=4,'dp'=4] {'expert','dp'}, dimensions={0} | all-to-all | bytes 294912 | tf_op jit(solution)/shard_map/all_to_all | solution.py:497
  136.3 0.0 copy-done.15
  136.3 1.0 shard_map.75
  (28 shorter events, 0.0 us)
Async XLA Ops:
  0.6 9.0 %collective-permute-start = (bf16[128,2048]{1,0:T(8,128)(2,1)}, bf16[128,2048]{1,0:T(8,128)(2,1)S(1)}, u32[]{:S(2)}, u32[]{:S(2)}) collective-permute-start(bf16[128,2048]{1,0:T(8,128)(2,1)} %refs_0_.1), channel_id=1, source_target_pairs={{0,1},{1,0},{2,3},{3,2},{4,5},{5,4},{6,7},{7,6},{8,9},{9,8},{10,11... | collective-permute-start | bytes 1572872 | tf_op jit(solution)/shard_map/ppermute | solution.py:482
  1.1 18.6 %collective-permute-start.2 = (bf16[128,2048]{1,0:T(8,128)(2,1)}, bf16[128,2048]{1,0:T(8,128)(2,1)S(1)}, u32[]{:S(2)}, u32[]{:S(2)}) collective-permute-start(bf16[128,2048]{1,0:T(8,128)(2,1)} %refs_0_.1), channel_id=1, source_target_pairs={{0,2},{1,3},{2,0},{3,1},{4,6},{5,7},{6,4},{7,5},{8,10},{9,11},{10,... | collective-permute-start | bytes 1572872 | tf_op jit(solution)/shard_map/ppermute | solution.py:482
  3.7 25.5 %collective-permute-start.1 = (bf16[128,2048]{1,0:T(8,128)(2,1)}, bf16[128,2048]{1,0:T(8,128)(2,1)S(1)}, u32[]{:S(2)}, u32[]{:S(2)}) collective-permute-start(bf16[128,2048]{1,0:T(8,128)(2,1)} %refs_0_.1), channel_id=1, source_target_pairs={{0,4},{4,0},{8,12},{12,8},{1,5},{5,1},{9,13},{13,9},{2,6},{6,2},{1... | collective-permute-start | bytes 1572872 | tf_op jit(solution)/shard_map/ppermute | solution.py:482
  5.3 26.7 %collective-permute-start.3 = (bf16[128,2048]{1,0:T(8,128)(2,1)}, bf16[128,2048]{1,0:T(8,128)(2,1)S(1)}, u32[]{:S(2)}, u32[]{:S(2)}) collective-permute-start(bf16[128,2048]{1,0:T(8,128)(2,1)} %refs_0_.1), channel_id=1, source_target_pairs={{0,8},{4,12},{8,0},{12,4},{1,9},{5,13},{9,1},{13,5},{2,10},{6,14},... | collective-permute-start | bytes 1572872 | tf_op jit(solution)/shard_map/ppermute | solution.py:482
  9.7 5.4 %copy-start.10 = (bf16[128,2048]{1,0:T(8,128)(2,1)}, bf16[128,2048]{1,0:T(8,128)(2,1)S(1)}, u32[]{:S(2)}) copy-start(bf16[128,2048]{1,0:T(8,128)(2,1)S(1)} %collective-permute-done.early.refs_4_) | copy-start | bytes 1572868
  9.7 0.7 copy-start.13
  10.4 1.4 %copy-start.17 = (bf16[128,8,768]{2,1,0:T(8,128)(2,1)S(1)}, bf16[128,8,768]{2,1,0:T(8,128)(2,1)}, u32[]{:S(2)}) copy-start(bf16[128,8,768]{2,1,0:T(8,128)(2,1)} %param.7) | copy-start | bytes 4718596
  15.1 1.2 copy-start.1
  16.3 16.5 %all-to-all-start = ((s32[16,8,128]{2,1,0:T(8,128)}), s32[16,8,128]{2,1,0:T(8,128)S(1)}, u32[]{:S(2)}, u32[]{:S(2)}) async-start(s32[16,8,128]{2,1,0:T(8,128)} %get-tuple-element.8), calls=%async_computation | async-start | bytes 131072 | tf_op jit(solution)/shard_map/all_to_all | solution.py:497
  19.8 12.2 %copy-start.7 = (bf16[128,2048]{1,0:T(8,128)(2,1)}, bf16[128,2048]{1,0:T(8,128)(2,1)S(1)}, u32[]{:S(2)}) copy-start(bf16[128,2048]{1,0:T(8,128)(2,1)S(1)} %collective-permute-done.2.refs_2_) | copy-start | bytes 1572868
  29.2 2.8 %copy-start.5 = (bf16[128,2048]{1,0:T(8,128)(2,1)}, bf16[128,2048]{1,0:T(8,128)(2,1)S(1)}, u32[]{:S(2)}) copy-start(bf16[128,2048]{1,0:T(8,128)(2,1)S(1)} %collective-permute-done.1.refs_1_) | copy-start | bytes 1572868
  32.0 0.8 copy-start.3
  32.8 4.7 %copy-start.8 = (bf16[128,2048]{1,0:T(8,128)(2,1)S(1)}, bf16[128,2048]{1,0:T(8,128)(2,1)}, u32[]{:S(2)}) copy-start(bf16[128,2048]{1,0:T(8,128)(2,1)} %copy-done.7) | copy-start | bytes 1572868
  32.8 5.2 %copy-start.6 = (bf16[128,2048]{1,0:T(8,128)(2,1)S(1)}, bf16[128,2048]{1,0:T(8,128)(2,1)}, u32[]{:S(2)}) copy-start(bf16[128,2048]{1,0:T(8,128)(2,1)} %copy-done.5) | copy-start | bytes 1572868
  32.8 5.3 %copy-start.4 = (bf16[128,2048]{1,0:T(8,128)(2,1)S(1)}, bf16[128,2048]{1,0:T(8,128)(2,1)}, u32[]{:S(2)}) copy-start(bf16[128,2048]{1,0:T(8,128)(2,1)} %copy-done.3) | copy-start | bytes 1572868
  32.8 26.6 %copy-start.12 = (s32[16,8,128]{2,1,0:T(8,128)}, s32[16,8,128]{2,1,0:T(8,128)S(1)}, u32[]{:S(2)}) copy-start(s32[16,8,128]{2,1,0:T(8,128)S(1)} %all-to-all-done.routes_t) | copy-start | bytes 196612
  32.8 49.7 %all-to-all-start.1 = ((bf16[16,144,384]{2,1,0:T(8,128)(2,1)}), bf16[16,144,384]{2,1,0:T(8,128)(2,1)S(1)}, u32[]{:S(2)}, u32[]{:S(2)}) async-start(bf16[16,144,384]{2,1,0:T(8,128)(2,1)} %shard_map.69), calls=%async_computation.1 | async-start | bytes 3538944 | tf_op jit(solution)/shard_map/all_to_all | solution.py:497
  37.5 4.2 %collective-permute-start.5 = (bf16[128,2048]{1,0:T(8,128)(2,1)S(1)}, bf16[128,2048]{1,0:T(8,128)(2,1)}, u32[]{:S(2)}, u32[]{:S(2)}) collective-permute-start(bf16[128,2048]{1,0:T(8,128)(2,1)S(1)} %copy-done.8), channel_id=1, source_target_pairs={{0,1},{1,0},{2,3},{3,2},{4,5},{5,4},{6,7},{7,6},{8,9},{9,8},{10,11... | collective-permute-start | bytes 1572872 | tf_op jit(solution)/shard_map/ppermute | solution.py:482
  38.0 4.3 %collective-permute-start.4 = (bf16[128,2048]{1,0:T(8,128)(2,1)S(1)}, bf16[128,2048]{1,0:T(8,128)(2,1)}, u32[]{:S(2)}, u32[]{:S(2)}) collective-permute-start(bf16[128,2048]{1,0:T(8,128)(2,1)S(1)} %copy-done.6), channel_id=1, source_target_pairs={{0,1},{1,0},{2,3},{3,2},{4,5},{5,4},{6,7},{7,6},{8,9},{9,8},{10,11... | collective-permute-start | bytes 1572872 | tf_op jit(solution)/shard_map/ppermute | solution.py:482
  38.1 4.2 %collective-permute-start.6 = (bf16[128,2048]{1,0:T(8,128)(2,1)S(1)}, bf16[128,2048]{1,0:T(8,128)(2,1)}, u32[]{:S(2)}, u32[]{:S(2)}) collective-permute-start(bf16[128,2048]{1,0:T(8,128)(2,1)S(1)} %copy-done.4), channel_id=1, source_target_pairs={{0,1},{1,0},{2,3},{3,2},{4,5},{5,4},{6,7},{7,6},{8,9},{9,8},{10,11... | collective-permute-start | bytes 1572872 | tf_op jit(solution)/shard_map/ppermute | solution.py:482
  38.5 42.0 %collective-permute-start.9 = (bf16[128,2048]{1,0:T(8,128)(2,1)S(1)}, bf16[128,2048]{1,0:T(8,128)(2,1)}, u32[]{:S(2)}, u32[]{:S(2)}) collective-permute-start(bf16[128,2048]{1,0:T(8,128)(2,1)S(1)} %copy-done.4), channel_id=1, source_target_pairs={{0,4},{4,0},{8,12},{12,8},{1,5},{5,1},{9,13},{13,9},{2,6},{6,2},{1... | collective-permute-start | bytes 1572872 | tf_op jit(solution)/shard_map/ppermute | solution.py:482
  40.3 42.3 %copy-start.16 = (s32[2]{0:T(128)}, s32[2]{0:T(128)S(1)}, u32[]{:S(2)}) copy-start(s32[2]{0:T(128)S(1)} %pad_add_fusion.place) | copy-start | bytes 28
  40.3 41.7 %collective-permute-start.7 = (bf16[128,2048]{1,0:T(8,128)(2,1)S(1)}, bf16[128,2048]{1,0:T(8,128)(2,1)}, u32[]{:S(2)}, u32[]{:S(2)}) collective-permute-start(bf16[128,2048]{1,0:T(8,128)(2,1)S(1)} %copy-done.6), channel_id=1, source_target_pairs={{0,2},{1,3},{2,0},{3,1},{4,6},{5,7},{6,4},{7,5},{8,10},{9,11},{10,... | collective-permute-start | bytes 1572872 | tf_op jit(solution)/shard_map/ppermute | solution.py:482
  41.7 40.8 %collective-permute-start.8 = (bf16[128,2048]{1,0:T(8,128)(2,1)S(1)}, bf16[128,2048]{1,0:T(8,128)(2,1)}, u32[]{:S(2)}, u32[]{:S(2)}) collective-permute-start(bf16[128,2048]{1,0:T(8,128)(2,1)S(1)} %copy-done.4), channel_id=1, source_target_pairs={{0,2},{1,3},{2,0},{3,1},{4,6},{5,7},{6,4},{7,5},{8,10},{9,11},{10,... | collective-permute-start | bytes 1572872 | tf_op jit(solution)/shard_map/ppermute | solution.py:482
  42.3 1.0 copy-start.9
  43.4 1.0 copy-start.11
  59.4 1.4 %copy-start.2 = (f32[16,144,192]{2,1,0:T(8,128)}, f32[16,144,192]{2,1,0:T(8,128)S(1)}, u32[]{:S(2)}) copy-start(f32[16,144,192]{2,1,0:T(8,128)S(1)} %get-tuple-element.10.refs_1_.backs) | copy-start | bytes 5308420
  80.5 13.7 %collective-permute-start.10 = (bf16[128,2048]{1,0:T(8,128)(2,1)}, bf16[128,2048]{1,0:T(8,128)(2,1)S(1)}, u32[]{:S(2)}, u32[]{:S(2)}) collective-permute-start(bf16[128,2048]{1,0:T(8,128)(2,1)} %shard_map.72.refs_2_), channel_id=1, source_target_pairs={{0,2},{1,3},{2,0},{3,1},{4,6},{5,7},{6,4},{7,5},{8,10},{9,11},{10,... | collective-permute-start | bytes 1572872 | tf_op jit(solution)/shard_map/ppermute | solution.py:482
  82.0 13.0 %collective-permute-start.13 = (bf16[128,2048]{1,0:T(8,128)(2,1)}, bf16[128,2048]{1,0:T(8,128)(2,1)}, u32[]{:S(2)}, u32[]{:S(2)}) collective-permute-start(bf16[128,2048]{1,0:T(8,128)(2,1)} %shard_map.72.refs_2_), channel_id=1, source_target_pairs={{0,1},{1,0},{2,3},{3,2},{4,5},{5,4},{6,7},{7,6},{8,9},{9,8},{10,11... | collective-permute-start | bytes 1572872 | tf_op jit(solution)/shard_map/ppermute | solution.py:482
  82.0 13.0 %collective-permute-start.11 = (bf16[128,2048]{1,0:T(8,128)(2,1)}, bf16[128,2048]{1,0:T(8,128)(2,1)S(1)}, u32[]{:S(2)}, u32[]{:S(2)}) collective-permute-start(bf16[128,2048]{1,0:T(8,128)(2,1)} %collective-permute-done.7.refs_0_), channel_id=1, source_target_pairs={{0,1},{1,0},{2,3},{3,2},{4,5},{5,4},{6,7},{7,6},{8,9},{9,8},{10,11... | collective-permute-start | bytes 1572872 | tf_op jit(solution)/shard_map/ppermute | solution.py:482
  82.5 12.5 %collective-permute-start.12 = (bf16[128,2048]{1,0:T(8,128)(2,1)}, bf16[128,2048]{1,0:T(8,128)(2,1)S(1)}, u32[]{:S(2)}, u32[]{:S(2)}) collective-permute-start(bf16[128,2048]{1,0:T(8,128)(2,1)} %collective-permute-done.8.refs_1_), channel_id=1, source_target_pairs={{0,1},{1,0},{2,3},{3,2},{4,5},{5,4},{6,7},{7,6},{8,9},{9,8},{10,11... | collective-permute-start | bytes 1572872 | tf_op jit(solution)/shard_map/ppermute | solution.py:482
  84.6 1.4 %copy-start = (bf16[16,288,192]{2,1,0:T(8,128)(2,1)}, bf16[16,288,192]{2,1,0:T(8,128)(2,1)S(1)}, u32[]{:S(2)}) copy-start(bf16[16,288,192]{2,1,0:T(8,128)(2,1)S(1)} %shard_map.70.refs_1_.hidden) | copy-start | bytes 5308420
  94.2 0.8 copy-start.18
  95.0 2.1 %collective-permute-start.14 = (bf16[128,2048]{1,0:T(8,128)(2,1)}, bf16[128,2048]{1,0:T(8,128)(2,1)S(1)}, u32[]{:S(2)}, u32[]{:S(2)}) collective-permute-start(bf16[128,2048]{1,0:T(8,128)(2,1)} %shard_map.73.refs_3_), channel_id=1, source_target_pairs={{0,1},{1,0},{2,3},{3,2},{4,5},{5,4},{6,7},{7,6},{8,9},{9,8},{10,11... | collective-permute-start | bytes 1572872 | tf_op jit(solution)/shard_map/ppermute | solution.py:482
  95.0 2.1 %copy-start.19 = (bf16[128,2048]{1,0:T(8,128)(2,1)}, bf16[128,2048]{1,0:T(8,128)(2,1)S(1)}, u32[]{:S(2)}) copy-start(bf16[128,2048]{1,0:T(8,128)(2,1)S(1)} %collective-permute-done.11.refs_4_) | copy-start | bytes 1572868
  95.0 2.1 %copy-start.20 = (bf16[128,2048]{1,0:T(8,128)(2,1)}, bf16[128,2048]{1,0:T(8,128)(2,1)S(1)}, u32[]{:S(2)}) copy-start(bf16[128,2048]{1,0:T(8,128)(2,1)S(1)} %collective-permute-done.12.refs_5_) | copy-start | bytes 1572868
  97.1 0.8 copy-start.21
  97.9 38.5 %copy-start.14 = (s32[128,8]{0,1:T(8,128)S(1)}, s32[128,8]{0,1:T(8,128)}, u32[]{:S(2)}) copy-start(s32[128,8]{0,1:T(8,128)} %param.5) | copy-start | bytes 12292
  97.9 38.5 %copy-start.15 = (bf16[128,8]{0,1:T(8,128)(2,1)S(1)}, bf16[128,8]{0,1:T(8,128)(2,1)}, u32[]{:S(2)}) copy-start(bf16[128,8]{0,1:T(8,128)(2,1)} %param.6) | copy-start | bytes 6148

commit v7 on v6

--- a/solution.py
+++ b/solution.py
@@ -184,16 +184,22 @@
 
 
 def fetch(sources, held, sems):
-    copies = [
-        pltpu.make_async_copy(source, held.at[i], sems.at[i]) for i, source in enumerate(sources)
-    ]
-    for copy in copies:
+    copies = [[] for _ in range(held.shape[0])]
+    rows = held.shape[1]
+    for n, source in enumerate(sources):
+        i = next(i for i, parts in enumerate(copies) if sum(p for p, _ in parts) < rows)
+        filled = sum(size for size, _ in copies[i])
+        size = source.shape[0]
+        target = held.at[i, pl.ds(filled, size)]
+        copy = pltpu.make_async_copy(source, target, sems.at[n])
+        copies[i].append((size, copy))
         copy.start()
     waited = set()
 
     def block(i):
         if i not in waited:
-            copies[i].wait()
+            for _, copy in copies[i]:
+                copy.wait()
             waited.add(i)
         return held.at[i]
 
@@ -339,7 +345,7 @@
 
 
 def gradients_kernel(orders, place, routes_t, weights, hidden, backs, early, *refs):
-    count = SUPER
+    count = len(refs) - 6
     blocks, (out, summed, sums, held, rows, sems) = refs[:count], refs[count:]
     step = pl.program_id(0)
     tall = SUPER * MOST
@@ -385,6 +391,7 @@
     tok = blocks[0].shape[0]
     tall = SUPER * MOST
     count = 2 * SUPER
+    sources = len(blocks)
     grouped = lambda rows, columns: pl.BlockSpec((GROUPED, rows, columns), lambda e: (e, 0, 0))
     return pl.pallas_call(
         functools.partial(gradients_kernel, orders),
@@ -397,7 +404,7 @@
             grouped(tall, part),
             grouped(tall, width),
         ]
-        + [ANYWHERE] * SUPER,
+        + [ANYWHERE] * sources,
         out_specs=[
             grouped(part, width),
             pl.BlockSpec((count, MOST, 128), lambda e: (0, 0, 0)),
@@ -410,7 +417,7 @@
             pltpu.VMEM((rows, 128), f32),
             pltpu.VMEM((SUPER, tok, width), bf16),
             pltpu.VMEM((ex_local, tall, width), bf16),
-            pltpu.SemaphoreType.DMA((SUPER,)),
+            pltpu.SemaphoreType.DMA((sources,)),
         ],
         compiler_params=params(56),
         cost_estimate=cost(
@@ -524,10 +531,12 @@
         orders = [[n for n, _ in early], [6, 10, 12, 14, 7, 11, 13, 15]]
         early = [x for _, x in early]
         backs, rows = early_products(place, orders[0], all_routes, w_down, early)
-        both = after(both, backs)
-        both_side = hop(both, "dp", 2)
+        both, far_side = after(both, backs), after(far_side, backs)
+        middle = tok // 2
+        upper = hop(both[:middle], "dp", 2)
+        lower = hop(far_side[middle:], "expert", 1)
         arranged = arrange(place, orders, received, ex_local)
-        late = [near_side, far_side, both, after(both_side, arranged)]
+        late = [near_side, far_side, both, after(upper, arranged), lower]
         late += [hop(x, "dp", 1) for x in late]
         d_w_down, sums = gradients(
             place, orders, all_routes, w_down, arranged, backs, rows, late

time: 138 us -> 135 us (0.978)
  waiting for transfers between devices: 42.2 us -> 37.3 us
  local copies, waits for them, and re-layouts: 12.4 us -> 14.2 us
    ppermute x15 -> x17, waiting for transfers between devices: 42.2 us -> 37.3 us  [hop(): return lax.ppermute(block, axis, [(i, i ^ flip) for i in range(size)])]
    slice x0 -> x2, local copies, waits for them, and re-layouts: none -> 1.94 us  [the longest x1 0.97 us: body(): upper = hop(both[:middle], 'dp', 2)]
    ppermute x15 -> x17, starting transfers between devices: 14 us -> 14.4 us  [hop(): return lax.ppermute(block, axis, [(i, i ^ flip) for i in range(size)])]
  transfers between devices with their start and end apart: 17 -> 19, of which waited for: 5 -> 7; matrix products, arithmetic and copies ran while one was open for 1% -> 3% of each run, Pallas kernels for 15% -> 15%
where the time goes in v7:
time: 135 us; the launch traced here: 134 us
  Pallas kernels  45.7 us (34%)
  waiting for transfers between devices  37.3 us (28%)
  starting transfers between devices  22.5 us (17%)
  local copies, waits for them, and re-layouts  14.2 us (11%)
  blocking collectives  13.7 us (10%)
    ppermute x17, waiting for transfers between devices, hop(): return lax.ppermute(block, axis, [(i, i ^ flip) for i in range(size)])  37.3 us
    pallas_call x1, Pallas kernels, gradients(): pl.pallas_call(functools.partial(gradients_kernel, orders), grid=(ex_loca...  24.5 us
    pallas_call x1, Pallas kernels, early_products(): pl.pallas_call(functools.partial(early_kernel, order), grid=(ex_local //...  15 us
    ppermute x17, starting transfers between devices, hop(): return lax.ppermute(block, axis, [(i, i ^ flip) for i in range(size)])  14.4 us
    all_to_all x1, blocking collectives, body(): lax.all_to_all(x, GROUP, split_axis=0, concat_axis=0, tiled=True)  13.7 us
    unnamed x46, local copies, waits for them, and re-layouts  12.1 us
    all_to_all x2, starting transfers between devices, body(): lax.all_to_all(x, GROUP, split_axis=0, concat_axis=0, tiled=True)  8.14 us
    pallas_call x1, Pallas kernels, pack(): pl.pallas_call(functools.partial(pack_kernel, n_dp, half), grid=(n_expert...  3.27 us
  transfers between devices with their start and end apart: 19, of which 7 were waited for; matrix products, arithmetic and copies ran while one was open for 3% of the time, Pallas kernels for 15%

profile of v7, /device:TPU:0, one launch (start us, length us, event | category | flops | bytes accessed | tf_op | source)
XLA Modules:
  0.0 134.3 jit_solution(9487688074653333904)
XLA Ops:
  0.6 0.5 collective-permute-start
  1.1 2.6 %collective-permute-start.2 = (bf16[128,2048]{1,0:T(8,128)(2,1)}, bf16[128,2048]{1,0:T(8,128)(2,1)S(1)}, u32[]{:S(2)}, u32[]{:S(2)}) collective-permute-start(bf16[128,2048]{1,0:T(8,128)(2,1)} %refs_0_.1), channel_id=1, source_target_pairs={{0,2},{1,3},{2,0},{3,1},{4,6},{5,7},{6,4},{7,5},{8,10},{9,11},{10,... | collective-permute-start | bytes 1572872 | tf_op jit(solution)/shard_map/ppermute | solution.py:489
  3.7 1.6 %collective-permute-start.1 = (bf16[128,2048]{1,0:T(8,128)(2,1)}, bf16[128,2048]{1,0:T(8,128)(2,1)S(1)}, u32[]{:S(2)}, u32[]{:S(2)}) collective-permute-start(bf16[128,2048]{1,0:T(8,128)(2,1)} %refs_0_.1), channel_id=1, source_target_pairs={{0,4},{4,0},{8,12},{12,8},{1,5},{5,1},{9,13},{13,9},{2,6},{6,2},{1... | collective-permute-start | bytes 1572872 | tf_op jit(solution)/shard_map/ppermute | solution.py:489
  5.3 2.6 %collective-permute-start.3 = (bf16[128,2048]{1,0:T(8,128)(2,1)}, bf16[128,2048]{1,0:T(8,128)(2,1)S(1)}, u32[]{:S(2)}, u32[]{:S(2)}) collective-permute-start(bf16[128,2048]{1,0:T(8,128)(2,1)} %refs_0_.1), channel_id=1, source_target_pairs={{0,8},{4,12},{8,0},{12,4},{1,9},{5,13},{9,1},{13,5},{2,10},{6,14},... | collective-permute-start | bytes 1572872 | tf_op jit(solution)/shard_map/ppermute | solution.py:489
  7.9 0.8 copy.14
  8.7 0.1 reshape.14.weights_flat
  8.8 0.8 copy.13
  9.6 0.1 reshape.13.routes_flat
  9.7 0.0 collective-permute-done.early.refs_4_
  9.7 0.0 copy-start.13
  9.7 0.7 copy-done.13
  10.4 1.4 %copy-done.17 = bf16[128,8,768]{2,1,0:T(8,128)(2,1)S(1)} copy-done((bf16[128,8,768]{2,1,0:T(8,128)(2,1)S(1)}, bf16[128,8,768]{2,1,0:T(8,128)(2,1)}, u32[]{:S(2)}) %copy-start.17) | copy-done | bytes 1572888
  11.8 3.3 %shard_map.68 = (bf16[16,144,384]{2,1,0:T(8,128)(2,1)S(1)}, s32[16,8,128]{2,1,0:T(8,128)}) custom-call(s32[8,128]{1,0:T(8,128)S(1)} %bitcast.6, s32[1,1024]{1,0:T(1,128)S(1)} %reshape.13.routes_flat, bf16[1,1024]{1,0:T(2,128)(2,1)S(1)} %reshape.14.weights_flat, bf16[1024,768]{1,0:T(8,128)(2,1)S(1)} %bitcast.9, ...), custom_call_target="tpu_custom_call" | custom-call | flops 1811939328 | bytes 4718592 | tf_op jit(solution)/shard_map/pallas_call | solution.py:83
  15.1 1.2 copy-done.2
  16.3 3.5 %all-to-all-start = ((s32[16,8,128]{2,1,0:T(8,128)}), s32[16,8,128]{2,1,0:T(8,128)S(1)}, u32[]{:S(2)}, u32[]{:S(2)}) async-start(s32[16,8,128]{2,1,0:T(8,128)} %get-tuple-element.8), calls=%async_computation | async-start | bytes 131072 | tf_op jit(solution)/shard_map/all_to_all | solution.py:504
  19.8 0.0 collective-permute-done.2.refs_2_
  19.8 0.0 copy-start.7
  19.8 9.4 %collective-permute-done.1.refs_1_ = bf16[128,2048]{1,0:T(8,128)(2,1)S(1)} collective-permute-done((bf16[128,2048]{1,0:T(8,128)(2,1)}, bf16[128,2048]{1,0:T(8,128)(2,1)S(1)}, u32[]{:S(2)}, u32[]{:S(2)}) %collective-permute-start.1) | collective-permute-done | bytes 524320 | tf_op jit(solution)/shard_map/ppermute | solution.py:489
  29.2 2.8 %collective-permute-done.3.refs_3_ = bf16[128,2048]{1,0:T(8,128)(2,1)S(1)} collective-permute-done((bf16[128,2048]{1,0:T(8,128)(2,1)}, bf16[128,2048]{1,0:T(8,128)(2,1)S(1)}, u32[]{:S(2)}, u32[]{:S(2)}) %collective-permute-start.3) | collective-permute-done | bytes 524320 | tf_op jit(solution)/shard_map/ppermute | solution.py:489
  32.0 0.8 copy-done.3
  32.8 0.0 all-to-all-done.routes_t
  32.9 4.7 %all-to-all-start.1 = ((bf16[16,144,384]{2,1,0:T(8,128)(2,1)}), bf16[16,144,384]{2,1,0:T(8,128)(2,1)S(1)}, u32[]{:S(2)}, u32[]{:S(2)}) async-start(bf16[16,144,384]{2,1,0:T(8,128)(2,1)} %shard_map.69), calls=%async_computation.1 | async-start | bytes 3538944 | tf_op jit(solution)/shard_map/all_to_all | solution.py:504
  37.5 0.5 collective-permute-start.5
  38.0 0.1 collective-permute-start.4
  38.1 0.4 collective-permute-start.6
  38.5 1.7 %collective-permute-start.8 = (bf16[128,2048]{1,0:T(8,128)(2,1)S(1)}, bf16[128,2048]{1,0:T(8,128)(2,1)}, u32[]{:S(2)}, u32[]{:S(2)}) collective-permute-start(bf16[128,2048]{1,0:T(8,128)(2,1)S(1)} %copy-done.4), channel_id=1, source_target_pairs={{0,2},{1,3},{2,0},{3,1},{4,6},{5,7},{6,4},{7,5},{8,10},{9,11},{10,... | collective-permute-start | bytes 1572872 | tf_op jit(solution)/shard_map/ppermute | solution.py:489
  40.2 0.3 collective-permute-start.7
  40.5 0.0 collective-permute-done.5.refs_6_
  40.5 1.7 %collective-permute-start.9 = (bf16[128,2048]{1,0:T(8,128)(2,1)S(1)}, bf16[128,2048]{1,0:T(8,128)(2,1)}, u32[]{:S(2)}, u32[]{:S(2)}) collective-permute-start(bf16[128,2048]{1,0:T(8,128)(2,1)S(1)} %copy-done.4), channel_id=1, source_target_pairs={{0,4},{4,0},{8,12},{12,8},{1,5},{5,1},{9,13},{13,9},{2,6},{6,2},{1... | collective-permute-start | bytes 1572872 | tf_op jit(solution)/shard_map/ppermute | solution.py:489
  42.2 0.1 pad_add_fusion.place
  42.3 0.0 collective-permute-done.4.refs_5_
  42.3 0.0 collective-permute-done.6.refs_7_
  42.3 0.0 copy-start.9
  42.3 1.0 copy-done.9
  43.4 1.0 copy-done.11
  44.4 15.0 %shard_map.71 = (f32[16,144,192]{2,1,0:T(8,128)S(1)}, bf16[16,144,2048]{2,1,0:T(8,128)(2,1)}) custom-call(s32[2]{0:T(128)S(1)} %pad_add_fusion.place, s32[16,8,128]{2,1,0:T(8,128)S(1)} %all-to-all-done.routes_t, bf16[16,192,2048]{2,1,0:T(8,128)(2,1)} %weights.3, bf16[128,2048]{1,0:T(8,128)(2,1)S(1)} %copy-done.9, bf16[128,2048]{1,0:T(8,128)(2,1)S(1)} %copy-done.6, ...), custom_call_target="tpu_custom_call" | custom-call | flops 4227858432 | bytes 12582912 | tf_op jit(solution)/shard_map/pallas_call | solution.py:323
  59.4 1.4 %copy-done.1 = f32[16,144,192]{2,1,0:T(8,128)} copy-done((f32[16,144,192]{2,1,0:T(8,128)}, f32[16,144,192]{2,1,0:T(8,128)S(1)}, u32[]{:S(2)}) %copy-start.1) | copy-done | bytes 1769496
  60.8 5.9 %collective-permute-done.8.refs_0_ = bf16[128,2048]{1,0:T(8,128)(2,1)} collective-permute-done((bf16[128,2048]{1,0:T(8,128)(2,1)S(1)}, bf16[128,2048]{1,0:T(8,128)(2,1)}, u32[]{:S(2)}, u32[]{:S(2)}) %collective-permute-start.8) | collective-permute-done | bytes 524320 | tf_op jit(solution)/shard_map/ppermute | solution.py:489
  66.7 1.0 slice.9
  67.7 1.5 %collective-permute-start.11 = (bf16[64,2048]{1,0:T(8,128)(2,1)S(1)}, bf16[64,2048]{1,0:T(8,128)(2,1)}, u32[]{:S(2)}, u32[]{:S(2)}) collective-permute-start(bf16[64,2048]{1,0:T(8,128)(2,1)S(1)} %slice.9), channel_id=1, source_target_pairs={{0,4},{4,0},{8,12},{12,8},{1,5},{5,1},{9,13},{13,9},{2,6},{6,2},{1... | collective-permute-start | bytes 786440 | tf_op jit(solution)/shard_map/ppermute | solution.py:489
  69.2 0.0 collective-permute-start.13
  69.2 13.0 %collective-permute-done.7.refs_0_ = bf16[128,2048]{1,0:T(8,128)(2,1)} collective-permute-done((bf16[128,2048]{1,0:T(8,128)(2,1)S(1)}, bf16[128,2048]{1,0:T(8,128)(2,1)}, u32[]{:S(2)}, u32[]{:S(2)}) %collective-permute-start.7) | collective-permute-done | bytes 524320 | tf_op jit(solution)/shard_map/ppermute | solution.py:489
  82.2 0.0 collective-permute-start.12
  82.2 0.0 collective-permute-done.9.refs_0_
  82.2 1.0 slice.8
  83.2 0.6 collective-permute-start.14
  83.7 0.4 collective-permute-start.10
  84.1 2.0 %collective-permute-done.11.refs_4_ = bf16[64,2048]{1,0:T(8,128)(2,1)} collective-permute-done((bf16[64,2048]{1,0:T(8,128)(2,1)S(1)}, bf16[64,2048]{1,0:T(8,128)(2,1)}, u32[]{:S(2)}, u32[]{:S(2)}) %collective-permute-start.11) | collective-permute-done | bytes 262176 | tf_op jit(solution)/shard_map/ppermute | solution.py:489
  86.1 0.0 collective-permute-start.16
  86.1 0.0 all-to-all-done.1.received
  86.1 2.0 %shard_map.70.refs_1_.hidden = bf16[16,288,192]{2,1,0:T(8,128)(2,1)S(1)} custom-call(s32[2]{0:T(128)S(1)} %pad_add_fusion.place, bf16[16,144,384]{2,1,0:T(8,128)(2,1)S(1)} %all-to-all-done.1.received), custom_call_target="tpu_custom_call" | custom-call | flops 1019215872 | bytes 4194304 | tf_op jit(solution)/shard_map/pallas_call | solution.py:245
  88.1 1.4 %copy-done = bf16[16,288,192]{2,1,0:T(8,128)(2,1)} copy-done((bf16[16,288,192]{2,1,0:T(8,128)(2,1)}, bf16[16,288,192]{2,1,0:T(8,128)(2,1)S(1)}, u32[]{:S(2)}) %copy-start) | copy-done | bytes 1769496
  89.6 2.5 %collective-permute-done.10.refs_0_ = bf16[64,2048]{1,0:T(8,128)(2,1)S(1)} collective-permute-done((bf16[64,2048]{1,0:T(8,128)(2,1)S(1)}, bf16[64,2048]{1,0:T(8,128)(2,1)S(1)}, u32[]{:S(2)}, u32[]{:S(2)}) %collective-permute-start.10) | collective-permute-done | bytes 262176 | tf_op jit(solution)/shard_map/ppermute | solution.py:489
  92.0 0.7 copy-done.18
  92.7 0.0 collective-permute-start.15
  92.7 0.0 collective-permute-done.12.refs_5_
  92.7 0.0 collective-permute-done.13.refs_6_
  92.8 0.0 collective-permute-done.14.refs_7_
  92.8 0.0 collective-permute-done.16.refs_9_
  92.8 1.7 %collective-permute-done.15.refs_8_ = bf16[64,2048]{1,0:T(8,128)(2,1)S(1)} collective-permute-done((bf16[64,2048]{1,0:T(8,128)(2,1)}, bf16[64,2048]{1,0:T(8,128)(2,1)S(1)}, u32[]{:S(2)}, u32[]{:S(2)}) %collective-permute-start.15) | collective-permute-done | bytes 262176 | tf_op jit(solution)/shard_map/ppermute | solution.py:489
  94.5 0.7 copy-done.21
  95.2 24.5 %shard_map.75 = (bf16[16,192,2048]{2,1,0:T(8,128)(2,1)}, f32[16,18,128]{2,1,0:T(8,128)}) custom-call(s32[2]{0:T(128)} %copy-done.16, s32[16,8,128]{2,1,0:T(8,128)} %copy-done.12, bf16[16,192,2048]{2,1,0:T(8,128)(2,1)} %weights.3, bf16[16,288,192]{2,1,0:T(8,128)(2,1)} %copy-done, f32[16,144,192]{2,1,0:T(8,128)} %copy-done.1, ...), custom_call_target="tpu_custom_call" | custom-call | flops 12079595520 | bytes 25165824 | tf_op jit(solution)/shard_map/pallas_call | solution.py:396
  119.7 13.7 %all_to_all.15.returned = f32[16,18,128]{2,1,0:T(8,128)S(1)} all-to-all(f32[16,18,128]{2,1,0:T(8,128)} %get-tuple-element.13), channel_id=1, replica_groups=mesh['groups'=2,'expert'=4,'dp'=4] {'expert','dp'}, dimensions={0} | all-to-all | bytes 294912 | tf_op jit(solution)/shard_map/all_to_all | solution.py:504
  133.3 1.0 shard_map.76
  (35 shorter events, 0.1 us)
Async XLA Ops:
  0.6 9.0 %collective-permute-start = (bf16[128,2048]{1,0:T(8,128)(2,1)}, bf16[128,2048]{1,0:T(8,128)(2,1)S(1)}, u32[]{:S(2)}, u32[]{:S(2)}) collective-permute-start(bf16[128,2048]{1,0:T(8,128)(2,1)} %refs_0_.1), channel_id=1, source_target_pairs={{0,1},{1,0},{2,3},{3,2},{4,5},{5,4},{6,7},{7,6},{8,9},{9,8},{10,11... | collective-permute-start | bytes 1572872 | tf_op jit(solution)/shard_map/ppermute | solution.py:489
  1.1 18.6 %collective-permute-start.2 = (bf16[128,2048]{1,0:T(8,128)(2,1)}, bf16[128,2048]{1,0:T(8,128)(2,1)S(1)}, u32[]{:S(2)}, u32[]{:S(2)}) collective-permute-start(bf16[128,2048]{1,0:T(8,128)(2,1)} %refs_0_.1), channel_id=1, source_target_pairs={{0,2},{1,3},{2,0},{3,1},{4,6},{5,7},{6,4},{7,5},{8,10},{9,11},{10,... | collective-permute-start | bytes 1572872 | tf_op jit(solution)/shard_map/ppermute | solution.py:489
  3.7 25.5 %collective-permute-start.1 = (bf16[128,2048]{1,0:T(8,128)(2,1)}, bf16[128,2048]{1,0:T(8,128)(2,1)S(1)}, u32[]{:S(2)}, u32[]{:S(2)}) collective-permute-start(bf16[128,2048]{1,0:T(8,128)(2,1)} %refs_0_.1), channel_id=1, source_target_pairs={{0,4},{4,0},{8,12},{12,8},{1,5},{5,1},{9,13},{13,9},{2,6},{6,2},{1... | collective-permute-start | bytes 1572872 | tf_op jit(solution)/shard_map/ppermute | solution.py:489
  5.3 26.7 %collective-permute-start.3 = (bf16[128,2048]{1,0:T(8,128)(2,1)}, bf16[128,2048]{1,0:T(8,128)(2,1)S(1)}, u32[]{:S(2)}, u32[]{:S(2)}) collective-permute-start(bf16[128,2048]{1,0:T(8,128)(2,1)} %refs_0_.1), channel_id=1, source_target_pairs={{0,8},{4,12},{8,0},{12,4},{1,9},{5,13},{9,1},{13,5},{2,10},{6,14},... | collective-permute-start | bytes 1572872 | tf_op jit(solution)/shard_map/ppermute | solution.py:489
  9.7 5.4 %copy-start.10 = (bf16[128,2048]{1,0:T(8,128)(2,1)}, bf16[128,2048]{1,0:T(8,128)(2,1)S(1)}, u32[]{:S(2)}) copy-start(bf16[128,2048]{1,0:T(8,128)(2,1)S(1)} %collective-permute-done.early.refs_4_) | copy-start | bytes 1572868
  9.7 0.7 copy-start.13
  10.4 1.4 %copy-start.17 = (bf16[128,8,768]{2,1,0:T(8,128)(2,1)S(1)}, bf16[128,8,768]{2,1,0:T(8,128)(2,1)}, u32[]{:S(2)}) copy-start(bf16[128,8,768]{2,1,0:T(8,128)(2,1)} %param.7) | copy-start | bytes 4718596
  15.1 1.2 copy-start.2
  16.3 16.5 %all-to-all-start = ((s32[16,8,128]{2,1,0:T(8,128)}), s32[16,8,128]{2,1,0:T(8,128)S(1)}, u32[]{:S(2)}, u32[]{:S(2)}) async-start(s32[16,8,128]{2,1,0:T(8,128)} %get-tuple-element.8), calls=%async_computation | async-start | bytes 131072 | tf_op jit(solution)/shard_map/all_to_all | solution.py:504
  19.8 12.2 %copy-start.7 = (bf16[128,2048]{1,0:T(8,128)(2,1)}, bf16[128,2048]{1,0:T(8,128)(2,1)S(1)}, u32[]{:S(2)}) copy-start(bf16[128,2048]{1,0:T(8,128)(2,1)S(1)} %collective-permute-done.2.refs_2_) | copy-start | bytes 1572868
  29.2 2.8 %copy-start.5 = (bf16[128,2048]{1,0:T(8,128)(2,1)}, bf16[128,2048]{1,0:T(8,128)(2,1)S(1)}, u32[]{:S(2)}) copy-start(bf16[128,2048]{1,0:T(8,128)(2,1)S(1)} %collective-permute-done.1.refs_1_) | copy-start | bytes 1572868
  32.0 0.8 copy-start.3
  32.8 4.7 %copy-start.8 = (bf16[128,2048]{1,0:T(8,128)(2,1)S(1)}, bf16[128,2048]{1,0:T(8,128)(2,1)}, u32[]{:S(2)}) copy-start(bf16[128,2048]{1,0:T(8,128)(2,1)} %copy-done.7) | copy-start | bytes 1572868
  32.8 5.2 %copy-start.6 = (bf16[128,2048]{1,0:T(8,128)(2,1)S(1)}, bf16[128,2048]{1,0:T(8,128)(2,1)}, u32[]{:S(2)}) copy-start(bf16[128,2048]{1,0:T(8,128)(2,1)} %copy-done.5) | copy-start | bytes 1572868
  32.8 5.3 %copy-start.4 = (bf16[128,2048]{1,0:T(8,128)(2,1)S(1)}, bf16[128,2048]{1,0:T(8,128)(2,1)}, u32[]{:S(2)}) copy-start(bf16[128,2048]{1,0:T(8,128)(2,1)} %copy-done.3) | copy-start | bytes 1572868
  32.8 26.6 %copy-start.12 = (s32[16,8,128]{2,1,0:T(8,128)}, s32[16,8,128]{2,1,0:T(8,128)S(1)}, u32[]{:S(2)}) copy-start(s32[16,8,128]{2,1,0:T(8,128)S(1)} %all-to-all-done.routes_t) | copy-start | bytes 196612
  32.9 53.3 %all-to-all-start.1 = ((bf16[16,144,384]{2,1,0:T(8,128)(2,1)}), bf16[16,144,384]{2,1,0:T(8,128)(2,1)S(1)}, u32[]{:S(2)}, u32[]{:S(2)}) async-start(bf16[16,144,384]{2,1,0:T(8,128)(2,1)} %shard_map.69), calls=%async_computation.1 | async-start | bytes 3538944 | tf_op jit(solution)/shard_map/all_to_all | solution.py:504
  37.5 3.0 %collective-permute-start.5 = (bf16[128,2048]{1,0:T(8,128)(2,1)S(1)}, bf16[128,2048]{1,0:T(8,128)(2,1)}, u32[]{:S(2)}, u32[]{:S(2)}) collective-permute-start(bf16[128,2048]{1,0:T(8,128)(2,1)S(1)} %copy-done.8), channel_id=1, source_target_pairs={{0,1},{1,0},{2,3},{3,2},{4,5},{5,4},{6,7},{7,6},{8,9},{9,8},{10,11... | collective-permute-start | bytes 1572872 | tf_op jit(solution)/shard_map/ppermute | solution.py:489
  38.0 4.3 %collective-permute-start.4 = (bf16[128,2048]{1,0:T(8,128)(2,1)S(1)}, bf16[128,2048]{1,0:T(8,128)(2,1)}, u32[]{:S(2)}, u32[]{:S(2)}) collective-permute-start(bf16[128,2048]{1,0:T(8,128)(2,1)S(1)} %copy-done.6), channel_id=1, source_target_pairs={{0,1},{1,0},{2,3},{3,2},{4,5},{5,4},{6,7},{7,6},{8,9},{9,8},{10,11... | collective-permute-start | bytes 1572872 | tf_op jit(solution)/shard_map/ppermute | solution.py:489
  38.1 4.2 %collective-permute-start.6 = (bf16[128,2048]{1,0:T(8,128)(2,1)S(1)}, bf16[128,2048]{1,0:T(8,128)(2,1)}, u32[]{:S(2)}, u32[]{:S(2)}) collective-permute-start(bf16[128,2048]{1,0:T(8,128)(2,1)S(1)} %copy-done.4), channel_id=1, source_target_pairs={{0,1},{1,0},{2,3},{3,2},{4,5},{5,4},{6,7},{7,6},{8,9},{9,8},{10,11... | collective-permute-start | bytes 1572872 | tf_op jit(solution)/shard_map/ppermute | solution.py:489
  38.5 28.2 %collective-permute-start.8 = (bf16[128,2048]{1,0:T(8,128)(2,1)S(1)}, bf16[128,2048]{1,0:T(8,128)(2,1)}, u32[]{:S(2)}, u32[]{:S(2)}) collective-permute-start(bf16[128,2048]{1,0:T(8,128)(2,1)S(1)} %copy-done.4), channel_id=1, source_target_pairs={{0,2},{1,3},{2,0},{3,1},{4,6},{5,7},{6,4},{7,5},{8,10},{9,11},{10,... | collective-permute-start | bytes 1572872 | tf_op jit(solution)/shard_map/ppermute | solution.py:489
  40.2 42.0 %collective-permute-start.7 = (bf16[128,2048]{1,0:T(8,128)(2,1)S(1)}, bf16[128,2048]{1,0:T(8,128)(2,1)}, u32[]{:S(2)}, u32[]{:S(2)}) collective-permute-start(bf16[128,2048]{1,0:T(8,128)(2,1)S(1)} %copy-done.6), channel_id=1, source_target_pairs={{0,2},{1,3},{2,0},{3,1},{4,6},{5,7},{6,4},{7,5},{8,10},{9,11},{10,... | collective-permute-start | bytes 1572872 | tf_op jit(solution)/shard_map/ppermute | solution.py:489
  40.5 41.6 %collective-permute-start.9 = (bf16[128,2048]{1,0:T(8,128)(2,1)S(1)}, bf16[128,2048]{1,0:T(8,128)(2,1)}, u32[]{:S(2)}, u32[]{:S(2)}) collective-permute-start(bf16[128,2048]{1,0:T(8,128)(2,1)S(1)} %copy-done.4), channel_id=1, source_target_pairs={{0,4},{4,0},{8,12},{12,8},{1,5},{5,1},{9,13},{13,9},{2,6},{6,2},{1... | collective-permute-start | bytes 1572872 | tf_op jit(solution)/shard_map/ppermute | solution.py:489
  42.3 43.8 %copy-start.16 = (s32[2]{0:T(128)}, s32[2]{0:T(128)S(1)}, u32[]{:S(2)}) copy-start(s32[2]{0:T(128)S(1)} %pad_add_fusion.place) | copy-start | bytes 28
  42.3 1.0 copy-start.9
  43.4 1.0 copy-start.11
  59.4 1.4 %copy-start.1 = (f32[16,144,192]{2,1,0:T(8,128)}, f32[16,144,192]{2,1,0:T(8,128)S(1)}, u32[]{:S(2)}) copy-start(f32[16,144,192]{2,1,0:T(8,128)S(1)} %get-tuple-element.10.refs_1_.backs) | copy-start | bytes 5308420
  67.7 18.5 %collective-permute-start.11 = (bf16[64,2048]{1,0:T(8,128)(2,1)S(1)}, bf16[64,2048]{1,0:T(8,128)(2,1)}, u32[]{:S(2)}, u32[]{:S(2)}) collective-permute-start(bf16[64,2048]{1,0:T(8,128)(2,1)S(1)} %slice.9), channel_id=1, source_target_pairs={{0,4},{4,0},{8,12},{12,8},{1,5},{5,1},{9,13},{13,9},{2,6},{6,2},{1... | collective-permute-start | bytes 786440 | tf_op jit(solution)/shard_map/ppermute | solution.py:489
  69.2 23.6 %collective-permute-start.13 = (bf16[128,2048]{1,0:T(8,128)(2,1)}, bf16[128,2048]{1,0:T(8,128)(2,1)}, u32[]{:S(2)}, u32[]{:S(2)}) collective-permute-start(bf16[128,2048]{1,0:T(8,128)(2,1)} %shard_map.72.refs_1_), channel_id=1, source_target_pairs={{0,1},{1,0},{2,3},{3,2},{4,5},{5,4},{6,7},{7,6},{8,9},{9,8},{10,11... | collective-permute-start | bytes 1572872 | tf_op jit(solution)/shard_map/ppermute | solution.py:489
  82.2 10.6 %collective-permute-start.12 = (bf16[128,2048]{1,0:T(8,128)(2,1)}, bf16[128,2048]{1,0:T(8,128)(2,1)S(1)}, u32[]{:S(2)}, u32[]{:S(2)}) collective-permute-start(bf16[128,2048]{1,0:T(8,128)(2,1)} %collective-permute-done.7.refs_0_), channel_id=1, source_target_pairs={{0,1},{1,0},{2,3},{3,2},{4,5},{5,4},{6,7},{7,6},{8,9},{9,8},{10,11... | collective-permute-start | bytes 1572872 | tf_op jit(solution)/shard_map/ppermute | solution.py:489
  83.2 9.6 %collective-permute-start.14 = (bf16[128,2048]{1,0:T(8,128)(2,1)}, bf16[128,2048]{1,0:T(8,128)(2,1)}, u32[]{:S(2)}, u32[]{:S(2)}) collective-permute-start(bf16[128,2048]{1,0:T(8,128)(2,1)} %shard_map.73.refs_2_), channel_id=1, source_target_pairs={{0,1},{1,0},{2,3},{3,2},{4,5},{5,4},{6,7},{7,6},{8,9},{9,8},{10,11... | collective-permute-start | bytes 1572872 | tf_op jit(solution)/shard_map/ppermute | solution.py:489
  83.7 8.3 %collective-permute-start.10 = (bf16[64,2048]{1,0:T(8,128)(2,1)S(1)}, bf16[64,2048]{1,0:T(8,128)(2,1)S(1)}, u32[]{:S(2)}, u32[]{:S(2)}) collective-permute-start(bf16[64,2048]{1,0:T(8,128)(2,1)S(1)} %slice.8), channel_id=1, source_target_pairs={{0,2},{1,3},{2,0},{3,1},{4,6},{5,7},{6,4},{7,5},{8,10},{9,11},{10,... | collective-permute-start | bytes 786440 | tf_op jit(solution)/shard_map/ppermute | solution.py:489
  86.1 6.6 %collective-permute-start.16 = (bf16[64,2048]{1,0:T(8,128)(2,1)}, bf16[64,2048]{1,0:T(8,128)(2,1)S(1)}, u32[]{:S(2)}, u32[]{:S(2)}) collective-permute-start(bf16[64,2048]{1,0:T(8,128)(2,1)} %collective-permute-done.11.refs_4_), channel_id=1, source_target_pairs={{0,1},{1,0},{2,3},{3,2},{4,5},{5,4},{6,7},{7,6},{8,9},{9,8},{10,11... | collective-permute-start | bytes 786440 | tf_op jit(solution)/shard_map/ppermute | solution.py:489
  88.1 1.4 %copy-start = (bf16[16,288,192]{2,1,0:T(8,128)(2,1)}, bf16[16,288,192]{2,1,0:T(8,128)(2,1)S(1)}, u32[]{:S(2)}) copy-start(bf16[16,288,192]{2,1,0:T(8,128)(2,1)S(1)} %shard_map.70.refs_1_.hidden) | copy-start | bytes 5308420
  92.0 0.7 copy-start.18
  92.7 1.7 %collective-permute-start.15 = (bf16[64,2048]{1,0:T(8,128)(2,1)}, bf16[64,2048]{1,0:T(8,128)(2,1)S(1)}, u32[]{:S(2)}, u32[]{:S(2)}) collective-permute-start(bf16[64,2048]{1,0:T(8,128)(2,1)} %shard_map.74.refs_3_), channel_id=1, source_target_pairs={{0,1},{1,0},{2,3},{3,2},{4,5},{5,4},{6,7},{7,6},{8,9},{9,8},{10,11... | collective-permute-start | bytes 786440 | tf_op jit(solution)/shard_map/ppermute | solution.py:489
  92.7 1.7 %copy-start.19 = (bf16[128,2048]{1,0:T(8,128)(2,1)}, bf16[128,2048]{1,0:T(8,128)(2,1)S(1)}, u32[]{:S(2)}) copy-start(bf16[128,2048]{1,0:T(8,128)(2,1)S(1)} %collective-permute-done.12.refs_5_) | copy-start | bytes 1572868
  92.8 1.7 %copy-start.20 = (bf16[64,2048]{1,0:T(8,128)(2,1)}, bf16[64,2048]{1,0:T(8,128)(2,1)S(1)}, u32[]{:S(2)}) copy-start(bf16[64,2048]{1,0:T(8,128)(2,1)S(1)} %collective-permute-done.16.refs_9_) | copy-start | bytes 786436
  94.5 0.7 copy-start.21
  95.2 38.1 %copy-start.14 = (s32[128,8]{0,1:T(8,128)S(1)}, s32[128,8]{0,1:T(8,128)}, u32[]{:S(2)}) copy-start(s32[128,8]{0,1:T(8,128)} %param.5) | copy-start | bytes 12292
  95.2 38.1 %copy-start.15 = (bf16[128,8]{0,1:T(8,128)(2,1)S(1)}, bf16[128,8]{0,1:T(8,128)(2,1)}, u32[]{:S(2)}) copy-start(bf16[128,8]{0,1:T(8,128)(2,1)} %param.6) | copy-start | bytes 6148

commit v8 on v7

--- a/solution.py
+++ b/solution.py
@@ -350,7 +350,7 @@
     step = pl.program_id(0)
     tall = SUPER * MOST
     width = out.shape[2]
-    columns = min(512, width)
+    columns = min(1024, width)
 
     @pl.when(step == 0)
     def _():

time: 135 us -> 135 us (level)
  no operation moved by 1% of the time
where the time goes in v8:
time: 135 us; the launch traced here: 134 us
  Pallas kernels  45.6 us (34%)
  waiting for transfers between devices  37.3 us (28%)
  starting transfers between devices  22.5 us (17%)
  local copies, waits for them, and re-layouts  14.2 us (11%)
  blocking collectives  13.7 us (10%)
    ppermute x17, waiting for transfers between devices, hop(): return lax.ppermute(block, axis, [(i, i ^ flip) for i in range(size)])  37.3 us
    pallas_call x1, Pallas kernels, gradients(): pl.pallas_call(functools.partial(gradients_kernel, orders), grid=(ex_loca...  24.4 us
    pallas_call x1, Pallas kernels, early_products(): pl.pallas_call(functools.partial(early_kernel, order), grid=(ex_local //...  15 us
    ppermute x17, starting transfers between devices, hop(): return lax.ppermute(block, axis, [(i, i ^ flip) for i in range(size)])  14.4 us
    all_to_all x1, blocking collectives, body(): lax.all_to_all(x, GROUP, split_axis=0, concat_axis=0, tiled=True)  13.7 us
    unnamed x46, local copies, waits for them, and re-layouts  12.1 us
    all_to_all x2, starting transfers between devices, body(): lax.all_to_all(x, GROUP, split_axis=0, concat_axis=0, tiled=True)  8.14 us
    pallas_call x1, Pallas kernels, pack(): pl.pallas_call(functools.partial(pack_kernel, n_dp, half), grid=(n_expert...  3.27 us
  transfers between devices with their start and end apart: 19, of which 7 were waited for; matrix products, arithmetic and copies ran while one was open for 3% of the time, Pallas kernels for 15%

profile of v8, /device:TPU:0, one launch (start us, length us, event | category | flops | bytes accessed | tf_op | source)
XLA Modules:
  0.0 134.2 jit_solution(17599972033811369935)
XLA Ops:
  0.6 0.5 collective-permute-start
  1.1 2.6 %collective-permute-start.2 = (bf16[128,2048]{1,0:T(8,128)(2,1)}, bf16[128,2048]{1,0:T(8,128)(2,1)S(1)}, u32[]{:S(2)}, u32[]{:S(2)}) collective-permute-start(bf16[128,2048]{1,0:T(8,128)(2,1)} %refs_0_.1), channel_id=1, source_target_pairs={{0,2},{1,3},{2,0},{3,1},{4,6},{5,7},{6,4},{7,5},{8,10},{9,11},{10,... | collective-permute-start | bytes 1572872 | tf_op jit(solution)/shard_map/ppermute | solution.py:489
  3.7 1.6 %collective-permute-start.1 = (bf16[128,2048]{1,0:T(8,128)(2,1)}, bf16[128,2048]{1,0:T(8,128)(2,1)S(1)}, u32[]{:S(2)}, u32[]{:S(2)}) collective-permute-start(bf16[128,2048]{1,0:T(8,128)(2,1)} %refs_0_.1), channel_id=1, source_target_pairs={{0,4},{4,0},{8,12},{12,8},{1,5},{5,1},{9,13},{13,9},{2,6},{6,2},{1... | collective-permute-start | bytes 1572872 | tf_op jit(solution)/shard_map/ppermute | solution.py:489
  5.3 2.6 %collective-permute-start.3 = (bf16[128,2048]{1,0:T(8,128)(2,1)}, bf16[128,2048]{1,0:T(8,128)(2,1)S(1)}, u32[]{:S(2)}, u32[]{:S(2)}) collective-permute-start(bf16[128,2048]{1,0:T(8,128)(2,1)} %refs_0_.1), channel_id=1, source_target_pairs={{0,8},{4,12},{8,0},{12,4},{1,9},{5,13},{9,1},{13,5},{2,10},{6,14},... | collective-permute-start | bytes 1572872 | tf_op jit(solution)/shard_map/ppermute | solution.py:489
  7.9 0.8 copy.14
  8.7 0.1 reshape.14.weights_flat
  8.8 0.8 copy.13
  9.6 0.1 reshape.13.routes_flat
  9.7 0.0 collective-permute-done.early.refs_4_
  9.7 0.0 copy-start.13
  9.7 0.7 copy-done.13
  10.4 1.4 %copy-done.17 = bf16[128,8,768]{2,1,0:T(8,128)(2,1)S(1)} copy-done((bf16[128,8,768]{2,1,0:T(8,128)(2,1)S(1)}, bf16[128,8,768]{2,1,0:T(8,128)(2,1)}, u32[]{:S(2)}) %copy-start.17) | copy-done | bytes 1572888
  11.8 3.3 %shard_map.68 = (bf16[16,144,384]{2,1,0:T(8,128)(2,1)S(1)}, s32[16,8,128]{2,1,0:T(8,128)}) custom-call(s32[8,128]{1,0:T(8,128)S(1)} %bitcast.6, s32[1,1024]{1,0:T(1,128)S(1)} %reshape.13.routes_flat, bf16[1,1024]{1,0:T(2,128)(2,1)S(1)} %reshape.14.weights_flat, bf16[1024,768]{1,0:T(8,128)(2,1)S(1)} %bitcast.9, ...), custom_call_target="tpu_custom_call" | custom-call | flops 1811939328 | bytes 4718592 | tf_op jit(solution)/shard_map/pallas_call | solution.py:83
  15.1 1.2 copy-done.2
  16.3 3.5 %all-to-all-start = ((s32[16,8,128]{2,1,0:T(8,128)}), s32[16,8,128]{2,1,0:T(8,128)S(1)}, u32[]{:S(2)}, u32[]{:S(2)}) async-start(s32[16,8,128]{2,1,0:T(8,128)} %get-tuple-element.8), calls=%async_computation | async-start | bytes 131072 | tf_op jit(solution)/shard_map/all_to_all | solution.py:504
  19.8 0.0 collective-permute-done.2.refs_2_
  19.8 0.0 copy-start.7
  19.8 9.4 %collective-permute-done.1.refs_1_ = bf16[128,2048]{1,0:T(8,128)(2,1)S(1)} collective-permute-done((bf16[128,2048]{1,0:T(8,128)(2,1)}, bf16[128,2048]{1,0:T(8,128)(2,1)S(1)}, u32[]{:S(2)}, u32[]{:S(2)}) %collective-permute-start.1) | collective-permute-done | bytes 524320 | tf_op jit(solution)/shard_map/ppermute | solution.py:489
  29.2 2.8 %collective-permute-done.3.refs_3_ = bf16[128,2048]{1,0:T(8,128)(2,1)S(1)} collective-permute-done((bf16[128,2048]{1,0:T(8,128)(2,1)}, bf16[128,2048]{1,0:T(8,128)(2,1)S(1)}, u32[]{:S(2)}, u32[]{:S(2)}) %collective-permute-start.3) | collective-permute-done | bytes 524320 | tf_op jit(solution)/shard_map/ppermute | solution.py:489
  32.0 0.8 copy-done.3
  32.8 0.0 all-to-all-done.routes_t
  32.9 4.7 %all-to-all-start.1 = ((bf16[16,144,384]{2,1,0:T(8,128)(2,1)}), bf16[16,144,384]{2,1,0:T(8,128)(2,1)S(1)}, u32[]{:S(2)}, u32[]{:S(2)}) async-start(bf16[16,144,384]{2,1,0:T(8,128)(2,1)} %shard_map.69), calls=%async_computation.1 | async-start | bytes 3538944 | tf_op jit(solution)/shard_map/all_to_all | solution.py:504
  37.5 0.5 collective-permute-start.5
  38.0 0.1 collective-permute-start.4
  38.1 0.4 collective-permute-start.6
  38.5 1.7 %collective-permute-start.8 = (bf16[128,2048]{1,0:T(8,128)(2,1)S(1)}, bf16[128,2048]{1,0:T(8,128)(2,1)}, u32[]{:S(2)}, u32[]{:S(2)}) collective-permute-start(bf16[128,2048]{1,0:T(8,128)(2,1)S(1)} %copy-done.4), channel_id=1, source_target_pairs={{0,2},{1,3},{2,0},{3,1},{4,6},{5,7},{6,4},{7,5},{8,10},{9,11},{10,... | collective-permute-start | bytes 1572872 | tf_op jit(solution)/shard_map/ppermute | solution.py:489
  40.2 0.3 collective-permute-start.7
  40.5 0.0 collective-permute-done.5.refs_6_
  40.5 1.7 %collective-permute-start.9 = (bf16[128,2048]{1,0:T(8,128)(2,1)S(1)}, bf16[128,2048]{1,0:T(8,128)(2,1)}, u32[]{:S(2)}, u32[]{:S(2)}) collective-permute-start(bf16[128,2048]{1,0:T(8,128)(2,1)S(1)} %copy-done.4), channel_id=1, source_target_pairs={{0,4},{4,0},{8,12},{12,8},{1,5},{5,1},{9,13},{13,9},{2,6},{6,2},{1... | collective-permute-start | bytes 1572872 | tf_op jit(solution)/shard_map/ppermute | solution.py:489
  42.2 0.1 pad_add_fusion.place
  42.3 0.0 collective-permute-done.4.refs_5_
  42.3 0.0 collective-permute-done.6.refs_7_
  42.3 0.0 copy-start.9
  42.3 1.0 copy-done.9
  43.4 1.0 copy-done.11
  44.4 15.0 %shard_map.71 = (f32[16,144,192]{2,1,0:T(8,128)S(1)}, bf16[16,144,2048]{2,1,0:T(8,128)(2,1)}) custom-call(s32[2]{0:T(128)S(1)} %pad_add_fusion.place, s32[16,8,128]{2,1,0:T(8,128)S(1)} %all-to-all-done.routes_t, bf16[16,192,2048]{2,1,0:T(8,128)(2,1)} %weights.3, bf16[128,2048]{1,0:T(8,128)(2,1)S(1)} %copy-done.9, bf16[128,2048]{1,0:T(8,128)(2,1)S(1)} %copy-done.6, ...), custom_call_target="tpu_custom_call" | custom-call | flops 4227858432 | bytes 12582912 | tf_op jit(solution)/shard_map/pallas_call | solution.py:323
  59.4 1.4 %copy-done.1 = f32[16,144,192]{2,1,0:T(8,128)} copy-done((f32[16,144,192]{2,1,0:T(8,128)}, f32[16,144,192]{2,1,0:T(8,128)S(1)}, u32[]{:S(2)}) %copy-start.1) | copy-done | bytes 1769496
  60.8 5.9 %collective-permute-done.8.refs_0_ = bf16[128,2048]{1,0:T(8,128)(2,1)} collective-permute-done((bf16[128,2048]{1,0:T(8,128)(2,1)S(1)}, bf16[128,2048]{1,0:T(8,128)(2,1)}, u32[]{:S(2)}, u32[]{:S(2)}) %collective-permute-start.8) | collective-permute-done | bytes 524320 | tf_op jit(solution)/shard_map/ppermute | solution.py:489
  66.7 1.0 slice.9
  67.7 1.5 %collective-permute-start.11 = (bf16[64,2048]{1,0:T(8,128)(2,1)S(1)}, bf16[64,2048]{1,0:T(8,128)(2,1)}, u32[]{:S(2)}, u32[]{:S(2)}) collective-permute-start(bf16[64,2048]{1,0:T(8,128)(2,1)S(1)} %slice.9), channel_id=1, source_target_pairs={{0,4},{4,0},{8,12},{12,8},{1,5},{5,1},{9,13},{13,9},{2,6},{6,2},{1... | collective-permute-start | bytes 786440 | tf_op jit(solution)/shard_map/ppermute | solution.py:489
  69.2 0.0 collective-permute-start.13
  69.2 13.0 %collective-permute-done.7.refs_0_ = bf16[128,2048]{1,0:T(8,128)(2,1)} collective-permute-done((bf16[128,2048]{1,0:T(8,128)(2,1)S(1)}, bf16[128,2048]{1,0:T(8,128)(2,1)}, u32[]{:S(2)}, u32[]{:S(2)}) %collective-permute-start.7) | collective-permute-done | bytes 524320 | tf_op jit(solution)/shard_map/ppermute | solution.py:489
  82.2 0.0 collective-permute-start.12
  82.2 0.0 collective-permute-done.9.refs_0_
  82.2 1.0 slice.8
  83.2 0.6 collective-permute-start.14
  83.7 0.4 collective-permute-start.10
  84.1 2.0 %collective-permute-done.11.refs_4_ = bf16[64,2048]{1,0:T(8,128)(2,1)} collective-permute-done((bf16[64,2048]{1,0:T(8,128)(2,1)S(1)}, bf16[64,2048]{1,0:T(8,128)(2,1)}, u32[]{:S(2)}, u32[]{:S(2)}) %collective-permute-start.11) | collective-permute-done | bytes 262176 | tf_op jit(solution)/shard_map/ppermute | solution.py:489
  86.1 0.0 collective-permute-start.16
  86.1 0.0 all-to-all-done.1.received
  86.1 2.0 %shard_map.70.refs_1_.hidden = bf16[16,288,192]{2,1,0:T(8,128)(2,1)S(1)} custom-call(s32[2]{0:T(128)S(1)} %pad_add_fusion.place, bf16[16,144,384]{2,1,0:T(8,128)(2,1)S(1)} %all-to-all-done.1.received), custom_call_target="tpu_custom_call" | custom-call | flops 1019215872 | bytes 4194304 | tf_op jit(solution)/shard_map/pallas_call | solution.py:245
  88.1 1.4 %copy-done = bf16[16,288,192]{2,1,0:T(8,128)(2,1)} copy-done((bf16[16,288,192]{2,1,0:T(8,128)(2,1)}, bf16[16,288,192]{2,1,0:T(8,128)(2,1)S(1)}, u32[]{:S(2)}) %copy-start) | copy-done | bytes 1769496
  89.6 2.5 %collective-permute-done.10.refs_0_ = bf16[64,2048]{1,0:T(8,128)(2,1)S(1)} collective-permute-done((bf16[64,2048]{1,0:T(8,128)(2,1)S(1)}, bf16[64,2048]{1,0:T(8,128)(2,1)S(1)}, u32[]{:S(2)}, u32[]{:S(2)}) %collective-permute-start.10) | collective-permute-done | bytes 262176 | tf_op jit(solution)/shard_map/ppermute | solution.py:489
  92.0 0.7 copy-done.18
  92.7 0.0 collective-permute-start.15
  92.7 0.0 collective-permute-done.12.refs_5_
  92.7 0.0 collective-permute-done.13.refs_6_
  92.8 0.0 collective-permute-done.14.refs_7_
  92.8 0.0 collective-permute-done.16.refs_9_
  92.8 1.7 %collective-permute-done.15.refs_8_ = bf16[64,2048]{1,0:T(8,128)(2,1)S(1)} collective-permute-done((bf16[64,2048]{1,0:T(8,128)(2,1)}, bf16[64,2048]{1,0:T(8,128)(2,1)S(1)}, u32[]{:S(2)}, u32[]{:S(2)}) %collective-permute-start.15) | collective-permute-done | bytes 262176 | tf_op jit(solution)/shard_map/ppermute | solution.py:489
  94.5 0.7 copy-done.21
  95.2 24.4 %shard_map.75 = (bf16[16,192,2048]{2,1,0:T(8,128)(2,1)}, f32[16,18,128]{2,1,0:T(8,128)}) custom-call(s32[2]{0:T(128)} %copy-done.16, s32[16,8,128]{2,1,0:T(8,128)} %copy-done.12, bf16[16,192,2048]{2,1,0:T(8,128)(2,1)} %weights.3, bf16[16,288,192]{2,1,0:T(8,128)(2,1)} %copy-done, f32[16,144,192]{2,1,0:T(8,128)} %copy-done.1, ...), custom_call_target="tpu_custom_call" | custom-call | flops 12079595520 | bytes 25165824 | tf_op jit(solution)/shard_map/pallas_call | solution.py:396
  119.6 13.7 %all_to_all.15.returned = f32[16,18,128]{2,1,0:T(8,128)S(1)} all-to-all(f32[16,18,128]{2,1,0:T(8,128)} %get-tuple-element.13), channel_id=1, replica_groups=mesh['groups'=2,'expert'=4,'dp'=4] {'expert','dp'}, dimensions={0} | all-to-all | bytes 294912 | tf_op jit(solution)/shard_map/all_to_all | solution.py:504
  133.2 1.0 shard_map.76
  (35 shorter events, 0.1 us)
Async XLA Ops:
  0.6 9.0 %collective-permute-start = (bf16[128,2048]{1,0:T(8,128)(2,1)}, bf16[128,2048]{1,0:T(8,128)(2,1)S(1)}, u32[]{:S(2)}, u32[]{:S(2)}) collective-permute-start(bf16[128,2048]{1,0:T(8,128)(2,1)} %refs_0_.1), channel_id=1, source_target_pairs={{0,1},{1,0},{2,3},{3,2},{4,5},{5,4},{6,7},{7,6},{8,9},{9,8},{10,11... | collective-permute-start | bytes 1572872 | tf_op jit(solution)/shard_map/ppermute | solution.py:489
  1.1 18.6 %collective-permute-start.2 = (bf16[128,2048]{1,0:T(8,128)(2,1)}, bf16[128,2048]{1,0:T(8,128)(2,1)S(1)}, u32[]{:S(2)}, u32[]{:S(2)}) collective-permute-start(bf16[128,2048]{1,0:T(8,128)(2,1)} %refs_0_.1), channel_id=1, source_target_pairs={{0,2},{1,3},{2,0},{3,1},{4,6},{5,7},{6,4},{7,5},{8,10},{9,11},{10,... | collective-permute-start | bytes 1572872 | tf_op jit(solution)/shard_map/ppermute | solution.py:489
  3.7 25.5 %collective-permute-start.1 = (bf16[128,2048]{1,0:T(8,128)(2,1)}, bf16[128,2048]{1,0:T(8,128)(2,1)S(1)}, u32[]{:S(2)}, u32[]{:S(2)}) collective-permute-start(bf16[128,2048]{1,0:T(8,128)(2,1)} %refs_0_.1), channel_id=1, source_target_pairs={{0,4},{4,0},{8,12},{12,8},{1,5},{5,1},{9,13},{13,9},{2,6},{6,2},{1... | collective-permute-start | bytes 1572872 | tf_op jit(solution)/shard_map/ppermute | solution.py:489
  5.3 26.7 %collective-permute-start.3 = (bf16[128,2048]{1,0:T(8,128)(2,1)}, bf16[128,2048]{1,0:T(8,128)(2,1)S(1)}, u32[]{:S(2)}, u32[]{:S(2)}) collective-permute-start(bf16[128,2048]{1,0:T(8,128)(2,1)} %refs_0_.1), channel_id=1, source_target_pairs={{0,8},{4,12},{8,0},{12,4},{1,9},{5,13},{9,1},{13,5},{2,10},{6,14},... | collective-permute-start | bytes 1572872 | tf_op jit(solution)/shard_map/ppermute | solution.py:489
  9.7 5.4 %copy-start.10 = (bf16[128,2048]{1,0:T(8,128)(2,1)}, bf16[128,2048]{1,0:T(8,128)(2,1)S(1)}, u32[]{:S(2)}) copy-start(bf16[128,2048]{1,0:T(8,128)(2,1)S(1)} %collective-permute-done.early.refs_4_) | copy-start | bytes 1572868
  9.7 0.7 copy-start.13
  10.4 1.4 %copy-start.17 = (bf16[128,8,768]{2,1,0:T(8,128)(2,1)S(1)}, bf16[128,8,768]{2,1,0:T(8,128)(2,1)}, u32[]{:S(2)}) copy-start(bf16[128,8,768]{2,1,0:T(8,128)(2,1)} %param.7) | copy-start | bytes 4718596
  15.1 1.2 copy-start.2
  16.3 16.5 %all-to-all-start = ((s32[16,8,128]{2,1,0:T(8,128)}), s32[16,8,128]{2,1,0:T(8,128)S(1)}, u32[]{:S(2)}, u32[]{:S(2)}) async-start(s32[16,8,128]{2,1,0:T(8,128)} %get-tuple-element.8), calls=%async_computation | async-start | bytes 131072 | tf_op jit(solution)/shard_map/all_to_all | solution.py:504
  19.8 12.2 %copy-start.7 = (bf16[128,2048]{1,0:T(8,128)(2,1)}, bf16[128,2048]{1,0:T(8,128)(2,1)S(1)}, u32[]{:S(2)}) copy-start(bf16[128,2048]{1,0:T(8,128)(2,1)S(1)} %collective-permute-done.2.refs_2_) | copy-start | bytes 1572868
  29.2 2.8 %copy-start.5 = (bf16[128,2048]{1,0:T(8,128)(2,1)}, bf16[128,2048]{1,0:T(8,128)(2,1)S(1)}, u32[]{:S(2)}) copy-start(bf16[128,2048]{1,0:T(8,128)(2,1)S(1)} %collective-permute-done.1.refs_1_) | copy-start | bytes 1572868
  32.0 0.8 copy-start.3
  32.8 4.7 %copy-start.8 = (bf16[128,2048]{1,0:T(8,128)(2,1)S(1)}, bf16[128,2048]{1,0:T(8,128)(2,1)}, u32[]{:S(2)}) copy-start(bf16[128,2048]{1,0:T(8,128)(2,1)} %copy-done.7) | copy-start | bytes 1572868
  32.8 5.2 %copy-start.6 = (bf16[128,2048]{1,0:T(8,128)(2,1)S(1)}, bf16[128,2048]{1,0:T(8,128)(2,1)}, u32[]{:S(2)}) copy-start(bf16[128,2048]{1,0:T(8,128)(2,1)} %copy-done.5) | copy-start | bytes 1572868
  32.8 5.3 %copy-start.4 = (bf16[128,2048]{1,0:T(8,128)(2,1)S(1)}, bf16[128,2048]{1,0:T(8,128)(2,1)}, u32[]{:S(2)}) copy-start(bf16[128,2048]{1,0:T(8,128)(2,1)} %copy-done.3) | copy-start | bytes 1572868
  32.8 26.6 %copy-start.12 = (s32[16,8,128]{2,1,0:T(8,128)}, s32[16,8,128]{2,1,0:T(8,128)S(1)}, u32[]{:S(2)}) copy-start(s32[16,8,128]{2,1,0:T(8,128)S(1)} %all-to-all-done.routes_t) | copy-start | bytes 196612
  32.9 53.3 %all-to-all-start.1 = ((bf16[16,144,384]{2,1,0:T(8,128)(2,1)}), bf16[16,144,384]{2,1,0:T(8,128)(2,1)S(1)}, u32[]{:S(2)}, u32[]{:S(2)}) async-start(bf16[16,144,384]{2,1,0:T(8,128)(2,1)} %shard_map.69), calls=%async_computation.1 | async-start | bytes 3538944 | tf_op jit(solution)/shard_map/all_to_all | solution.py:504
  37.5 3.0 %collective-permute-start.5 = (bf16[128,2048]{1,0:T(8,128)(2,1)S(1)}, bf16[128,2048]{1,0:T(8,128)(2,1)}, u32[]{:S(2)}, u32[]{:S(2)}) collective-permute-start(bf16[128,2048]{1,0:T(8,128)(2,1)S(1)} %copy-done.8), channel_id=1, source_target_pairs={{0,1},{1,0},{2,3},{3,2},{4,5},{5,4},{6,7},{7,6},{8,9},{9,8},{10,11... | collective-permute-start | bytes 1572872 | tf_op jit(solution)/shard_map/ppermute | solution.py:489
  38.0 4.3 %collective-permute-start.4 = (bf16[128,2048]{1,0:T(8,128)(2,1)S(1)}, bf16[128,2048]{1,0:T(8,128)(2,1)}, u32[]{:S(2)}, u32[]{:S(2)}) collective-permute-start(bf16[128,2048]{1,0:T(8,128)(2,1)S(1)} %copy-done.6), channel_id=1, source_target_pairs={{0,1},{1,0},{2,3},{3,2},{4,5},{5,4},{6,7},{7,6},{8,9},{9,8},{10,11... | collective-permute-start | bytes 1572872 | tf_op jit(solution)/shard_map/ppermute | solution.py:489
  38.1 4.2 %collective-permute-start.6 = (bf16[128,2048]{1,0:T(8,128)(2,1)S(1)}, bf16[128,2048]{1,0:T(8,128)(2,1)}, u32[]{:S(2)}, u32[]{:S(2)}) collective-permute-start(bf16[128,2048]{1,0:T(8,128)(2,1)S(1)} %copy-done.4), channel_id=1, source_target_pairs={{0,1},{1,0},{2,3},{3,2},{4,5},{5,4},{6,7},{7,6},{8,9},{9,8},{10,11... | collective-permute-start | bytes 1572872 | tf_op jit(solution)/shard_map/ppermute | solution.py:489
  38.5 28.2 %collective-permute-start.8 = (bf16[128,2048]{1,0:T(8,128)(2,1)S(1)}, bf16[128,2048]{1,0:T(8,128)(2,1)}, u32[]{:S(2)}, u32[]{:S(2)}) collective-permute-start(bf16[128,2048]{1,0:T(8,128)(2,1)S(1)} %copy-done.4), channel_id=1, source_target_pairs={{0,2},{1,3},{2,0},{3,1},{4,6},{5,7},{6,4},{7,5},{8,10},{9,11},{10,... | collective-permute-start | bytes 1572872 | tf_op jit(solution)/shard_map/ppermute | solution.py:489
  40.2 42.0 %collective-permute-start.7 = (bf16[128,2048]{1,0:T(8,128)(2,1)S(1)}, bf16[128,2048]{1,0:T(8,128)(2,1)}, u32[]{:S(2)}, u32[]{:S(2)}) collective-permute-start(bf16[128,2048]{1,0:T(8,128)(2,1)S(1)} %copy-done.6), channel_id=1, source_target_pairs={{0,2},{1,3},{2,0},{3,1},{4,6},{5,7},{6,4},{7,5},{8,10},{9,11},{10,... | collective-permute-start | bytes 1572872 | tf_op jit(solution)/shard_map/ppermute | solution.py:489
  40.5 41.6 %collective-permute-start.9 = (bf16[128,2048]{1,0:T(8,128)(2,1)S(1)}, bf16[128,2048]{1,0:T(8,128)(2,1)}, u32[]{:S(2)}, u32[]{:S(2)}) collective-permute-start(bf16[128,2048]{1,0:T(8,128)(2,1)S(1)} %copy-done.4), channel_id=1, source_target_pairs={{0,4},{4,0},{8,12},{12,8},{1,5},{5,1},{9,13},{13,9},{2,6},{6,2},{1... | collective-permute-start | bytes 1572872 | tf_op jit(solution)/shard_map/ppermute | solution.py:489
  42.3 43.8 %copy-start.16 = (s32[2]{0:T(128)}, s32[2]{0:T(128)S(1)}, u32[]{:S(2)}) copy-start(s32[2]{0:T(128)S(1)} %pad_add_fusion.place) | copy-start | bytes 28
  42.3 1.0 copy-start.9
  43.4 1.0 copy-start.11
  59.4 1.4 %copy-start.1 = (f32[16,144,192]{2,1,0:T(8,128)}, f32[16,144,192]{2,1,0:T(8,128)S(1)}, u32[]{:S(2)}) copy-start(f32[16,144,192]{2,1,0:T(8,128)S(1)} %get-tuple-element.10.refs_1_.backs) | copy-start | bytes 5308420
  67.7 18.5 %collective-permute-start.11 = (bf16[64,2048]{1,0:T(8,128)(2,1)S(1)}, bf16[64,2048]{1,0:T(8,128)(2,1)}, u32[]{:S(2)}, u32[]{:S(2)}) collective-permute-start(bf16[64,2048]{1,0:T(8,128)(2,1)S(1)} %slice.9), channel_id=1, source_target_pairs={{0,4},{4,0},{8,12},{12,8},{1,5},{5,1},{9,13},{13,9},{2,6},{6,2},{1... | collective-permute-start | bytes 786440 | tf_op jit(solution)/shard_map/ppermute | solution.py:489
  69.2 23.6 %collective-permute-start.13 = (bf16[128,2048]{1,0:T(8,128)(2,1)}, bf16[128,2048]{1,0:T(8,128)(2,1)}, u32[]{:S(2)}, u32[]{:S(2)}) collective-permute-start(bf16[128,2048]{1,0:T(8,128)(2,1)} %shard_map.72.refs_1_), channel_id=1, source_target_pairs={{0,1},{1,0},{2,3},{3,2},{4,5},{5,4},{6,7},{7,6},{8,9},{9,8},{10,11... | collective-permute-start | bytes 1572872 | tf_op jit(solution)/shard_map/ppermute | solution.py:489
  82.2 10.6 %collective-permute-start.12 = (bf16[128,2048]{1,0:T(8,128)(2,1)}, bf16[128,2048]{1,0:T(8,128)(2,1)S(1)}, u32[]{:S(2)}, u32[]{:S(2)}) collective-permute-start(bf16[128,2048]{1,0:T(8,128)(2,1)} %collective-permute-done.7.refs_0_), channel_id=1, source_target_pairs={{0,1},{1,0},{2,3},{3,2},{4,5},{5,4},{6,7},{7,6},{8,9},{9,8},{10,11... | collective-permute-start | bytes 1572872 | tf_op jit(solution)/shard_map/ppermute | solution.py:489
  83.2 9.6 %collective-permute-start.14 = (bf16[128,2048]{1,0:T(8,128)(2,1)}, bf16[128,2048]{1,0:T(8,128)(2,1)}, u32[]{:S(2)}, u32[]{:S(2)}) collective-permute-start(bf16[128,2048]{1,0:T(8,128)(2,1)} %shard_map.73.refs_2_), channel_id=1, source_target_pairs={{0,1},{1,0},{2,3},{3,2},{4,5},{5,4},{6,7},{7,6},{8,9},{9,8},{10,11... | collective-permute-start | bytes 1572872 | tf_op jit(solution)/shard_map/ppermute | solution.py:489
  83.7 8.3 %collective-permute-start.10 = (bf16[64,2048]{1,0:T(8,128)(2,1)S(1)}, bf16[64,2048]{1,0:T(8,128)(2,1)S(1)}, u32[]{:S(2)}, u32[]{:S(2)}) collective-permute-start(bf16[64,2048]{1,0:T(8,128)(2,1)S(1)} %slice.8), channel_id=1, source_target_pairs={{0,2},{1,3},{2,0},{3,1},{4,6},{5,7},{6,4},{7,5},{8,10},{9,11},{10,... | collective-permute-start | bytes 786440 | tf_op jit(solution)/shard_map/ppermute | solution.py:489
  86.1 6.6 %collective-permute-start.16 = (bf16[64,2048]{1,0:T(8,128)(2,1)}, bf16[64,2048]{1,0:T(8,128)(2,1)S(1)}, u32[]{:S(2)}, u32[]{:S(2)}) collective-permute-start(bf16[64,2048]{1,0:T(8,128)(2,1)} %collective-permute-done.11.refs_4_), channel_id=1, source_target_pairs={{0,1},{1,0},{2,3},{3,2},{4,5},{5,4},{6,7},{7,6},{8,9},{9,8},{10,11... | collective-permute-start | bytes 786440 | tf_op jit(solution)/shard_map/ppermute | solution.py:489
  88.1 1.4 %copy-start = (bf16[16,288,192]{2,1,0:T(8,128)(2,1)}, bf16[16,288,192]{2,1,0:T(8,128)(2,1)S(1)}, u32[]{:S(2)}) copy-start(bf16[16,288,192]{2,1,0:T(8,128)(2,1)S(1)} %shard_map.70.refs_1_.hidden) | copy-start | bytes 5308420
  92.0 0.7 copy-start.18
  92.7 1.7 %collective-permute-start.15 = (bf16[64,2048]{1,0:T(8,128)(2,1)}, bf16[64,2048]{1,0:T(8,128)(2,1)S(1)}, u32[]{:S(2)}, u32[]{:S(2)}) collective-permute-start(bf16[64,2048]{1,0:T(8,128)(2,1)} %shard_map.74.refs_3_), channel_id=1, source_target_pairs={{0,1},{1,0},{2,3},{3,2},{4,5},{5,4},{6,7},{7,6},{8,9},{9,8},{10,11... | collective-permute-start | bytes 786440 | tf_op jit(solution)/shard_map/ppermute | solution.py:489
  92.7 1.7 %copy-start.19 = (bf16[128,2048]{1,0:T(8,128)(2,1)}, bf16[128,2048]{1,0:T(8,128)(2,1)S(1)}, u32[]{:S(2)}) copy-start(bf16[128,2048]{1,0:T(8,128)(2,1)S(1)} %collective-permute-done.12.refs_5_) | copy-start | bytes 1572868
  92.8 1.7 %copy-start.20 = (bf16[64,2048]{1,0:T(8,128)(2,1)}, bf16[64,2048]{1,0:T(8,128)(2,1)S(1)}, u32[]{:S(2)}) copy-start(bf16[64,2048]{1,0:T(8,128)(2,1)S(1)} %collective-permute-done.16.refs_9_) | copy-start | bytes 786436
  94.5 0.7 copy-start.21
  95.2 38.0 %copy-start.14 = (s32[128,8]{0,1:T(8,128)S(1)}, s32[128,8]{0,1:T(8,128)}, u32[]{:S(2)}) copy-start(s32[128,8]{0,1:T(8,128)} %param.5) | copy-start | bytes 12292
  95.2 38.0 %copy-start.15 = (bf16[128,8]{0,1:T(8,128)(2,1)S(1)}, bf16[128,8]{0,1:T(8,128)(2,1)}, u32[]{:S(2)}) copy-start(bf16[128,8]{0,1:T(8,128)(2,1)} %param.6) | copy-start | bytes 6148
